TPU v7x, 32 devices: a whole 2x2x4 slice. The times are simulated.
32 devices in a mesh: dp: 8 (over z, y), fsdp: 4 (over x, core).
Axes of the slice: x: 2, y: 2, z: 4, core: 2. Of those that a mesh axis runs over, the one named last changes fastest.
Arguments:
- tokens: bfloat16 [32768, 768], P(('dp', 'fsdp')), may hold values from -6 to 6
- doc_ids: int32 [32768], P(('dp', 'fsdp')), may hold values from 0 to 4, as said below
- d_out: bfloat16 [32768, 768], P(('dp', 'fsdp')), may hold values from -6 to 6
- ln1_gain: bfloat16 [768], P(('dp', 'fsdp')), may hold values from 0.5 to 1.5
- ln1_shift: bfloat16 [768], P(('dp', 'fsdp')), may hold values from -1.5 to 1.5
- qkv_weight: bfloat16 [768, 2304], P(('dp', 'fsdp')), may hold values from -0.21875 to 0.21875
- qv_bias: bfloat16 [1536], P(('dp', 'fsdp')), may hold values from -1.5 to 1.5
- out_weight: bfloat16 [768, 768], P(('dp', 'fsdp')), may hold values from -0.625 to 0.625
- out_bias: bfloat16 [768], P(('dp', 'fsdp')), may hold values from -1.5 to 1.5
- ln2_gain: bfloat16 [768], P(('dp', 'fsdp')), may hold values from 0.5 to 1.5
- ln2_shift: bfloat16 [768], P(('dp', 'fsdp')), may hold values from -1.5 to 1.5
- fc_weight: bfloat16 [768, 3072], P(('dp', 'fsdp')), may hold values from -0.21875 to 0.21875
- fc_bias: bfloat16 [3072], P(('dp', 'fsdp')), may hold values from -1.5 to 1.5
- proj_weight: bfloat16 [3072, 768], P(('dp', 'fsdp')), may hold values from -0.109375 to 0.109375
- proj_bias: bfloat16 [768], P(('dp', 'fsdp')), may hold values from -1.5 to 1.5
Outputs:
- block_out: bfloat16 [32768, 768], P(('dp', 'fsdp'))
- input_grad: float32 [32768, 768], P(('dp', 'fsdp'))
- ln1_gain_grad: float32 [768], P(('dp', 'fsdp'))
- ln1_shift_grad: float32 [768], P(('dp', 'fsdp'))
- qkv_weight_grad: float32 [768, 2304], P(('dp', 'fsdp'))
- qv_bias_grad: float32 [1536], P(('dp', 'fsdp'))
- out_weight_grad: float32 [768, 768], P(('dp', 'fsdp'))
- out_bias_grad: float32 [768], P(('dp', 'fsdp'))
- ln2_gain_grad: float32 [768], P(('dp', 'fsdp'))
- ln2_shift_grad: float32 [768], P(('dp', 'fsdp'))
- fc_weight_grad: float32 [768, 3072], P(('dp', 'fsdp'))
- fc_bias_grad: float32 [3072], P(('dp', 'fsdp'))
- proj_weight_grad: float32 [3072, 768], P(('dp', 'fsdp'))
- proj_bias_grad: float32 [768], P(('dp', 'fsdp'))
Inputs may be any that keep to these rules, and one draw needn't show every extreme that they name: `doc_ids`: within each packed row of 1024 tokens (rows start at multiples of 1024) the ids start at 1, rise by one at each new document, never fall until the row's padding, and the row ends with one or more padding tokens of id 0; no document crosses a row's end; a row holds at most 4 documents, and some row holds exactly 4.
All inputs are finite; a program needn't handle non-finite values.
Results may differ from a plain program's by a relative error of at most 0.0088.
Values may be sent and summed in bfloat16 or wider, within the bound.
No kernel may reach another device: no remote copies, remote signals or barrier semaphores. Data moves between devices by JAX's collectives and lax.ppermute only.
A program may use at most 192 MiB of HBM per device.

v0:
```python
import math

import jax
import jax.numpy as jnp
from jax import lax
from jax.sharding import PartitionSpec as P

HD = 64
LEN = 1024


EPS = 1e-05
NEG = -1e30


def normalize(v, gain, shift):
    center = v - jnp.mean(v, -1, keepdims=True)
    spread = jnp.mean(center * center, -1, keepdims=True)
    return center * lax.rsqrt(spread + EPS) * gain + shift


def gelu_tanh(v):
    return jax.nn.gelu(v, approximate=True)


def collect(shards):
    (
        gain_one,
        shift_one,
        w_qkv,
        b_qv,
        w_out,
        b_out,
        gain_two,
        shift_two,
        w_fc,
        b_fc,
        w_proj,
        b_proj,
    ) = shards
    return (
        lax.all_gather(gain_one, ("dp", "fsdp"), axis=0, tiled=True),
        lax.all_gather(shift_one, ("dp", "fsdp"), axis=0, tiled=True),
        lax.all_gather(w_qkv, ("dp", "fsdp"), axis=0, tiled=True),
        lax.all_gather(b_qv, ("dp", "fsdp"), axis=0, tiled=True),
        lax.all_gather(w_out, ("dp", "fsdp"), axis=0, tiled=True),
        lax.all_gather(b_out, ("dp", "fsdp"), axis=0, tiled=True),
        lax.all_gather(gain_two, ("dp", "fsdp"), axis=0, tiled=True),
        lax.all_gather(shift_two, ("dp", "fsdp"), axis=0, tiled=True),
        lax.all_gather(w_fc, ("dp", "fsdp"), axis=0, tiled=True),
        lax.all_gather(b_fc, ("dp", "fsdp"), axis=0, tiled=True),
        lax.all_gather(w_proj, ("dp", "fsdp"), axis=0, tiled=True),
        lax.all_gather(b_proj, ("dp", "fsdp"), axis=0, tiled=True),
    )


def spread_sums(grads):
    (
        gain_one,
        shift_one,
        w_qkv,
        b_qv,
        w_out,
        b_out,
        gain_two,
        shift_two,
        w_fc,
        b_fc,
        w_proj,
        b_proj,
    ) = grads
    return (
        lax.psum_scatter(gain_one, ("dp", "fsdp"), scatter_dimension=0, tiled=True),
        lax.psum_scatter(shift_one, ("dp", "fsdp"), scatter_dimension=0, tiled=True),
        lax.psum_scatter(w_qkv, ("dp", "fsdp"), scatter_dimension=0, tiled=True),
        lax.psum_scatter(b_qv, ("dp", "fsdp"), scatter_dimension=0, tiled=True),
        lax.psum_scatter(w_out, ("dp", "fsdp"), scatter_dimension=0, tiled=True),
        lax.psum_scatter(b_out, ("dp", "fsdp"), scatter_dimension=0, tiled=True),
        lax.psum_scatter(gain_two, ("dp", "fsdp"), scatter_dimension=0, tiled=True),
        lax.psum_scatter(shift_two, ("dp", "fsdp"), scatter_dimension=0, tiled=True),
        lax.psum_scatter(w_fc, ("dp", "fsdp"), scatter_dimension=0, tiled=True),
        lax.psum_scatter(b_fc, ("dp", "fsdp"), scatter_dimension=0, tiled=True),
        lax.psum_scatter(w_proj, ("dp", "fsdp"), scatter_dimension=0, tiled=True),
        lax.psum_scatter(b_proj, ("dp", "fsdp"), scatter_dimension=0, tiled=True),
    )


def masked_scores(qblock, keys, docs, first, rows):
    scale = 1.0 / math.sqrt(HD)
    qpos = first + jnp.arange(rows)
    kpos = jnp.arange(LEN)
    qdoc = docs[first : first + rows]
    allow = (
        (kpos[None, :] <= qpos[:, None]) & (qdoc[:, None] == docs[None, :]) & (docs[None, :] > 0)
    )
    allow = allow | (kpos[None, :] == qpos[:, None])
    score = jnp.einsum("qhd,khd->hqk", qblock, keys, preferred_element_type=jnp.float32) * scale
    return jnp.where(allow[None], score, NEG)


def pair_slice(array, row0, col0):
    return lax.dynamic_slice(array, (row0, col0), (LEN, 2 * HD)).reshape(LEN, 2, HD)


def attend(query, keys, values, doc_ids, nseq):
    rows_all, width = query.shape
    pairs = width // (2 * HD)
    block = min(512, LEN)

    def one_pair(index, carry):
        result, lse_all = carry
        seq = index // pairs
        group = index % pairs
        row0 = seq * LEN
        col0 = group * 2 * HD
        q_pair = pair_slice(query, row0, col0)
        k_pair = pair_slice(keys, row0, col0)
        v_pair = pair_slice(values, row0, col0)
        pieces = []
        logs = []
        for first in range(0, LEN, block):
            score = masked_scores(q_pair[first : first + block], k_pair, doc_ids, first, block)
            top = jnp.max(score, -1, keepdims=True)
            expo = jnp.exp(score - top)
            total = jnp.sum(expo, -1, keepdims=True)
            prob = (expo / total).astype(jnp.bfloat16)
            part = jnp.einsum("hqk,khd->qhd", prob, v_pair, preferred_element_type=jnp.float32)
            pieces.append(part.reshape(block, 2 * HD))
            logs.append((top + jnp.log(total))[:, :, 0])
        result = lax.dynamic_update_slice(result, jnp.concatenate(pieces, 0), (row0, col0))
        lse_all = lax.dynamic_update_slice(
            lse_all, jnp.concatenate(logs, 1)[None], (seq, group * 2, 0)
        )
        return (result, lse_all)

    start = (
        jnp.zeros((rows_all, width), jnp.float32),
        jnp.zeros((nseq, 2 * pairs, LEN), jnp.float32),
    )
    return lax.fori_loop(0, nseq * pairs, one_pair, start)


def attend_back(query, keys, values, grad_out, lse_all, doc_ids, nseq):
    rows_all, width = query.shape
    pairs = width // (2 * HD)
    block = min(512, LEN)
    scale = 1.0 / math.sqrt(HD)

    def one_pair(index, carry):
        grad_q, grad_k, grad_v = carry
        seq = index // pairs
        group = index % pairs
        row0 = seq * LEN
        col0 = group * 2 * HD
        q_pair = pair_slice(query, row0, col0)
        k_pair = pair_slice(keys, row0, col0)
        v_pair = pair_slice(values, row0, col0)
        o_pair = pair_slice(grad_out, row0, col0)
        logs = lax.dynamic_slice(lse_all, (seq, group * 2, 0), (1, 2, LEN))[0]
        key_sum = jnp.zeros((LEN, 2, HD), jnp.float32)
        value_sum = jnp.zeros((LEN, 2, HD), jnp.float32)
        pieces = []
        for first in range(0, LEN, block):
            qblock = q_pair[first : first + block]
            gblock = o_pair[first : first + block]
            score = masked_scores(qblock, k_pair, doc_ids, first, block)
            prob = jnp.exp(score - logs[:, first : first + block, None])
            value_sum = value_sum + jnp.einsum(
                "hqk,qhd->khd",
                prob.astype(jnp.bfloat16),
                gblock,
                preferred_element_type=jnp.float32,
            )
            dprob = jnp.einsum("qhd,khd->hqk", gblock, v_pair, preferred_element_type=jnp.float32)
            inner = jnp.sum(prob * dprob, -1, keepdims=True)
            dscore = (prob * (dprob - inner)).astype(jnp.bfloat16)
            part = (
                jnp.einsum("hqk,khd->qhd", dscore, k_pair, preferred_element_type=jnp.float32)
                * scale
            )
            pieces.append(part.reshape(block, 2 * HD))
            key_sum = (
                key_sum
                + jnp.einsum("hqk,qhd->khd", dscore, qblock, preferred_element_type=jnp.float32)
                * scale
            )
        grad_q = lax.dynamic_update_slice(grad_q, jnp.concatenate(pieces, 0), (row0, col0))
        grad_k = lax.dynamic_update_slice(grad_k, key_sum.reshape(LEN, 2 * HD), (row0, col0))
        grad_v = lax.dynamic_update_slice(grad_v, value_sum.reshape(LEN, 2 * HD), (row0, col0))
        return (grad_q, grad_k, grad_v)

    empty = jnp.zeros((rows_all, width), jnp.float32)
    return lax.fori_loop(0, nseq * pairs, one_pair, (empty, empty, empty))


def local(
    tokens,
    doc_ids,
    d_out,
    ln1_gain,
    ln1_shift,
    qkv_weight,
    qv_bias,
    out_weight,
    out_bias,
    ln2_gain,
    ln2_shift,
    fc_weight,
    fc_bias,
    proj_weight,
    proj_bias,
):
    shards = (
        ln1_gain,
        ln1_shift,
        qkv_weight,
        qv_bias,
        out_weight,
        out_bias,
        ln2_gain,
        ln2_shift,
        fc_weight,
        fc_bias,
        proj_weight,
        proj_bias,
    )
    gathered = collect(shards)
    (
        gain_one,
        shift_one,
        w_qkv,
        b_qv,
        w_out,
        b_out,
        gain_two,
        shift_two,
        w_fc,
        b_fc,
        w_proj,
        b_proj,
    ) = gathered
    width = tokens.shape[1]
    nseq = tokens.shape[0] // LEN
    g1 = gain_one.astype(jnp.float32)
    b1 = shift_one.astype(jnp.float32)
    g2 = gain_two.astype(jnp.float32)
    b2 = shift_two.astype(jnp.float32)
    inputs = tokens.astype(jnp.float32)
    h_one = normalize(inputs, g1, b1).astype(jnp.bfloat16)
    mixed = jnp.dot(h_one, w_qkv, preferred_element_type=jnp.float32)
    bias_qv = b_qv.astype(jnp.float32)
    query = (mixed[:, :width] + bias_qv[:width]).astype(jnp.bfloat16)
    keys = mixed[:, width : 2 * width].astype(jnp.bfloat16)
    values = (mixed[:, 2 * width :] + bias_qv[width:]).astype(jnp.bfloat16)
    attended, lse_all = attend(query, keys, values, doc_ids, nseq)
    attended = attended.astype(jnp.bfloat16)
    resid = (
        inputs
        + jnp.dot(attended, w_out, preferred_element_type=jnp.float32)
        + b_out.astype(jnp.float32)
    )
    h_two = normalize(resid, g2, b2).astype(jnp.bfloat16)
    hidden = jnp.dot(h_two, w_fc, preferred_element_type=jnp.float32) + b_fc.astype(jnp.float32)
    active = gelu_tanh(hidden).astype(jnp.bfloat16)
    result = (
        resid
        + jnp.dot(active, w_proj, preferred_element_type=jnp.float32)
        + b_proj.astype(jnp.float32)
    )
    block_out = result.astype(jnp.bfloat16)
    again = collect(shards)
    (
        gain_one,
        shift_one,
        w_qkv,
        b_qv,
        w_out,
        b_out,
        gain_two,
        shift_two,
        w_fc,
        b_fc,
        w_proj,
        b_proj,
    ) = again
    g1 = gain_one.astype(jnp.float32)
    b1 = shift_one.astype(jnp.float32)
    g2 = gain_two.astype(jnp.float32)
    b2 = shift_two.astype(jnp.float32)
    cotangent = d_out.astype(jnp.float32)
    proj_w_grad = jnp.einsum("tf,td->fd", active, d_out, preferred_element_type=jnp.float32)
    proj_b_grad = jnp.sum(cotangent, 0)
    grad_a = jnp.einsum("td,fd->tf", d_out, w_proj, preferred_element_type=jnp.float32)
    _, gelu_pull = jax.vjp(gelu_tanh, hidden)
    grad_u = gelu_pull(grad_a)[0].astype(jnp.bfloat16)
    fc_b_grad = jnp.sum(grad_u.astype(jnp.float32), 0)
    fc_w_grad = jnp.einsum("td,tf->df", h_two, grad_u, preferred_element_type=jnp.float32)
    grad_h2 = jnp.einsum("tf,df->td", grad_u, w_fc, preferred_element_type=jnp.float32)
    _, norm_pull = jax.vjp(normalize, resid, g2, b2)
    grad_r, gain_two_grad, shift_two_grad = norm_pull(grad_h2)
    grad_r = cotangent + grad_r
    grad_t = grad_r.astype(jnp.bfloat16)
    out_b_grad = jnp.sum(grad_t.astype(jnp.float32), 0)
    out_w_grad = jnp.einsum("td,te->de", attended, grad_t, preferred_element_type=jnp.float32)
    grad_o = jnp.einsum("te,de->td", grad_t, w_out, preferred_element_type=jnp.float32).astype(
        jnp.bfloat16
    )
    grad_q, grad_k, grad_v = attend_back(query, keys, values, grad_o, lse_all, doc_ids, nseq)
    grad_q = grad_q.astype(jnp.bfloat16)
    grad_k = grad_k.astype(jnp.bfloat16)
    grad_v = grad_v.astype(jnp.bfloat16)
    qv_grad = jnp.concatenate(
        [jnp.sum(grad_q.astype(jnp.float32), 0), jnp.sum(grad_v.astype(jnp.float32), 0)], 0
    )
    grad_mixed = jnp.concatenate([grad_q, grad_k, grad_v], 1)
    qkv_grad = jnp.einsum("td,te->de", h_one, grad_mixed, preferred_element_type=jnp.float32)
    grad_h1 = jnp.einsum("te,de->td", grad_mixed, w_qkv, preferred_element_type=jnp.float32)
    _, first_pull = jax.vjp(normalize, inputs, g1, b1)
    grad_x, gain_one_grad, shift_one_grad = first_pull(grad_h1)
    input_grad = grad_r + grad_x
    summed = spread_sums(
        (
            gain_one_grad,
            shift_one_grad,
            qkv_grad,
            qv_grad,
            out_w_grad,
            out_b_grad,
            gain_two_grad,
            shift_two_grad,
            fc_w_grad,
            fc_b_grad,
            proj_w_grad,
            proj_b_grad,
        )
    )
    return (block_out, input_grad) + tuple(summed)


def solution(mesh):
    placed = (
        P(("dp", "fsdp"), None),
        P(("dp", "fsdp")),
        P(("dp", "fsdp"), None),
        P(("dp", "fsdp")),
        P(("dp", "fsdp")),
        P(("dp", "fsdp"), None),
        P(("dp", "fsdp")),
        P(("dp", "fsdp"), None),
        P(("dp", "fsdp")),
        P(("dp", "fsdp")),
        P(("dp", "fsdp")),
        P(("dp", "fsdp"), None),
        P(("dp", "fsdp")),
        P(("dp", "fsdp"), None),
        P(("dp", "fsdp")),
    )
    return jax.shard_map(
        local,
        mesh=mesh,
        in_specs=placed,
        out_specs=(
            P(("dp", "fsdp"), None),
            P(("dp", "fsdp"), None),
            P(("dp", "fsdp")),
            P(("dp", "fsdp")),
            P(("dp", "fsdp"), None),
            P(("dp", "fsdp")),
            P(("dp", "fsdp"), None),
            P(("dp", "fsdp")),
            P(("dp", "fsdp")),
            P(("dp", "fsdp")),
            P(("dp", "fsdp"), None),
            P(("dp", "fsdp")),
            P(("dp", "fsdp"), None),
            P(("dp", "fsdp")),
        ),
        check_vma=False,
    )
```

profile of v0, /device:TPU:0, one launch (start us, length us, event | category | flops | bytes accessed | tf_op | source)
XLA Modules:
  0.0 845.6 jit_solution(15076919883471264309)
XLA Ops:
  16.8 43.0 %all-reduce.17 = (bf16[768]{0:T(1024)(128)(2,1)S(1)}, bf16[768]{0:T(1024)(128)(2,1)S(1)}, bf16[768]{0:T(1024)(128)(2,1)S(1)}, bf16[1536]{0:T(1024)(128)(2,1)S(1)...) all-reduce(bf16[768]{0:T(1024)(128)(2,1)S(1)} %dynamic-update-slice, ...), channel_id=1, replica_groups=mesh['dp'=8,'fsdp'=4] {'dp','fsdp'}, use_global_device_ids=true, to_apply=%add.3 | all-reduce | flops 9216 | bytes 36864
  59.8 1.8 copy.45
  63.0 1.6 copy.50
  64.6 9.2 %all-gather.5.cloned.1.call-done = bf16[768,2304]{1,0:T(8,128)(2,1)} async-done(((bf16[24,2304]{1,0:T(8,128)(2,1)}), bf16[768,2304]{1,0:T(8,128)(2,1)}) %all-gather.5.cloned.1.call-update) | async-done | bytes 3538960 | tf_op jit(solution)/shard_map/all_gather | solution.py:44
  73.8 6.1 fusion.72
  79.9 3.6 copy-done.11
  84.9 1.7 copy.48
  86.6 5.0 fusion.58
  91.6 2.6 copy.47
  94.2 2.6 copy.46
  98.2 72.7 %while.36 = (s32[]{:T(128)}, bf16[1024,768]{0,1:T(8,128)(2,1)}, f32[1,12,1024]{2,1,0:T(8,128)S(1)}, bf16[1024,768]{0,1:T(8,128)(2,1)}, s32[1024]{0:T(1024)S(1)},...) while((s32[]{:T(128)}, bf16[1024,768]{0,1:T(8,128)(2,1)}, ...), condition=%wide.region_7.8_spmd, body=%wide.region_2.7_spmd.sunk | while | flops 568854016 | bytes 33139008 | solution.py:140
  100.4 1.8 fusion.181
  112.5 1.8 fusion.181
  116.6 1.5 fusion.184
  124.6 1.8 fusion.181
  136.6 1.8 fusion.181
  140.7 1.5 fusion.184
  148.7 1.8 fusion.181
  160.8 1.8 fusion.181
  164.8 1.5 fusion.184
  170.8 4.0 fusion.83
  174.8 1.6 copy-done.2
  176.9 18.1 %all-gather.9.cloned.1.call-done = bf16[768,3072]{1,0:T(8,128)(2,1)} async-done(((bf16[24,3072]{1,0:T(8,128)(2,1)}), bf16[768,3072]{1,0:T(8,128)(2,1)}) %all-gather.9.cloned.1.call-update) | async-done | bytes 4718608 | tf_op jit(solution)/shard_map/all_gather | solution.py:50
  195.0 11.1 %fusion.75 = f32[1024,3072]{1,0:T(8,128)} fusion(bf16[768,3072]{1,0:T(8,128)(2,1)} %all-gather.9.cloned.1.call-done, f32[1024,768]{0,1:T(8,128)} %copy-done.2, f32[768]{0:T(1024)S(1)} %convert_element_type.154, f32[768]{0:T(1024)S(1)} %convert_element_type.153, f32[1024]{0:T(1024)S(1)} %fusion.68, f32[1024]{0:T(1024)S(1)} %broadcast_multiply_fusion), kind=kOutput, calls=%fused_computation.145 | convolution fusion | flops 4835770368 | bytes 20461568 | tf_op jit(solution)/shard_map/dot_general | solution.py:263
  206.1 54.2 %all-gather.11.cloned.1.call-done = bf16[3072,768]{1,0:T(8,128)(2,1)} async-done(((bf16[96,768]{1,0:T(8,128)(2,1)}), bf16[3072,768]{1,0:T(8,128)(2,1)}) %all-gather.11.cloned.1.call-update) | async-done | bytes 4718608 | tf_op jit(solution)/shard_map/all_gather | solution.py:52
  260.3 15.9 %convert_reduce_fusion = (f32[3072]{0:T(1024)}, bf16[1024,3072]{1,0:T(8,128)(2,1)S(1)}) fusion(f32[1024,3072]{1,0:T(8,128)} %fusion.75, f32[3072]{0:T(1024)S(1)} %convert_element_type.156, bf16[1024,768]{1,0:T(8,128)(2,1)S(1)} %copy-done.16, bf16[3072,768]{1,0:T(8,128)(2,1)} %all-gather.11.cloned.1.call-done), kind=kOutput, calls=%fused_computation.86 | convolution fusion | flops 4904186880 | bytes 25190400 | tf_op jit(solution)/shard_map/td,fd->tf/dot_general | solution.py:293
  276.2 7.3 fusion.85
  283.5 3.7 copy.51
  287.2 3.5 multiply_reduce_fusion.2
  294.1 2.8 fusion.89
  297.0 2.6 convolution_convert_fusion
  303.7 123.6 %while.37 = (s32[]{:T(128)}, bf16[1024,768]{0,1:T(8,128)(2,1)}, bf16[1024,768]{0,1:T(8,128)(2,1)}, bf16[1024,768]{0,1:T(8,128)(2,1)}, bf16[1024,768]{0,1:T(8,128...) while((s32[]{:T(128)}, bf16[1024,768]{0,1:T(8,128)(2,1)}, ...), condition=%wide.region_15.16_spmd, body=%wide.region_12.15_spmd.sunk | while | flops 1381367296 | bytes 76908904 | solution.py:193
  308.3 1.8 fusion.212
  314.3 1.8 multiply_reduce_fusion.8
  318.7 1.8 multiply_reduce_fusion.7
  328.9 1.8 fusion.212
  334.9 1.8 multiply_reduce_fusion.8
  339.2 1.8 multiply_reduce_fusion.7
  349.4 1.8 fusion.212
  355.4 1.8 multiply_reduce_fusion.8
  359.7 1.8 multiply_reduce_fusion.7
  369.9 1.8 fusion.212
  375.9 1.8 multiply_reduce_fusion.8
  380.2 1.8 multiply_reduce_fusion.7
  390.4 1.8 fusion.212
  396.3 1.8 multiply_reduce_fusion.8
  400.7 1.8 multiply_reduce_fusion.7
  410.8 1.8 fusion.212
  416.8 1.8 multiply_reduce_fusion.8
  421.2 1.8 multiply_reduce_fusion.7
  427.4 9.4 %fusion.61 = f32[768,2304]{1,0:T(8,128)} fusion(bf16[1024,768]{0,1:T(8,128)(2,1)} %get-tuple-element.443, bf16[1024,768]{0,1:T(8,128)(2,1)} %get-tuple-element.442, bf16[1024,768]{0,1:T(8,128)(2,1)} %get-tuple-element.441, bf16[1024,768]{0,1:T(8,128)(2,1)S(1)} %copy-done.1, f32[768]{0:T(1024)S(1)} %copy-done.35, f32[768]{0:T(1024)S(1)} %copy-done.24, ...), kind=kOutput, calls=%fused_computation.123 | convolution fusion | flops 3642753024 | bytes 13383680 | tf_op jit(solution)/shard_map/td,te->de/dot_general | solution.py:316
  438.2 12.8 %fusion.76 = f32[3072,768]{1,0:T(8,128)} fusion(bf16[1024,768]{1,0:T(8,128)(2,1)S(1)} %copy-done.17, f32[1024,3072]{1,0:T(8,128)} %fusion.75, f32[3072]{0:T(1024)S(1)} %convert_element_type.156), kind=kOutput, calls=%fused_computation.146 | convolution fusion | flops 4863295488 | bytes 23605248 | tf_op jit(solution)/shard_map/tf,td->fd/dot_general | solution.py:291
  451.8 10.9 %fusion.74 = f32[768,3072]{1,0:T(8,128)} fusion(bf16[1024,3072]{1,0:T(8,128)(2,1)} %copy-done.39, f32[1024,768]{0,1:T(8,128)} %copy-done.2, f32[768]{0:T(1024)S(1)} %copy-done.20, f32[768]{0:T(1024)S(1)} %convert_element_type.153, f32[1024]{0:T(1024)S(1)} %fusion.68, f32[1024]{0:T(1024)S(1)} %broadcast_multiply_fusion), kind=kOutput, calls=%fused_computation.144 | convolution fusion | flops 4835770368 | bytes 18888704 | tf_op jit(solution)/shard_map/td,tf->df/dot_general | solution.py:297
  463.4 12.8 %add_convert_fusion = bf16[1024,768]{0,1:T(8,128)(2,1)} fusion(f32[1024,768]{0,1:T(8,128)} %copy-done.2, bf16[3072,768]{1,0:T(8,128)(2,1)} %all-gather.11.cloned.1.call-done, f32[768]{0:T(1024)S(1)} %convert_element_type.158, f32[1024,3072]{1,0:T(8,128)} %fusion.75, f32[3072]{0:T(1024)S(1)} %convert_element_type.156), kind=kOutput, calls=%fused_computation.119 | convolution fusion | flops 4865654784 | bytes 22035456 | tf_op jit(solution)/shard_map/dot_general | solution.py:267
  476.1 2.6 copy.59
  478.7 8.5 %fusion.84 = (f32[768]{0:T(1024)S(1)}, f32[1024,768]{1,0:T(8,128)}) fusion(bf16[768,2304]{1,0:T(8,128)(2,1)} %all-gather.5.cloned.1.call-done, bf16[1024,768]{0,1:T(8,128)(2,1)S(1)} %copy-done.12, bf16[1024,768]{0,1:T(8,128)(2,1)} %get-tuple-element.442, bf16[1024,768]{0,1:T(8,128)(2,1)} %get-tuple-element.441), kind=kOutput, calls=%fused_computation.153 | convolution fusion | flops 3638820096 | bytes 11406336 | tf_op jit(solution)/shard_map/te,de->td/dot_general | solution.py:317
  487.2 4.2 copy.56
  491.4 2.0 convert_reduce_fusion.4
  496.7 3.3 convert_reduce_fusion.2
  500.0 41.8 %all-reduce.16 = (f32[768]{0:T(1024)S(1)}, f32[768]{0:T(1024)S(1)}, f32[1536]{0:T(1024)S(1)}, f32[768]{0:T(1024)S(1)}, f32[768]{0:T(1024)S(1)}, /*index=5*/f32[7...) all-reduce(f32[768]{0:T(1024)S(1)} %get-tuple-element.508, ...), channel_id=2, replica_groups=mesh['dp'=8,'fsdp'=4] {'dp','fsdp'}, use_global_device_ids=true, to_apply=%region_19.20.clone | all-reduce | flops 9216 | bytes 73728
  545.3 3.5 copy.60
  550.0 4.8 reduce-scatter.5.cloned.1.call-done
  554.9 141.1 %reduce-scatter.11.cloned.1.call-done = f32[96,768]{1,0:T(8,128)} async-done(((f32[3072,768]{1,0:T(8,128)}), f32[96,768]{1,0:T(8,128)}) %reduce-scatter.11.cloned.1.call-update) | async-done | bytes 294928 | tf_op jit(solution)/shard_map/reduce_scatter | solution.py:83
  696.0 142.2 %reduce-scatter.9.cloned.1.call-done = f32[24,3072]{1,0:T(8,128)} async-done(((f32[768,3072]{1,0:T(8,128)}), f32[24,3072]{1,0:T(8,128)}) %reduce-scatter.9.cloned.1.call-update) | async-done | bytes 294928 | tf_op jit(solution)/shard_map/reduce_scatter | solution.py:81
  (369 shorter events, 179.5 us)
Async XLA Ops:
  7.2 66.6 %all-gather.5.cloned.1.call-start = ((), (), s32[]{:S(2)}) async-start(), calls=%async_computation.4 | async-start | bytes 3649536 | tf_op jit(solution)/shard_map/all_gather | solution.py:44
  7.9 162.9 %all-gather.7.cloned.1.call-start = ((), (), s32[]{:S(2)}) async-start(), calls=%async_computation.5 | async-start | bytes 1216512 | tf_op jit(solution)/shard_map/all_gather | solution.py:46
  8.7 186.4 %all-gather.9.cloned.1.call-start = ((), (), s32[]{:S(2)}) async-start(), calls=%async_computation.6 | async-start | bytes 4866048 | tf_op jit(solution)/shard_map/all_gather | solution.py:50
  9.4 250.9 %all-gather.11.cloned.1.call-start = ((), (), s32[]{:S(2)}) async-start(), calls=%async_computation.7 | async-start | bytes 4866048 | tf_op jit(solution)/shard_map/all_gather | solution.py:52
  10.0 540.1 %reduce-scatter.7.cloned.1.call-start = ((), (), s32[]{:S(2)}) async-start(), calls=%async_computation.9 | async-start | bytes 2433024 | tf_op jit(solution)/shard_map/reduce_scatter | solution.py:77
  59.7 14.1 %copy-start.23 = (f32[768]{0:T(1024)}, f32[768]{0:T(1024)S(1)}, u32[]{:S(2)}) copy-start(f32[768]{0:T(1024)S(1)} %convert_element_type.145) | copy-start | bytes 9220
  59.7 14.1 %copy-start.34 = (f32[768]{0:T(1024)}, f32[768]{0:T(1024)S(1)}, u32[]{:S(2)}) copy-start(f32[768]{0:T(1024)S(1)} %convert_element_type.146) | copy-start | bytes 9220
  59.8 135.3 %copy-start.19 = (f32[768]{0:T(1024)}, f32[768]{0:T(1024)S(1)}, u32[]{:S(2)}) copy-start(f32[768]{0:T(1024)S(1)} %convert_element_type.154) | copy-start | bytes 9220
  59.8 3.2 copy-start.15
  61.7 109.2 %copy-start = (bf16[1024,768]{0,1:T(8,128)(2,1)}, bf16[1024,768]{0,1:T(8,128)(2,1)S(1)}, u32[]{:S(2)}) copy-start(bf16[1024,768]{0,1:T(8,128)(2,1)S(1)} %copy.45) | copy-start | bytes 4718596
  61.9 18.0 %copy-start.21 = (f32[1024]{0:T(1024)}, f32[1024]{0:T(1024)S(1)}, u32[]{:S(2)}) copy-start(f32[1024]{0:T(1024)S(1)} %broadcast_multiply_fusion.1) | copy-start | bytes 12292
  62.4 0.6 copy-start.29
  63.0 16.9 %copy-start.25 = (f32[1024]{0:T(1024)}, f32[1024]{0:T(1024)S(1)}, u32[]{:S(2)}) copy-start(f32[1024]{0:T(1024)S(1)} %fusion.67) | copy-start | bytes 12292
  79.9 3.6 copy-start.11
  94.2 3.9 copy-start.14
  170.8 4.0 copy-start.10
  174.8 1.7 copy-start.2
  176.9 83.4 %copy-start.16 = (bf16[1024,768]{1,0:T(8,128)(2,1)S(1)}, bf16[1024,768]{1,0:T(8,128)(2,1)}, u32[]{:S(2)}) copy-start(bf16[1024,768]{1,0:T(8,128)(2,1)} %param.21) | copy-start | bytes 4718596
  260.3 15.9 %copy-start.13 = (bf16[768,3072]{1,0:T(8,128)(2,1)S(1)}, bf16[768,3072]{1,0:T(8,128)(2,1)}, u32[]{:S(2)}) copy-start(bf16[768,3072]{1,0:T(8,128)(2,1)} %all-gather.9.cloned.1.call-done) | copy-start | bytes 14155780
  276.1 7.3 copy-start.39
  283.5 3.7 copy-start.3
  287.2 3.5 copy-start.7
  290.7 1.4 copy-start.8
  291.6 1.7 copy-start.5
  291.6 1.6 copy-start.27
  292.1 2.0 copy-start.18
  294.1 2.9 copy-start.38
  296.9 257.9 %reduce-scatter.5.cloned.1.call-start = ((), (), s32[]{:S(2)}) async-start(), calls=%async_computation.8 | async-start | bytes 7299072 | tf_op jit(solution)/shard_map/reduce_scatter | solution.py:75
  303.7 123.7 %copy-start.1 = (bf16[1024,768]{0,1:T(8,128)(2,1)S(1)}, bf16[1024,768]{0,1:T(8,128)(2,1)}, u32[]{:S(2)}) copy-start(bf16[1024,768]{0,1:T(8,128)(2,1)} %copy-done) | copy-start | bytes 4718596
  303.7 123.7 %copy-start.22 = (f32[1024]{0:T(1024)S(1)}, f32[1024]{0:T(1024)}, u32[]{:S(2)}) copy-start(f32[1024]{0:T(1024)} %copy-done.21) | copy-start | bytes 12292
  303.7 123.7 %copy-start.24 = (f32[768]{0:T(1024)S(1)}, f32[768]{0:T(1024)}, u32[]{:S(2)}) copy-start(f32[768]{0:T(1024)} %copy-done.23) | copy-start | bytes 9220
  303.7 123.7 %copy-start.26 = (f32[1024]{0:T(1024)S(1)}, f32[1024]{0:T(1024)}, u32[]{:S(2)}) copy-start(f32[1024]{0:T(1024)} %copy-done.25) | copy-start | bytes 12292
  303.7 123.7 %copy-start.35 = (f32[768]{0:T(1024)S(1)}, f32[768]{0:T(1024)}, u32[]{:S(2)}) copy-start(f32[768]{0:T(1024)} %copy-done.34) | copy-start | bytes 9220
  436.8 1.4 copy-start.17
  436.8 259.2 %reduce-scatter.11.cloned.1.call-start = ((), (), s32[]{:S(2)}) async-start(), calls=%async_computation.11 | async-start | bytes 9732096 | tf_op jit(solution)/shard_map/reduce_scatter | solution.py:83
  451.1 0.7 copy-start.20
  451.1 387.2 %reduce-scatter.9.cloned.1.call-start = ((), (), s32[]{:S(2)}) async-start(), calls=%async_computation.10 | async-start | bytes 9732096 | tf_op jit(solution)/shard_map/reduce_scatter | solution.py:81
  462.7 0.7 copy-start.37
  463.4 15.4 %copy-start.12 = (bf16[1024,768]{0,1:T(8,128)(2,1)S(1)}, bf16[1024,768]{0,1:T(8,128)(2,1)}, u32[]{:S(2)}) copy-start(bf16[1024,768]{0,1:T(8,128)(2,1)} %get-tuple-element.443) | copy-start | bytes 4718596
  491.4 2.4 copy-start.4
  493.4 0.9 copy-start.30
  494.3 1.9 copy-start.6
  494.3 2.4 copy-start.9
  494.4 2.3 copy-start.28
  496.7 3.3 copy-start.31
  496.7 3.3 copy-start.32
  496.7 3.3 copy-start.33
  496.7 3.3 copy-start.36
Sparse Core Ops, SparseCore 0:
  10.9 62.8 all-gather.4
  76.7 52.8 all-gather.6
  132.5 62.4 all-gather.8
  197.8 62.4 all-gather.10
  297.1 97.9 reduce-scatter.6
  437.0 117.8 reduce-scatter.4
  561.3 134.6 reduce-scatter.10
  703.5 134.7 reduce-scatter.8
where the time goes:
time: 854 us; the launch traced here: 846 us
  waiting for transfers between devices  372 us (44%)
  matrix products  196 us (23%)
  local copies, waits for them, and re-layouts  95.2 us (11%)
  blocking collectives  84.8 us (10%)
  other arithmetic  80.2 us (9%)
  between operations  15.1 us (2%)
    reduce_scatter x1, waiting for transfers between devices, spread_sums(): lax.psum_scatter(w_fc, ('dp', 'fsdp'), scatter_dimension=0, tiled=True)  142 us
    reduce_scatter x1, waiting for transfers between devices, spread_sums(): lax.psum_scatter(w_proj, ('dp', 'fsdp'), scatter_dimension=0, tiled=True)  141 us
    unnamed x2, blocking collectives  84.8 us
    all_gather x1, waiting for transfers between devices, collect(): lax.all_gather(w_proj, ('dp', 'fsdp'), axis=0, tiled=True)  54.2 us
    unnamed x108, local copies, waits for them, and re-layouts  32.1 us
    dot_general x24, matrix products, masked_scores(): jnp.einsum('qhd,khd->hqk', qblock, keys, preferred_element_type=jnp.float32)  22 us
    or x12, other arithmetic, masked_scores(): allow = allow | (kpos[None, :] == qpos[:, None])  21.6 us
    dot_general x12, matrix products, one_pair(): jnp.einsum('qhd,khd->hqk', gblock, v_pair, preferred_element_type=jnp.flo...  21.2 us
  transfers between devices with their start and end apart: 8, of which 6 were waited for; matrix products, arithmetic and copies ran while one was open for 38% of the time, Pallas kernels for 0%

commit v1 on v0

v1 whole, which is shorter than its diff:
```python
import functools
import math

import jax
import jax.numpy as jnp
from jax import lax
from jax.experimental import pallas as pl
from jax.experimental.pallas import tpu as pltpu
from jax.sharding import PartitionSpec as P

HD = 64
LEN = 1024
PAIR = 2 * HD
EPS = 1e-05
NEG = -1e30
AXES = ("dp", "fsdp")

F32 = jnp.float32
BF16 = jnp.bfloat16
NN = (((1,), (0,)), ((), ()))
NT = (((1,), (1,)), ((), ()))
TN = (((0,), (0,)), ((), ()))
ANY = pl.BlockSpec(memory_space=pl.ANY)
SMEM = pl.BlockSpec(memory_space=pltpu.SMEM)
VMEM_LIMIT = 56 << 20

CORE, X, Y, Z0, Z1 = 1, 2, 4, 8, 16
CX, CY, CZ0, CZ1 = 1, 2, 4, 8
GROUPS = (
    (0, CZ0, CY, CY | CZ0),
    (CX, CX | CZ0, CX | CY, CX | CY | CZ0),
    (CZ1, CZ1 | CZ0, CZ1 | CX, CZ1 | CX | CZ0),
    (CZ1 | CY, CZ1 | CY | CZ0, CZ1 | CY | CX, CZ1 | CY | CX | CZ0),
)


def dot(a, b, dims):
    return lax.dot_general(a, b, dims, preferred_element_type=F32)


def params(**more):
    return pltpu.CompilerParams(vmem_limit_bytes=VMEM_LIMIT, **more)


def cost(flops, size):
    return pl.CostEstimate(flops=int(flops), bytes_accessed=int(size), transcendentals=0)


def whole(shape):
    return pl.BlockSpec(shape, lambda *g: (0,) * len(shape))


def rows(block, width):
    return pl.BlockSpec((block, width), lambda i: (i, 0))


def swap(array, bit):
    count = lax.axis_size("dp") * lax.axis_size("fsdp")
    return lax.ppermute(array, AXES, [(i, i ^ bit) for i in range(count)])


def halves(array, core):
    width = array.shape[1] // 2
    low, high = array[:, :width], array[:, width:]
    first = core == 0
    return jnp.where(first, low, high), jnp.where(first, high, low)


def pair_block(array, core):
    keep, send = halves(array, core)
    other = swap(send, CORE)
    first = core == 0
    return jnp.concatenate([jnp.where(first, keep, other), jnp.where(first, other, keep)], 0)


def gather_blocks(block):
    near = swap(block, Z0)
    first = jnp.stack([block, near])
    second = swap(first, Z1)
    by_y = swap(first, Y)
    by_x = swap(second, X)
    a_two = jnp.concatenate([first, by_y], 0)
    b_two = jnp.concatenate([second, by_x], 0)
    a_three = swap(a_two, X)
    b_three = swap(b_two, Y)
    own = (a_two, a_three, b_two, b_three)
    return own + tuple(swap(piece, CORE) for piece in own)


def scatter_sum(mine, other):
    got = swap(other, CORE)

    def total(a, b):
        return (a.astype(F32) + b.astype(F32)).astype(BF16)

    a_keep = total(mine[0], got[0])
    a_send = total(mine[1], got[1])
    b_keep = total(mine[2], got[2])
    b_send = total(mine[3], got[3])
    by_x = swap(a_send, X)
    by_y = swap(b_send, Y)
    a_keep = (a_keep, by_x)
    b_keep = (b_keep, by_y)
    a_low = total(a_keep[0][:2], a_keep[1][:2])
    a_high = total(a_keep[0][2:], a_keep[1][2:])
    b_low = total(b_keep[0][:2], b_keep[1][:2])
    b_high = total(b_keep[0][2:], b_keep[1][2:])
    a_got = swap(a_high, Y)
    b_got = swap(b_high, X)
    b_sum = total(b_low, b_got)
    far = swap(b_sum, Z1)
    near = a_low.astype(F32) + a_got.astype(F32) + far.astype(F32)
    last = swap(near[1].astype(BF16), Z0)
    return near[0] + last.astype(F32)


def own_rows(block, core):
    count = block.shape[0] // 2
    low, high = block[:count], block[count:]
    first = core == 0
    keep = jnp.where(first, low, high)
    got = swap(jnp.where(first, high, low), CORE)
    return jnp.where(first, keep, got), jnp.where(first, got, keep)


def gather_all(array):
    return lax.all_gather(array, AXES, axis=0, tiled=True)


def scatter_all(array):
    return lax.psum_scatter(array, AXES, scatter_dimension=0, tiled=True)


def gather_small(vector, index):
    table = vector.reshape(1, -1)
    for bit in (CORE, X, Y, Z0, Z1):
        other = swap(table, bit)
        low = (index & bit) == 0
        table = jnp.concatenate([jnp.where(low, table, other), jnp.where(low, other, table)], 0)
    return table


def scatter_small(table, index):
    for bit in (Z1, Z0, Y, X, CORE):
        count = table.shape[0] // 2
        low = (index & bit) == 0
        keep = jnp.where(low, table[:count], table[count:])
        send = jnp.where(low, table[count:], table[:count])
        table = keep + swap(send, bit)
    return table.reshape(-1)


def fetch(place, pieces, which, lane, width, into, sem, groups=1):
    if len(pieces) < 8:
        pltpu.make_async_copy(pieces[which], into, sem).start()
        return lambda: pltpu.make_async_copy(into, into, sem).wait()
    chip, core = place[0], place[1]
    step = 48
    for side in range(2):
        half = core if side == 0 else 1 - core
        column = pl.ds(pl.multiple_of(half * width, 128), width)
        for group in range(4):
            for spot, relative in enumerate(GROUPS[group]):
                owner = lax.bitwise_xor(chip, relative)
                for part in range(groups):
                    start = pl.multiple_of((owner * groups + part) * step, step)
                    pltpu.make_async_copy(
                        pieces[4 * side + group].at[spot, :, pl.ds(lane + part * width, width)],
                        into.at[pl.ds(start, step), column],
                        sem,
                    ).start()
    return lambda: pltpu.make_async_copy(into, into, sem).wait()


def normal(v):
    center = v - jnp.mean(v, -1, keepdims=True)
    spread = jnp.mean(center * center, -1, keepdims=True)
    factor = lax.rsqrt(spread + EPS)
    return center * factor, factor


def project_kernel(place, x, gain, shift, q_bias, v_bias, *rest):
    pieces, (mixed, hidden, weight, sem) = rest[:-4], rest[-4:]
    width = x.shape[1]

    @pl.when(pl.program_id(0) == 0)
    def _():
        fetch(place, pieces, 0, 0, 3 * width // 2, weight, sem)()

    unit, _ = normal(x[...].astype(F32))
    h = (unit * gain[...] + shift[...]).astype(BF16)
    hidden[...] = h
    scale = 1.0 / math.sqrt(HD)
    q = dot(h, weight[:, :width], NN) + q_bias[...]
    mixed[:, :width] = (q.astype(BF16).astype(F32) * scale).astype(BF16)
    mixed[:, width : 2 * width] = dot(h, weight[:, width : 2 * width], NN).astype(BF16)
    mixed[:, 2 * width :] = (dot(h, weight[:, 2 * width :], NN) + v_bias[...]).astype(BF16)


def project(place, x, gain, shift, q_bias, v_bias, pieces):
    count, width = x.shape
    block = 256
    return pl.pallas_call(
        project_kernel,
        grid=(count // block,),
        in_specs=[SMEM, rows(block, width)] + [whole((1, width))] * 4 + [ANY] * len(pieces),
        out_specs=[rows(block, 3 * width), rows(block, width)],
        out_shape=[
            jax.ShapeDtypeStruct((count, 3 * width), BF16),
            jax.ShapeDtypeStruct((count, width), BF16),
        ],
        scratch_shapes=[pltpu.VMEM((width, 3 * width), BF16), pltpu.SemaphoreType.DMA],
        compiler_params=params(),
        cost_estimate=cost(6 * count * width * width, 12e6),
        name="project",
    )(place, x, gain, shift, q_bias, v_bias, *pieces)


def allowed(q_doc, k_doc, first, shape, q_dim):
    q_pos = lax.broadcasted_iota(jnp.int32, shape, q_dim) + first
    k_pos = lax.broadcasted_iota(jnp.int32, shape, 1 - q_dim)
    allow = ((k_pos <= q_pos) & (q_doc == k_doc) & (k_doc > 0)) | (k_pos == q_pos)
    return jnp.where(allow, 0.0, NEG)


def attend_kernel(block, q_docs, k_docs, q_all, k_all, v_all, out, lse, bias):
    count = LEN // block

    @pl.when(pl.program_id(0) == 0)
    def _():
        for i in range(count):
            sl, reach = slice(i * block, (i + 1) * block), (i + 1) * block
            bias[sl, :reach] = allowed(q_docs[sl, :], k_docs[:, :reach], i * block, (block, reach), 0)

    low = lax.broadcasted_iota(jnp.int32, (block, PAIR), 1) < HD
    for i in range(count):
        sl, reach = slice(i * block, (i + 1) * block), (i + 1) * block
        q = q_all[sl, :]
        outs, logs = [], []
        for head in range(2):
            q_one = jnp.where(low if head == 0 else ~low, q, jnp.zeros_like(q))
            score = dot(q_one, k_all[:reach, :], NT) + bias[sl, :reach]
            top = jnp.max(score, -1, keepdims=True)
            expo = jnp.exp(score - top)
            total = jnp.sum(expo, -1, keepdims=True)
            outs.append(dot(expo.astype(BF16), v_all[:reach, :], NN) / total)
            logs.append(top + jnp.log(total))
        out[sl, :] = jnp.where(low, outs[0], outs[1]).astype(BF16)
        turned = jnp.where(low, logs[0], logs[1]).T
        lse[0, 0:1, sl] = turned[0:1, :]
        lse[0, 1:2, sl] = turned[HD : HD + 1, :]


def attend(mixed, docs):
    width = mixed.shape[1] // 3
    pairs = width // PAIR
    block = 512
    column = lambda base: pl.BlockSpec((LEN, PAIR), lambda g: (0, base + g))
    return pl.pallas_call(
        functools.partial(attend_kernel, block),
        grid=(pairs,),
        in_specs=[whole((LEN, 1)), whole((1, LEN)), column(0), column(pairs), column(2 * pairs)],
        out_specs=[column(0), pl.BlockSpec((1, 2, LEN), lambda g: (g, 0, 0))],
        out_shape=[
            jax.ShapeDtypeStruct((LEN, width), BF16),
            jax.ShapeDtypeStruct((pairs, 2, LEN), F32),
        ],
        scratch_shapes=[pltpu.VMEM((LEN, LEN), F32)],
        compiler_params=params(),
        cost_estimate=cost(24e9, 8e6),
        name="attend",
    )(docs.reshape(LEN, 1), docs.reshape(1, LEN), mixed, mixed, mixed)


def attend_back_kernel(block, q_docs, k_docs, q_all, k_all, v_all, o_all, g_all, lse, dq, dk, dv, bias, k_sum, v_sum):
    count = LEN // block

    @pl.when(pl.program_id(0) == 0)
    def _():
        for i in range(count):
            sl, reach = slice(i * block, (i + 1) * block), (i + 1) * block
            bias[:reach, sl] = allowed(q_docs[:, sl], k_docs[:reach, :], i * block, (reach, block), 1)

    low = lax.broadcasted_iota(jnp.int32, (block, PAIR), 1) < HD
    low_all = lax.broadcasted_iota(jnp.int32, (LEN, PAIR), 1) < HD
    keys = k_all[...]
    key_one = [jnp.where(low_all, keys, jnp.zeros_like(keys)), jnp.where(low_all, jnp.zeros_like(keys), keys)]
    for i in reversed(range(count)):
        sl, reach = slice(i * block, (i + 1) * block), (i + 1) * block
        q, grad = q_all[sl, :], g_all[sl, :]
        turned = (grad.astype(F32) * o_all[sl, :].astype(F32)).T
        parts = []
        for head in range(2):
            lane = low if head == 0 else ~low
            q_one = jnp.where(lane, q, jnp.zeros_like(q))
            g_one = jnp.where(lane, grad, jnp.zeros_like(grad))
            inner = jnp.sum(turned[head * HD : (head + 1) * HD, :], 0, keepdims=True)
            score = dot(k_all[:reach, :], q_one, NT) + bias[:reach, sl]
            prob = jnp.exp(score - lse[0, head : head + 1, sl])
            v_part = dot(prob.astype(BF16), g_one, NN)
            slope = dot(v_all[:reach, :], g_one, NT)
            dscore = (prob * (slope - inner)).astype(BF16)
            k_part = dot(dscore, q_one, NN)
            if i == count - 1 and head == 0:
                k_sum[...] = k_part
                v_sum[...] = v_part
            else:
                k_sum[:reach, :] += k_part
                v_sum[:reach, :] += v_part
            parts.append(dot(dscore, key_one[head][:reach], TN))
        dq[sl, :] = ((parts[0] + parts[1]) * (1.0 / math.sqrt(HD))).astype(BF16)
    dk[...] = k_sum[...].astype(BF16)
    dv[...] = v_sum[...].astype(BF16)


def attend_back(mixed, attended, grad_o, lse, docs, first, number):
    width = attended.shape[1]
    pairs = width // PAIR
    block = 256
    column = lambda base: pl.BlockSpec((LEN, PAIR), lambda g: (0, base + g))
    return pl.pallas_call(
        functools.partial(attend_back_kernel, block),
        grid=(number,),
        in_specs=[
            whole((1, LEN)),
            whole((LEN, 1)),
            column(first),
            column(pairs + first),
            column(2 * pairs + first),
            column(first),
            column(first),
            pl.BlockSpec((1, 2, LEN), lambda g: (first + g, 0, 0)),
        ],
        out_specs=[column(0)] * 3,
        out_shape=[jax.ShapeDtypeStruct((LEN, PAIR * number), BF16)] * 3,
        scratch_shapes=[
            pltpu.VMEM((LEN, LEN), F32),
            pltpu.VMEM((LEN, PAIR), F32),
            pltpu.VMEM((LEN, PAIR), F32),
        ],
        compiler_params=params(),
        cost_estimate=cost(36e9 * number / pairs, 10e6),
        name="attend_back",
    )(docs.reshape(1, LEN), docs.reshape(LEN, 1), mixed, mixed, mixed, attended, grad_o, lse)


def widen_kernel(place, x, attended, out_bias, gain, shift, fc_bias, *rest):
    pieces, (resid, hidden, active, slope, w_out, w_fc, sems) = rest[:-7], rest[-7:]
    width = x.shape[1]
    depth = w_fc.shape[1]

    @pl.when(pl.program_id(0) == 0)
    def _():
        wait_out = fetch(place, pieces, 0, 0, width // 2, w_out, sems.at[0])
        wait_fc = fetch(place, pieces, 1, width // 2, depth // 2, w_fc, sems.at[1])
        wait_out()
        wait_fc()

    r = x[...].astype(F32) + dot(attended[...], w_out[...], NN) + out_bias[...]
    resid[...] = r
    unit, _ = normal(r)
    h = (unit * gain[...] + shift[...]).astype(BF16)
    hidden[...] = h
    c = math.sqrt(2.0 / math.pi)
    for first in range(0, depth, width):
        sl = slice(first, first + width)
        u = dot(h, w_fc[:, sl], NN) + fc_bias[:, sl]
        square = u * u
        t = jnp.tanh(u * (c + (c * 0.044715) * square))
        half = 0.5 * (1.0 + t)
        active[:, sl] = (u * half).astype(BF16)
        slope[:, sl] = (half + 0.5 * u * (1.0 - t * t) * (c + (3 * c * 0.044715) * square)).astype(BF16)


def widen(place, x, attended, out_bias, gain, shift, fc_bias, pieces):
    count, width = x.shape
    depth = fc_bias.shape[1]
    block = 256
    return pl.pallas_call(
        widen_kernel,
        grid=(count // block,),
        in_specs=[SMEM, rows(block, width), rows(block, width)]
        + [whole((1, width))] * 3
        + [whole((1, depth))]
        + [ANY] * len(pieces),
        out_specs=[rows(block, width), rows(block, width), rows(block, depth), rows(block, depth)],
        out_shape=[
            jax.ShapeDtypeStruct((count, width), F32),
            jax.ShapeDtypeStruct((count, width), BF16),
            jax.ShapeDtypeStruct((count, depth), BF16),
            jax.ShapeDtypeStruct((count, depth), BF16),
        ],
        scratch_shapes=[
            pltpu.VMEM((width, width), BF16),
            pltpu.VMEM((width, depth), BF16),
            pltpu.SemaphoreType.DMA((2,)),
        ],
        compiler_params=params(),
        cost_estimate=cost(2 * count * width * (width + depth), 25e6),
        name="widen",
    )(place, x, attended, out_bias, gain, shift, fc_bias, *pieces)


def narrow_kernel(lane, place, resid, active, slope, cot, proj_bias, *rest):
    pieces, (result, grad_u, fc_sum, proj_sum, w_proj, sem) = rest[:-6], rest[-6:]
    width = resid.shape[1]
    depth = active.shape[1]

    @pl.when(pl.program_id(0) == 0)
    def _():
        fetch(place, pieces, 2, lane, width // 2, w_proj, sem, depth // width)()
        fc_sum[...] = jnp.zeros_like(fc_sum)
        proj_sum[...] = jnp.zeros_like(proj_sum)

    result[...] = (resid[...] + dot(active[...], w_proj[...], NN) + proj_bias[...]).astype(BF16)
    g = cot[...]
    proj_sum[...] += jnp.sum(g.astype(F32), 0, keepdims=True)
    for first in range(0, depth, width):
        sl = slice(first, first + width)
        du = (dot(g, w_proj[sl, :], NT) * slope[:, sl].astype(F32)).astype(BF16)
        grad_u[:, sl] = du
        fc_sum[:, sl] += jnp.sum(du.astype(F32), 0, keepdims=True)


def narrow(place, resid, active, slope, cot, proj_bias, pieces):
    count, width = resid.shape
    depth = active.shape[1]
    block = 256
    return pl.pallas_call(
        functools.partial(narrow_kernel, (width + depth) // 2),
        grid=(count // block,),
        in_specs=[SMEM, rows(block, width), rows(block, depth), rows(block, depth), rows(block, width)]
        + [whole((1, width))]
        + [ANY] * len(pieces),
        out_specs=[rows(block, width), rows(block, depth), whole((1, depth)), whole((1, width))],
        out_shape=[
            jax.ShapeDtypeStruct((count, width), BF16),
            jax.ShapeDtypeStruct((count, depth), BF16),
            jax.ShapeDtypeStruct((1, depth), F32),
            jax.ShapeDtypeStruct((1, width), F32),
        ],
        scratch_shapes=[pltpu.VMEM((depth, width), BF16), pltpu.SemaphoreType.DMA],
        compiler_params=params(),
        cost_estimate=cost(4 * count * width * depth, 30e6),
        name="narrow",
    )(place, resid, active, slope, cot, proj_bias, *pieces)


def norm_back(v, gain, grad):
    unit, factor = normal(v)
    g = grad * gain
    pulled = factor * (g - jnp.mean(g, -1, keepdims=True) - unit * jnp.mean(g * unit, -1, keepdims=True))
    return pulled, jnp.sum(grad * unit, 0, keepdims=True), jnp.sum(grad, 0, keepdims=True)


def middle_kernel(place, resid, grad_u, cot, gain, *rest):
    pieces, rest = rest[:-9], rest[-9:]
    grad_r, grad_t, grad_o, gain_sum, shift_sum, bias_sum, w_out, w_fc, sems = rest
    width = resid.shape[1]
    depth = grad_u.shape[1]

    @pl.when(pl.program_id(0) == 0)
    def _():
        wait_fc = fetch(place, pieces, 1, width // 2, depth // 2, w_fc, sems.at[0])
        wait_out = fetch(place, pieces, 0, 0, width // 2, w_out, sems.at[1])
        gain_sum[...] = jnp.zeros_like(gain_sum)
        shift_sum[...] = jnp.zeros_like(shift_sum)
        bias_sum[...] = jnp.zeros_like(bias_sum)
        wait_fc()
        wait_out()

    grad_h = dot(grad_u[...], w_fc[...], NT)
    pulled, gains, shifts = norm_back(resid[...], gain[...], grad_h)
    total = cot[...].astype(F32) + pulled
    grad_r[...] = total
    low = total.astype(BF16)
    grad_t[...] = low
    gain_sum[...] += gains
    shift_sum[...] += shifts
    bias_sum[...] += jnp.sum(low.astype(F32), 0, keepdims=True)
    grad_o[...] = dot(low, w_out[...], NT).astype(BF16)


def middle(place, resid, grad_u, cot, gain, pieces):
    count, width = resid.shape
    depth = grad_u.shape[1]
    block = 256
    return pl.pallas_call(
        middle_kernel,
        grid=(count // block,),
        in_specs=[SMEM, rows(block, width), rows(block, depth), rows(block, width), whole((1, width))]
        + [ANY] * len(pieces),
        out_specs=[rows(block, width)] * 3 + [whole((1, width))] * 3,
        out_shape=[
            jax.ShapeDtypeStruct((count, width), F32),
            jax.ShapeDtypeStruct((count, width), BF16),
            jax.ShapeDtypeStruct((count, width), BF16),
        ]
        + [jax.ShapeDtypeStruct((1, width), F32)] * 3,
        scratch_shapes=[
            pltpu.VMEM((width, width), BF16),
            pltpu.VMEM((width, depth), BF16),
            pltpu.SemaphoreType.DMA((2,)),
        ],
        compiler_params=params(),
        cost_estimate=cost(2 * count * width * (width + depth), 25e6),
        name="middle",
    )(place, resid, grad_u, cot, gain, *pieces)


def first_back_kernel(place, x, grad_r, gain, dq, dk, dv, *rest):
    pieces, (grad_x, gain_sum, shift_sum, weight, sem) = rest[:-5], rest[-5:]
    width = x.shape[1]

    @pl.when(pl.program_id(0) == 0)
    def _():
        fetch(place, pieces, 0, 0, 3 * width // 2, weight, sem)()
        gain_sum[...] = jnp.zeros_like(gain_sum)
        shift_sum[...] = jnp.zeros_like(shift_sum)

    grad_h = (
        dot(dq[...], weight[:, :width], NT)
        + dot(dk[...], weight[:, width : 2 * width], NT)
        + dot(dv[...], weight[:, 2 * width :], NT)
    )
    pulled, gains, shifts = norm_back(x[...].astype(F32), gain[...], grad_h)
    grad_x[...] = grad_r[...] + pulled
    gain_sum[...] += gains
    shift_sum[...] += shifts


def first_back(place, x, grad_r, gain, dq, dk, dv, pieces):
    count, width = x.shape
    block = 256
    return pl.pallas_call(
        first_back_kernel,
        grid=(count // block,),
        in_specs=[SMEM, rows(block, width), rows(block, width), whole((1, width))]
        + [rows(block, width)] * 3
        + [ANY] * len(pieces),
        out_specs=[rows(block, width)] + [whole((1, width))] * 2,
        out_shape=[jax.ShapeDtypeStruct((count, width), F32)] + [jax.ShapeDtypeStruct((1, width), F32)] * 2,
        scratch_shapes=[pltpu.VMEM((width, 3 * width), BF16), pltpu.SemaphoreType.DMA],
        compiler_params=params(),
        cost_estimate=cost(6 * count * width * width, 16e6),
        name="first_back",
    )(place, x, grad_r, gain, dq, dk, dv, *pieces)


def weight_grad_kernel(number, steps, step_rows, place, left, *rest):
    rights, mine, other, stage, sems = rest[:number], rest[number], rest[number + 1], rest[number + 2], rest[number + 3]
    tile = stage.shape[3]
    step = pl.program_id(0)
    slot = lax.rem(step, 2)
    chip, core = place[0], place[1]
    per_half = steps // 2

    def send(at, start):
        which = lax.rem(at, 2)
        own = (at // per_half) == core
        for index in range(number):
            lane = pl.multiple_of((index * per_half + lax.rem(at, per_half)) * tile, 128)
            for group in range(4):
                for spot, relative in enumerate(GROUPS[group]):
                    owner = lax.bitwise_xor(chip, relative)
                    source = stage.at[which, index, pl.ds(pl.multiple_of(owner * step_rows, 16), step_rows), :]
                    for flag, target in ((own, mine), (jnp.logical_not(own), other)):
                        copy = pltpu.make_async_copy(
                            source, target.at[group, spot, :, pl.ds(lane, tile)], sems.at[which]
                        )
                        if start:
                            pl.when(flag)(copy.start)

    def finish(which):
        pltpu.make_async_copy(stage.at[which], stage.at[which], sems.at[which]).wait()

    @pl.when(step >= 2)
    def _():
        finish(slot)

    for index in range(number):
        stage[slot, index] = dot(left[...], rights[index][...], TN).astype(BF16)
    send(step, True)

    @pl.when(step == steps - 1)
    def _():
        finish(slot)
        if steps > 1:
            finish(1 - slot)


def weight_grad(place, left, rights, tile, name):
    count, tall = left.shape
    wide = rights[0].shape[1]
    number = len(rights)
    steps = wide // tile
    step_rows = tall // 16
    shape = (4, 4, step_rows, number * wide // 2)
    return pl.pallas_call(
        functools.partial(weight_grad_kernel, number, steps, step_rows),
        grid=(steps,),
        in_specs=[SMEM, whole((count, tall))] + [pl.BlockSpec((count, tile), lambda i: (0, i))] * number,
        out_specs=[ANY, ANY],
        out_shape=[jax.ShapeDtypeStruct(shape, BF16)] * 2,
        scratch_shapes=[pltpu.VMEM((2, number, tall, tile), BF16), pltpu.SemaphoreType.DMA((2,))],
        compiler_params=params(),
        cost_estimate=cost(2 * count * tall * wide * number, 2 * (count * tall + wide * number * (count + tall))),
        name=name,
    )(place, left, *rights)


def whole_grad(place, left, rights, tile, name):
    return jnp.concatenate([dot(left, right, TN) for right in rights], 1)


def unpack(table):
    count = table.shape[1] // 12
    spans = (1, 1, 2, 1, 1, 1, 4, 1)
    found, at = [], 0
    for span in spans:
        found.append(table[:, at : at + span * count].reshape(1, -1).astype(F32))
        at += span * count
    return found


def pack(vectors, devices):
    return jnp.concatenate([v.reshape(devices, -1) for v in vectors], 1)


def staged(
    tokens,
    doc_ids,
    d_out,
    ln1_gain,
    ln1_shift,
    qkv_weight,
    qv_bias,
    out_weight,
    out_bias,
    ln2_gain,
    ln2_shift,
    fc_weight,
    fc_bias,
    proj_weight,
    proj_bias,
):
    width = tokens.shape[1]
    depth = fc_weight.shape[1]
    index = lax.axis_index("dp") * lax.axis_size("fsdp") + lax.axis_index("fsdp")
    core = index & 1
    place = jnp.stack([index >> 1, core]).astype(jnp.int32)
    devices = lax.axis_size("dp") * lax.axis_size("fsdp")

    smalls = jnp.concatenate([ln1_gain, ln1_shift, qv_bias, out_bias, ln2_gain, ln2_shift, fc_bias, proj_bias])
    by_stage = (lax.axis_size("dp"), lax.axis_size("fsdp")) == (8, 4)
    if by_stage:
        first_pieces = gather_blocks(pair_block(qkv_weight, core))
        table = gather_small(smalls, index)
        proj_block = pair_block(proj_weight, core)
        proj_parts = [proj_block[48 * j : 48 * (j + 1)] for j in range(depth // width)]
        rest_block = jnp.concatenate([pair_block(out_weight, core), pair_block(fc_weight, core)] + proj_parts, 1)
        rest_pieces = gather_blocks(rest_block)
    else:
        first_pieces, rest_pieces = [gather_all(qkv_weight)], [gather_all(w) for w in (out_weight, fc_weight, proj_weight)]
        table = gather_all(smalls.reshape(1, -1))
    g1, b1, qv_row, out_row, g2, b2, fc_row, proj_row = unpack(table)

    mixed, h_one = project(place, tokens, g1, b1, qv_row[:, :width], qv_row[:, width:], first_pieces)
    attended, lse = attend(mixed, doc_ids)
    resid, h_two, active, slope = widen(place, tokens, attended, out_row, g2, b2, fc_row, rest_pieces)
    grad_of = weight_grad if by_stage else whole_grad
    proj_terms = grad_of(place, active, [d_out], 384, "proj_grad")
    result, grad_u, fc_sum, proj_sum = narrow(place, resid, active, slope, d_out, proj_row, rest_pieces)
    fc_terms = grad_of(place, h_two, [grad_u], 384, "fc_grad")
    grad_r, grad_t, grad_o, gain_two, shift_two, out_sum = middle(place, resid, grad_u, d_out, g2, rest_pieces)
    out_terms = grad_of(place, attended, [grad_t], 384, "out_grad")
    pairs = width // PAIR
    parts = [
        attend_back(mixed, attended, grad_o, lse, doc_ids, first, pairs // 2) for first in (0, pairs // 2)
    ]
    dq, dk, dv = (jnp.concatenate(p, 1) for p in zip(*parts))
    qkv_terms = grad_of(place, h_one, [dq, dk, dv], 384, "qkv_grad")
    grad_x, gain_one, shift_one = first_back(place, tokens, grad_r, g1, dq, dk, dv, first_pieces)

    if by_stage:
        proj_grad = jnp.concatenate(own_rows(scatter_sum(*proj_terms), core), 1)
        fc_grad = jnp.concatenate(own_rows(scatter_sum(*fc_terms), core), 1)
        out_grad = jnp.concatenate(own_rows(scatter_sum(*out_terms), core), 1)
        sides = own_rows(scatter_sum(*qkv_terms), core)
        part = width // 2
        qkv_grad = jnp.concatenate([side[:, part * j : part * (j + 1)] for j in range(3) for side in sides], 1)
    else:
        proj_grad, fc_grad, out_grad, qkv_grad = (
            scatter_all(term) for term in (proj_terms, fc_terms, out_terms, qkv_terms)
        )
    q_sum = jnp.sum(dq.astype(F32), 0)
    v_sum = jnp.sum(dv.astype(F32), 0)
    sums = pack(
        [gain_one, shift_one, jnp.concatenate([q_sum, v_sum]), out_sum, gain_two, shift_two, fc_sum, proj_sum],
        devices,
    )
    own = scatter_small(sums, index) if by_stage else scatter_all(sums).reshape(-1)
    n = width // devices
    spots = (0, n, 2 * n, 4 * n, 5 * n, 6 * n, 7 * n, 11 * n, 12 * n)
    s = [own[a:b] for a, b in zip(spots[:-1], spots[1:])]
    return (
        result,
        grad_x,
        s[0],
        s[1],
        qkv_grad,
        s[2],
        out_grad,
        s[3],
        s[4],
        s[5],
        fc_grad,
        s[6],
        proj_grad,
        s[7],
    )


def solution(mesh):
    every, block = P(AXES), P(AXES, None)
    ins = (block, every, block, every, every, block, every, block, every, every, every, block, every, block, every)
    outs = (block, block, every, every, block, every, block, every, every, every, block, every, block, every)
    return jax.shard_map(staged, mesh=mesh, in_specs=ins, out_specs=outs, check_vma=False)
```

time: 854 us -> 457 us (0.54)
  matrix products: 196 us -> 0 us
  waiting for transfers between devices: 372 us -> 190 us
  Pallas kernels: 0 us -> 164 us
  blocking collectives: 84.8 us -> 0 us
  local copies, waits for them, and re-layouts: 95.2 us -> 25.1 us
  other arithmetic: 80.2 us -> 14.8 us
  starting transfers between devices: 0.32 us -> 56.6 us
  between operations: 15.1 us -> 2.02 us
    reduce_scatter x4 -> x0, waiting for transfers between devices: 288 us -> none  [the longest x1 142 us: spread_sums(): lax.psum_scatter(w_fc, ('dp', 'fsdp'), scatter_dimension=0, tiled=True)]
    dot_general x96 -> x0, matrix products: 196 us -> none  [the longest x24 22 us: masked_scores(): jnp.einsum('qhd,khd->hqk', qblock, keys, preferred_element_type=jnp.float32)]
    ppermute x0 -> x66, waiting for transfers between devices: none -> 190 us  [swap(): return lax.ppermute(array, AXES, [(i, i ^ bit) for i in range(count)])]
    pallas_call x0 -> x12, Pallas kernels: none -> 164 us  [the longest x4 37.4 us: weight_grad(): pl.pallas_call(functools.partial(weight_grad_kernel, number, steps, step_...]
    unnamed x2 -> x0, blocking collectives: 84.8 us -> none
    all_gather x4 -> x0, waiting for transfers between devices: 81.4 us -> none  [the longest x1 54.2 us: collect(): lax.all_gather(w_proj, ('dp', 'fsdp'), axis=0, tiled=True)]
    ppermute x0 -> x66, starting transfers between devices: none -> 56.6 us  [swap(): return lax.ppermute(array, AXES, [(i, i ^ bit) for i in range(count)])]
    reduce_sum x22 -> x2, other arithmetic: 27.8 us -> 0.56 us  [the longest x1 0.28 us: staged(): q_sum = jnp.sum(dq.astype(F32), 0)]
  transfers between devices with their start and end apart: 8 -> 66, of which waited for: 6 -> 28; matrix products, arithmetic and copies ran while one was open for 38% -> 5% of each run, Pallas kernels for 0% -> 15%
where the time goes in v1:
time: 457 us; the launch traced here: 452 us
  waiting for transfers between devices  190 us (42%)
  Pallas kernels  164 us (36%)
  starting transfers between devices  56.6 us (12%)
  local copies, waits for them, and re-layouts  25.1 us (5%)
  other arithmetic  14.8 us (3%)
    ppermute x66, waiting for transfers between devices, swap(): return lax.ppermute(array, AXES, [(i, i ^ bit) for i in range(count)])  190 us
    ppermute x66, starting transfers between devices, swap(): return lax.ppermute(array, AXES, [(i, i ^ bit) for i in range(count)])  56.6 us
    pallas_call x4, Pallas kernels, weight_grad(): pl.pallas_call(functools.partial(weight_grad_kernel, number, steps, step_...  37.4 us
    pallas_call x2, Pallas kernels, attend_back(): pl.pallas_call(functools.partial(attend_back_kernel, block), grid=(number...  31.2 us
    pallas_call x1, Pallas kernels, widen(): pl.pallas_call(widen_kernel, grid=(count // block,), in_specs=[SMEM, rows...  20.4 us
    pallas_call x1, Pallas kernels, attend(): pl.pallas_call(functools.partial(attend_kernel, block), grid=(pairs,), in...  20.2 us
    pallas_call x1, Pallas kernels, narrow(): pl.pallas_call(functools.partial(narrow_kernel, (width + depth) // 2), gr...  17.4 us
    pallas_call x1, Pallas kernels, middle(): pl.pallas_call(middle_kernel, grid=(count // block,), in_specs=[SMEM, row...  16.5 us
  transfers between devices with their start and end apart: 66, of which 28 were waited for; matrix products, arithmetic and copies ran while one was open for 5% of the time, Pallas kernels for 15%

profile of v1, /device:TPU:0, one launch (start us, length us, event | category | flops | bytes accessed | tf_op | source)
XLA Modules:
  0.0 452.1 jit_solution(12626138845527246069)
XLA Ops:
  0.7 5.5 %concatenate.76 = bf16[288]{0:T(512)(128)(2,1)S(1)} concatenate(bf16[24]{0:T(256)(128)(2,1)} %param.18, bf16[24]{0:T(256)(128)(2,1)} %param.19, bf16[48]{0:T(256)(128)(2,1)} %param.21, bf16[24]{0:T(256)(128)(2,1)} %param.23, bf16[24]{0:T(256)(128)(2,1)} %param.24, bf16[24]{0:T(256)(128)(2,1)} %param.25, bf16[96]{0:T(256)(128)(2,1)} %param.27, bf16[24]{0:T(256)(128)(2,1)} %param.29), dimensions={0} | concatenate | bytes 1152 | tf_op jit(solution)/shard_map/concatenate | solution.py:654
  8.9 2.6 collective-permute-start.1
  13.0 2.1 collective-permute-start.2
  16.2 1.7 copy.29.q_docs.k_docs
  19.6 1.6 collective-permute-start.6
  21.9 1.6 collective-permute-start.3
  23.6 1.9 collective-permute-done.6
  26.2 6.0 %collective-permute-done.19 = bf16[48,3456]{1,0:T(8,128)(2,1)S(1)} collective-permute-done((bf16[48,3456]{1,0:T(8,128)(2,1)S(1)}, bf16[48,3456]{1,0:T(8,128)(2,1)S(1)}, u32[]{:S(2)}, u32[]{:S(2)}) %collective-permute-start.19) | collective-permute-done | bytes 331808 | tf_op jit(solution)/shard_map/ppermute | solution.py:59
  32.3 2.7 collective-permute-start.22
  35.4 2.6 collective-permute-start.9
  38.2 1.6 collective-permute-start.8
  39.7 34.2 %collective-permute-done.9 = bf16[2,48,1152]{2,1,0:T(8,128)(2,1)S(1)} collective-permute-done((bf16[2,48,1152]{2,1,0:T(8,128)(2,1)S(1)}, bf16[2,48,1152]{2,1,0:T(8,128)(2,1)S(1)}, u32[]{:S(2)}, u32[]{:S(2)}) %collective-permute-start.9) | collective-permute-done | bytes 221216 | tf_op jit(solution)/shard_map/ppermute | solution.py:59
  74.7 1.5 collective-permute-start.23
  76.3 13.4 %collective-permute-done.20 = bf16[2,48,3456]{2,1,0:T(8,128)(2,1)S(1)} collective-permute-done((bf16[2,48,3456]{2,1,0:T(8,128)(2,1)S(1)}, bf16[2,48,3456]{2,1,0:T(8,128)(2,1)S(1)}, u32[]{:S(2)}, u32[]{:S(2)}) %collective-permute-start.20) | collective-permute-done | bytes 663584 | tf_op jit(solution)/shard_map/ppermute | solution.py:59
  89.7 1.5 collective-permute-start.10
  92.1 6.0 %collective-permute-done.10 = bf16[2,48,1152]{2,1,0:T(8,128)(2,1)S(1)} collective-permute-done((bf16[2,48,1152]{2,1,0:T(8,128)(2,1)S(1)}, bf16[2,48,1152]{2,1,0:T(8,128)(2,1)S(1)}, u32[]{:S(2)}, u32[]{:S(2)}) %collective-permute-start.10) | collective-permute-done | bytes 221216 | tf_op jit(solution)/shard_map/ppermute | solution.py:59
  99.1 1.7 collective-permute-start.11
  102.2 32.2 %collective-permute-done.11.rest_3_ = bf16[4,48,1152]{2,1,0:T(8,128)(2,1)} collective-permute-done((bf16[4,48,1152]{2,1,0:T(8,128)(2,1)}, bf16[4,48,1152]{2,1,0:T(8,128)(2,1)}, u32[]{:S(2)}, u32[]{:S(2)}) %collective-permute-start.11) | collective-permute-done | bytes 442400 | tf_op jit(solution)/shard_map/ppermute | solution.py:59
  140.4 9.6 %project.1 = (bf16[1024,2304]{1,0:T(8,128)(2,1)}, bf16[1024,768]{1,0:T(8,128)(2,1)}) custom-call(s32[2]{0:T(128)} %pad_add_fusion.place, bf16[1024,768]{1,0:T(8,128)(2,1)} %x.5, f32[1,768]{1,0:T(1,128)} %reshape.320.gain, f32[1,768]{1,0:T(1,128)} %reshape.321.shift, f32[1,768]{1,0:T(1,128)} %get-tuple-element.129.q_bias, ...), custom_call_target="tpu_custom_call" | custom-call | flops 3623878656 | bytes 12000000 | tf_op jit(solution)/shard_map/project/pallas_call | solution.py:203
  150.7 20.2 %attend.1 = (bf16[1024,768]{1,0:T(8,128)(2,1)}, f32[6,2,1024]{2,1,0:T(2,128)}) custom-call(s32[1024,1]{1,0:T(8,128)} %copy.29.q_docs.k_docs, s32[1,1024]{1,0:T(1,128)} %bitcast.152, bf16[1024,2304]{1,0:T(8,128)(2,1)} %get-tuple-element.49.q_all.k_all.v_all, bf16[1024,2304]{1,0:T(8,128)(2,1)} %get-tuple-element.49.q_all.k_all.v_all, ...), custom_call_target="tpu_custom_call" | custom-call | flops 24000000000 | bytes 8000000 | tf_op jit(solution)/shard_map/attend/pallas_call | solution.py:259
  171.0 1.1 copy-done.22
  172.9 20.4 %widen.1 = (f32[1024,768]{1,0:T(8,128)}, bf16[1024,768]{1,0:T(8,128)(2,1)}, bf16[1024,3072]{1,0:T(8,128)(2,1)}, bf16[1024,3072]{1,0:T(8,128)(2,1)}) custom-call(s32[2]{0:T(128)} %pad_add_fusion.place, bf16[1024,768]{1,0:T(8,128)(2,1)} %x.5, bf16[1024,768]{1,0:T(8,128)(2,1)} %get-tuple-element.50.attended.o_all.left, f32[1,768]{1,0:T(1,128)} %reshape.323.out_bias, ...), custom_call_target="tpu_custom_call" | custom-call | flops 6039797760 | bytes 25000000 | tf_op jit(solution)/shard_map/widen/pallas_call | solution.py:379
  193.3 17.4 %narrow.1 = (bf16[1024,768]{1,0:T(8,128)(2,1)}, bf16[1024,3072]{1,0:T(8,128)(2,1)}, f32[1,3072]{1,0:T(1,128)}, f32[1,768]{1,0:T(1,128)}) custom-call(s32[2]{0:T(128)} %pad_add_fusion.place, f32[1024,768]{1,0:T(8,128)} %get-tuple-element.51.resid, bf16[1024,3072]{1,0:T(8,128)(2,1)} %get-tuple-element.52.active.left, ...), custom_call_target="tpu_custom_call" | custom-call | flops 9663676416 | bytes 30000000 | tf_op jit(solution)/shard_map/narrow/pallas_call | solution.py:429
  210.7 16.5 %middle.1 = (f32[1024,768]{1,0:T(8,128)}, bf16[1024,768]{1,0:T(8,128)(2,1)}, bf16[1024,768]{1,0:T(8,128)(2,1)}, f32[1,768]{1,0:T(1,128)}, f32[1,768]{1,0:T(1,128)}, /*index=5*/f32[1,768]{1,0:T(1,128)}) custom-call(s32[2]{0:T(128)} %pad_add_fusion.place, f32[1024,768]{1,0:T(8,128)} %get-tuple-element.51.resid, ...), custom_call_target="tpu_custom_call" | custom-call | flops 6039797760 | bytes 25000000 | tf_op jit(solution)/shard_map/middle/pallas_call | solution.py:488
  227.2 15.5 %attend_back.3 = (bf16[1024,384]{1,0:T(8,128)(2,1)}, bf16[1024,384]{1,0:T(8,128)(2,1)}, bf16[1024,384]{1,0:T(8,128)(2,1)}) custom-call(s32[1,1024]{1,0:T(1,128)} %bitcast.153, s32[1024,1]{1,0:T(8,128)} %copy.29.q_docs.k_docs, bf16[1024,2304]{1,0:T(8,128)(2,1)} %get-tuple-element.49.q_all.k_all.v_all, bf16[1024,2304]{1,0:T(8,128)(2,1)} %get-tuple-element.49.q_all.k_all.v_all, ...), custom_call_target="tpu_custom_call" | custom-call | flops 17999998976 | bytes 10000000 | tf_op jit(solution)/shard_map/attend_back/pallas_call | solution.py:321
  242.7 15.7 %attend_back.2 = (bf16[1024,384]{1,0:T(8,128)(2,1)}, bf16[1024,384]{1,0:T(8,128)(2,1)}, bf16[1024,384]{1,0:T(8,128)(2,1)}) custom-call(s32[1,1024]{1,0:T(1,128)} %bitcast.154, s32[1024,1]{1,0:T(8,128)} %copy.29.q_docs.k_docs, bf16[1024,2304]{1,0:T(8,128)(2,1)} %get-tuple-element.49.q_all.k_all.v_all, bf16[1024,2304]{1,0:T(8,128)(2,1)} %get-tuple-element.49.q_all.k_all.v_all, ...), custom_call_target="tpu_custom_call" | custom-call | flops 17999998976 | bytes 10000000 | tf_op jit(solution)/shard_map/attend_back/pallas_call | solution.py:321
  260.2 1.2 constant_dynamic-update-slice_fusion.14
  262.0 2.6 constant_dynamic-update-slice_fusion.10
  266.8 11.1 %first_back.1 = (f32[1024,768]{1,0:T(8,128)}, f32[1,768]{1,0:T(1,128)}, f32[1,768]{1,0:T(1,128)}) custom-call(s32[2]{0:T(128)} %pad_add_fusion.place, bf16[1024,768]{1,0:T(8,128)(2,1)} %x.5, f32[1024,768]{1,0:T(8,128)} %get-tuple-element.56.grad_r, f32[1,768]{1,0:T(1,128)} %reshape.320.gain, bf16[1024,768]{1,0:T(8,128)(2,1)} %copy-done, ...), custom_call_target="tpu_custom_call" | custom-call | flops 3623878656 | bytes 16000000 | tf_op jit(solution)/shard_map/first_back/pallas_call | solution.py:535
  279.7 4.7 %collective-permute-done.29 = f32[16,288]{1,0:T(8,128)S(1)} collective-permute-done((f32[16,288]{1,0:T(8,128)S(1)}, f32[16,288]{1,0:T(8,128)S(1)}, u32[]{:S(2)}, u32[]{:S(2)}) %collective-permute-start.29) | collective-permute-done | bytes 18464 | tf_op jit(solution)/shard_map/ppermute | solution.py:59
  284.5 2.9 collective-permute-start.30
  287.4 11.5 %proj_grad.1 = (bf16[4,4,192,384]{3,2,1,0:T(8,128)(2,1)}, bf16[4,4,192,384]{3,2,1,0:T(8,128)(2,1)}) custom-call(s32[2]{0:T(128)} %pad_add_fusion.place, bf16[1024,3072]{1,0:T(8,128)(2,1)} %get-tuple-element.52.active.left, bf16[1024,768]{1,0:T(8,128)(2,1)} %rest_0_.1), custom_call_target="tpu_custom_call" | custom-call | flops 4831838208 | bytes 12582912 | tf_op jit(solution)/shard_map/proj_grad/pallas_call | solution.py:599
  298.9 1.1 collective-permute-start.31
  300.1 4.6 %out_grad.1 = (bf16[4,4,48,384]{3,2,1,0:T(8,128)(2,1)}, bf16[4,4,48,384]{3,2,1,0:T(8,128)(2,1)}) custom-call(s32[2]{0:T(128)} %pad_add_fusion.place, bf16[1024,768]{1,0:T(8,128)(2,1)} %get-tuple-element.50.attended.o_all.left, bf16[1024,768]{1,0:T(8,128)(2,1)} %get-tuple-element.76.rest_0_), custom_call_target="tpu_custom_call" | custom-call | flops 1207959552 | bytes 4325376 | tf_op jit(solution)/shard_map/out_grad/pallas_call | solution.py:599
  304.8 1.6 collective-permute-start.32
  306.4 11.9 %fc_grad.1 = (bf16[4,4,48,1536]{3,2,1,0:T(8,128)(2,1)}, bf16[4,4,48,1536]{3,2,1,0:T(8,128)(2,1)}) custom-call(s32[2]{0:T(128)} %pad_add_fusion.place, bf16[1024,768]{1,0:T(8,128)(2,1)} %get-tuple-element.79.left, bf16[1024,3072]{1,0:T(8,128)(2,1)} %get-tuple-element.55.grad_u.rest_0_), custom_call_target="tpu_custom_call" | custom-call | flops 4831838208 | bytes 12582912 | tf_op jit(solution)/shard_map/fc_grad/pallas_call | solution.py:599
  318.7 9.4 %qkv_grad.1 = (bf16[4,4,48,1152]{3,2,1,0:T(8,128)(2,1)}, bf16[4,4,48,1152]{3,2,1,0:T(8,128)(2,1)}) custom-call(s32[2]{0:T(128)} %pad_add_fusion.place, bf16[1024,768]{1,0:T(8,128)(2,1)} %get-tuple-element.73.left, bf16[1024,768]{1,0:T(8,128)(2,1)} %copy-done, bf16[1024,768]{1,0:T(8,128)(2,1)} %constant_dynamic-update-slice_fusion.11.dk.rest_1_, ...), custom_call_target="tpu_custom_call" | custom-call | flops 3623878656 | bytes 9830400 | tf_op jit(solution)/shard_map/qkv_grad/pallas_call | solution.py:599
  329.6 1.0 collective-permute-start.45
  331.8 4.0 collective-permute-done.45
  337.1 1.1 collective-permute-start.44
  338.2 2.0 collective-permute-done.46
  340.2 3.0 collective-permute-start.47
  343.8 2.0 collective-permute-done.47
  346.4 1.0 collective-permute-start.37
  347.5 2.4 collective-permute-done.48
  350.6 5.5 %collective-permute-done.37 = bf16[4,48,1152]{2,1,0:T(8,128)(2,1)S(1)} collective-permute-done((bf16[4,48,1152]{2,1,0:T(8,128)(2,1)S(1)}, bf16[4,48,1152]{2,1,0:T(8,128)(2,1)S(1)}, u32[]{:S(2)}, u32[]{:S(2)}) %collective-permute-start.37) | collective-permute-done | bytes 442400 | tf_op jit(solution)/shard_map/ppermute | solution.py:59
  356.8 6.3 %collective-permute-done.35 = bf16[4,48,1152]{2,1,0:T(8,128)(2,1)S(1)} collective-permute-done((bf16[4,48,1152]{2,1,0:T(8,128)(2,1)S(1)}, bf16[4,48,1152]{2,1,0:T(8,128)(2,1)S(1)}, u32[]{:S(2)}, u32[]{:S(2)}) %collective-permute-start.35) | collective-permute-done | bytes 442400 | tf_op jit(solution)/shard_map/ppermute | solution.py:59
  363.1 1.0 collective-permute-start.36
  364.1 3.2 collective-permute-done.38
  367.4 2.7 collective-permute-start.39
  370.8 8.8 %collective-permute-done.39 = bf16[2,48,1152]{2,1,0:T(8,128)(2,1)S(1)} collective-permute-done((bf16[2,48,1152]{2,1,0:T(8,128)(2,1)S(1)}, bf16[2,48,1152]{2,1,0:T(8,128)(2,1)S(1)}, u32[]{:S(2)}, u32[]{:S(2)}) %collective-permute-start.39) | collective-permute-done | bytes 221216 | tf_op jit(solution)/shard_map/ppermute | solution.py:59
  382.2 2.6 collective-permute-done.40
  385.7 1.0 collective-permute-start.61
  387.4 9.5 %collective-permute-done.53 = bf16[4,48,1536]{2,1,0:T(8,128)(2,1)S(1)} collective-permute-done((bf16[4,48,1536]{2,1,0:T(8,128)(2,1)S(1)}, bf16[4,48,1536]{2,1,0:T(8,128)(2,1)S(1)}, u32[]{:S(2)}, u32[]{:S(2)}) %collective-permute-start.53) | collective-permute-done | bytes 589856 | tf_op jit(solution)/shard_map/ppermute | solution.py:59
  397.9 1.1 collective-permute-start.52
  399.1 10.4 %collective-permute-done.61 = bf16[4,192,384]{2,1,0:T(8,128)(2,1)S(1)} collective-permute-done((bf16[4,192,384]{2,1,0:T(8,128)(2,1)S(1)}, bf16[4,192,384]{2,1,0:T(8,128)(2,1)S(1)}, u32[]{:S(2)}, u32[]{:S(2)}) %collective-permute-start.61) | collective-permute-done | bytes 589856 | tf_op jit(solution)/shard_map/ppermute | solution.py:59
  410.2 6.6 %collective-permute-done.54 = bf16[2,48,1536]{2,1,0:T(8,128)(2,1)S(1)} collective-permute-done((bf16[2,48,1536]{2,1,0:T(8,128)(2,1)S(1)}, bf16[2,48,1536]{2,1,0:T(8,128)(2,1)S(1)}, u32[]{:S(2)}, u32[]{:S(2)}) %collective-permute-start.54) | collective-permute-done | bytes 294944 | tf_op jit(solution)/shard_map/ppermute | solution.py:59
  416.9 3.3 collective-permute-start.55
  420.3 1.1 collective-permute-start.60
  422.0 1.7 collective-permute-start.63
  423.7 14.3 %collective-permute-done.55 = bf16[2,48,1536]{2,1,0:T(8,128)(2,1)S(1)} collective-permute-done((bf16[2,48,1536]{2,1,0:T(8,128)(2,1)S(1)}, bf16[2,48,1536]{2,1,0:T(8,128)(2,1)S(1)}, u32[]{:S(2)}, u32[]{:S(2)}) %collective-permute-start.55) | collective-permute-done | bytes 294944 | tf_op jit(solution)/shard_map/ppermute | solution.py:59
  438.3 5.2 %collective-permute-done.63 = bf16[2,192,384]{2,1,0:T(8,128)(2,1)S(1)} collective-permute-done((bf16[2,192,384]{2,1,0:T(8,128)(2,1)S(1)}, bf16[2,192,384]{2,1,0:T(8,128)(2,1)S(1)}, u32[]{:S(2)}, u32[]{:S(2)}) %collective-permute-start.63) | collective-permute-done | bytes 294944 | tf_op jit(solution)/shard_map/ppermute | solution.py:59
  443.7 2.9 collective-permute-done.56
  446.8 2.9 collective-permute-done.64
  (262 shorter events, 43.5 us)
Async XLA Ops:
  6.2 2.7 collective-permute-start
  7.4 10.5 %collective-permute-start.16 = (bf16[24,384]{1,0:T(8,128)(2,1)S(1)}, bf16[24,384]{1,0:T(8,128)(2,1)S(1)}, u32[]{:S(2)}, u32[]{:S(2)}) collective-permute-start(bf16[24,384]{1,0:T(8,128)(2,1)S(1)} %broadcast_select_fusion.22), channel_id=1, source_target_pairs={{0,1},{1,0},{2,3},{3,2},{4,5},{5,4},{6,7},{7,6},{8,9},{9,8},{10,11... | collective-permute-start | bytes 55304 | tf_op jit(solution)/shard_map/ppermute | solution.py:59
  8.3 10.4 %collective-permute-start.5 = (bf16[24,1152]{1,0:T(8,128)(2,1)S(1)}, bf16[24,1152]{1,0:T(8,128)(2,1)S(1)}, u32[]{:S(2)}, u32[]{:S(2)}) collective-permute-start(bf16[24,1152]{1,0:T(8,128)(2,1)S(1)} %broadcast_select_fusion.16), channel_id=1, source_target_pairs={{0,1},{1,0},{2,3},{3,2},{4,5},{5,4},{6,7},{7,6},{8,9},{9,8},{10,11... | collective-permute-start | bytes 165896 | tf_op jit(solution)/shard_map/ppermute | solution.py:59
  8.9 4.1 collective-permute-start.1
  12.4 8.9 %collective-permute-start.18 = (bf16[96,384]{1,0:T(8,128)(2,1)S(1)}, bf16[96,384]{1,0:T(8,128)(2,1)S(1)}, u32[]{:S(2)}, u32[]{:S(2)}) collective-permute-start(bf16[96,384]{1,0:T(8,128)(2,1)S(1)} %broadcast_select_fusion.4), channel_id=1, source_target_pairs={{0,1},{1,0},{2,3},{3,2},{4,5},{5,4},{6,7},{7,6},{8,9},{9,8},{10,11... | collective-permute-start | bytes 221192 | tf_op jit(solution)/shard_map/ppermute | solution.py:59
  13.0 4.8 %collective-permute-start.2 = (bf16[4,288]{1,0:T(4,128)(2,1)S(1)}, bf16[4,288]{1,0:T(4,128)(2,1)S(1)}, u32[]{:S(2)}, u32[]{:S(2)}) collective-permute-start(bf16[4,288]{1,0:T(4,128)(2,1)S(1)} %pad_maximum_fusion.12), channel_id=1, source_target_pairs={{0,4},{1,5},{2,6},{3,7},{4,0},{5,1},{6,2},{7,3},{8,12},{9,13},{10,... | collective-permute-start | bytes 6920 | tf_op jit(solution)/shard_map/ppermute | solution.py:59
  16.1 5.1 %collective-permute-start.17 = (bf16[24,1536]{1,0:T(8,128)(2,1)S(1)}, bf16[24,1536]{1,0:T(8,128)(2,1)S(1)}, u32[]{:S(2)}, u32[]{:S(2)}) collective-permute-start(bf16[24,1536]{1,0:T(8,128)(2,1)S(1)} %broadcast_select_fusion.10), channel_id=1, source_target_pairs={{0,1},{1,0},{2,3},{3,2},{4,5},{5,4},{6,7},{7,6},{8,9},{9,8},{10,11... | collective-permute-start | bytes 221192 | tf_op jit(solution)/shard_map/ppermute | solution.py:59
  19.6 5.9 %collective-permute-start.6 = (bf16[48,1152]{1,0:T(8,128)(2,1)S(1)}, bf16[48,1152]{1,0:T(8,128)(2,1)S(1)}, u32[]{:S(2)}, u32[]{:S(2)}) collective-permute-start(bf16[48,1152]{1,0:T(8,128)(2,1)S(1)} %get-tuple-element.115), channel_id=1, source_target_pairs={{0,8},{1,9},{2,10},{3,11},{4,12},{5,13},{6,14},{7,15},{8,0},{9,1},... | collective-permute-start | bytes 331784 | tf_op jit(solution)/shard_map/ppermute | solution.py:59
  21.4 10.9 %collective-permute-start.19 = (bf16[48,3456]{1,0:T(8,128)(2,1)S(1)}, bf16[48,3456]{1,0:T(8,128)(2,1)S(1)}, u32[]{:S(2)}, u32[]{:S(2)}) collective-permute-start(bf16[48,3456]{1,0:T(8,128)(2,1)S(1)} %constant_dynamic-update-slice_fusion.2), channel_id=1, source_target_pairs={{0,8},{1,9},{2,10},{3,11},{4,12},{5,13},{6,14},{7,15},{8,0},{9,1},... | collective-permute-start | bytes 995336 | tf_op jit(solution)/shard_map/ppermute | solution.py:59
  21.9 13.1 %collective-permute-start.3 = (bf16[8,288]{1,0:T(8,128)(2,1)S(1)}, bf16[8,288]{1,0:T(8,128)(2,1)S(1)}, u32[]{:S(2)}, u32[]{:S(2)}) collective-permute-start(bf16[8,288]{1,0:T(8,128)(2,1)S(1)} %pad_maximum_fusion.11), channel_id=1, source_target_pairs={{0,8},{1,9},{2,10},{3,11},{4,12},{5,13},{6,14},{7,15},{8,0},{9,1},... | collective-permute-start | bytes 13832 | tf_op jit(solution)/shard_map/ppermute | solution.py:59
  25.5 12.5 %collective-permute-start.7 = (bf16[2,48,1152]{2,1,0:T(8,128)(2,1)S(1)}, bf16[2,48,1152]{2,1,0:T(8,128)(2,1)S(1)}, u32[]{:S(2)}, u32[]{:S(2)}) collective-permute-start(bf16[2,48,1152]{2,1,0:T(8,128)(2,1)S(1)} %pad_maximum_fusion.5), channel_id=1, source_target_pairs={{0,4},{1,5},{2,6},{3,7},{4,0},{5,1},{6,2},{7,3},{8,12},{9,13},{10,... | collective-permute-start | bytes 663560 | tf_op jit(solution)/shard_map/ppermute | solution.py:59
  32.3 42.4 %collective-permute-start.22 = (bf16[2,48,3456]{2,1,0:T(8,128)(2,1)S(1)}, bf16[2,48,3456]{2,1,0:T(8,128)(2,1)S(1)}, u32[]{:S(2)}, u32[]{:S(2)}) collective-permute-start(bf16[2,48,3456]{2,1,0:T(8,128)(2,1)S(1)} %pad_maximum_fusion.1), channel_id=1, source_target_pairs={{0,16},{1,17},{2,18},{3,19},{4,20},{5,21},{6,22},{7,23},{8,24},{9,... | collective-permute-start | bytes 1990664 | tf_op jit(solution)/shard_map/ppermute | solution.py:59
  35.0 64.1 %collective-permute-start.4 = (bf16[16,288]{1,0:T(8,128)(2,1)S(1)}, bf16[16,288]{1,0:T(8,128)(2,1)S(1)}, u32[]{:S(2)}, u32[]{:S(2)}) collective-permute-start(bf16[16,288]{1,0:T(8,128)(2,1)S(1)} %pad_maximum_fusion.9), channel_id=1, source_target_pairs={{0,16},{1,17},{2,18},{3,19},{4,20},{5,21},{6,22},{7,23},{8,24},{9,... | collective-permute-start | bytes 27656 | tf_op jit(solution)/shard_map/ppermute | solution.py:59
  35.4 38.5 %collective-permute-start.9 = (bf16[2,48,1152]{2,1,0:T(8,128)(2,1)S(1)}, bf16[2,48,1152]{2,1,0:T(8,128)(2,1)S(1)}, u32[]{:S(2)}, u32[]{:S(2)}) collective-permute-start(bf16[2,48,1152]{2,1,0:T(8,128)(2,1)S(1)} %pad_maximum_fusion.5), channel_id=1, source_target_pairs={{0,16},{1,17},{2,18},{3,19},{4,20},{5,21},{6,22},{7,23},{8,24},{9,... | collective-permute-start | bytes 663560 | tf_op jit(solution)/shard_map/ppermute | solution.py:59
  38.1 63.5 %collective-permute-start.12 = (bf16[4,48,1152]{2,1,0:T(8,128)(2,1)S(1)}, bf16[4,48,1152]{2,1,0:T(8,128)(2,1)}, u32[]{:S(2)}, u32[]{:S(2)}) collective-permute-start(bf16[4,48,1152]{2,1,0:T(8,128)(2,1)S(1)} %pad_maximum_fusion.2.rest_0_), channel_id=1, source_target_pairs={{0,1},{1,0},{2,3},{3,2},{4,5},{5,4},{6,7},{7,6},{8,9},{9,8},{10,11... | collective-permute-start | bytes 1327112 | tf_op jit(solution)/shard_map/ppermute | solution.py:59
  38.2 63.5 %collective-permute-start.8 = (bf16[4,48,1152]{2,1,0:T(8,128)(2,1)S(1)}, bf16[4,48,1152]{2,1,0:T(8,128)(2,1)}, u32[]{:S(2)}, u32[]{:S(2)}) collective-permute-start(bf16[4,48,1152]{2,1,0:T(8,128)(2,1)S(1)} %pad_maximum_fusion.2.rest_0_), channel_id=1, source_target_pairs={{0,2},{1,3},{2,0},{3,1},{4,6},{5,7},{6,4},{7,5},{8,10},{9,11},{10,... | collective-permute-start | bytes 1327112 | tf_op jit(solution)/shard_map/ppermute | solution.py:59
  74.0 15.8 %collective-permute-start.20 = (bf16[2,48,3456]{2,1,0:T(8,128)(2,1)S(1)}, bf16[2,48,3456]{2,1,0:T(8,128)(2,1)S(1)}, u32[]{:S(2)}, u32[]{:S(2)}) collective-permute-start(bf16[2,48,3456]{2,1,0:T(8,128)(2,1)S(1)} %pad_maximum_fusion.1), channel_id=1, source_target_pairs={{0,4},{1,5},{2,6},{3,7},{4,0},{5,1},{6,2},{7,3},{8,12},{9,13},{10,... | collective-permute-start | bytes 1990664 | tf_op jit(solution)/shard_map/ppermute | solution.py:59
  74.7 16.7 %collective-permute-start.23 = (bf16[2,48,3456]{2,1,0:T(8,128)(2,1)S(1)}, bf16[2,48,3456]{2,1,0:T(8,128)(2,1)S(1)}, u32[]{:S(2)}, u32[]{:S(2)}) collective-permute-start(bf16[2,48,3456]{2,1,0:T(8,128)(2,1)S(1)} %collective-permute-done.22), channel_id=1, source_target_pairs={{0,2},{1,3},{2,0},{3,1},{4,6},{5,7},{6,4},{7,5},{8,10},{9,11},{10,... | collective-permute-start | bytes 1990664 | tf_op jit(solution)/shard_map/ppermute | solution.py:59
  89.7 8.4 %collective-permute-start.10 = (bf16[2,48,1152]{2,1,0:T(8,128)(2,1)S(1)}, bf16[2,48,1152]{2,1,0:T(8,128)(2,1)S(1)}, u32[]{:S(2)}, u32[]{:S(2)}) collective-permute-start(bf16[2,48,1152]{2,1,0:T(8,128)(2,1)S(1)} %collective-permute-done.9), channel_id=1, source_target_pairs={{0,2},{1,3},{2,0},{3,1},{4,6},{5,7},{6,4},{7,5},{8,10},{9,11},{10,... | collective-permute-start | bytes 663560 | tf_op jit(solution)/shard_map/ppermute | solution.py:59
  91.4 58.7 %collective-permute-start.21 = (bf16[4,48,3456]{2,1,0:T(8,128)(2,1)S(1)}, bf16[4,48,3456]{2,1,0:T(8,128)(2,1)}, u32[]{:S(2)}, u32[]{:S(2)}) collective-permute-start(bf16[4,48,3456]{2,1,0:T(8,128)(2,1)S(1)} %pad_maximum_fusion.rest_0_), channel_id=1, source_target_pairs={{0,2},{1,3},{2,0},{3,1},{4,6},{5,7},{6,4},{7,5},{8,10},{9,11},{10,... | collective-permute-start | bytes 3981320 | tf_op jit(solution)/shard_map/ppermute | solution.py:59
  98.1 52.5 %collective-permute-start.24 = (bf16[4,48,3456]{2,1,0:T(8,128)(2,1)S(1)}, bf16[4,48,3456]{2,1,0:T(8,128)(2,1)}, u32[]{:S(2)}, u32[]{:S(2)}) collective-permute-start(bf16[4,48,3456]{2,1,0:T(8,128)(2,1)S(1)} %constant_dynamic-update-slice_fusion.7.rest_2_), channel_id=1, source_target_pairs={{0,4},{1,5},{2,6},{3,7},{4,0},{5,1},{6,2},{7,3},{8,12},{9,13},{10,... | collective-permute-start | bytes 3981320 | tf_op jit(solution)/shard_map/ppermute | solution.py:59
  99.1 35.3 %collective-permute-start.11 = (bf16[4,48,1152]{2,1,0:T(8,128)(2,1)}, bf16[4,48,1152]{2,1,0:T(8,128)(2,1)}, u32[]{:S(2)}, u32[]{:S(2)}) collective-permute-start(bf16[4,48,1152]{2,1,0:T(8,128)(2,1)} %constant_dynamic-update-slice_fusion.rest_2_), channel_id=1, source_target_pairs={{0,4},{1,5},{2,6},{3,7},{4,0},{5,1},{6,2},{7,3},{8,12},{9,13},{10,... | collective-permute-start | bytes 1327112 | tf_op jit(solution)/shard_map/ppermute | solution.py:59
  101.6 38.3 %collective-permute-start.14 = (bf16[4,48,1152]{2,1,0:T(8,128)(2,1)}, bf16[4,48,1152]{2,1,0:T(8,128)(2,1)}, u32[]{:S(2)}, u32[]{:S(2)}) collective-permute-start(bf16[4,48,1152]{2,1,0:T(8,128)(2,1)} %constant_dynamic-update-slice_fusion.rest_2_), channel_id=1, source_target_pairs={{0,1},{1,0},{2,3},{3,2},{4,5},{5,4},{6,7},{7,6},{8,9},{9,8},{10,11... | collective-permute-start | bytes 1327112 | tf_op jit(solution)/shard_map/ppermute | solution.py:59
  101.7 38.7 %collective-permute-start.13 = (bf16[4,48,1152]{2,1,0:T(8,128)(2,1)}, bf16[4,48,1152]{2,1,0:T(8,128)(2,1)}, u32[]{:S(2)}, u32[]{:S(2)}) collective-permute-start(bf16[4,48,1152]{2,1,0:T(8,128)(2,1)} %collective-permute-done.8.rest_1_), channel_id=1, source_target_pairs={{0,1},{1,0},{2,3},{3,2},{4,5},{5,4},{6,7},{7,6},{8,9},{9,8},{10,11... | collective-permute-start | bytes 1327112 | tf_op jit(solution)/shard_map/ppermute | solution.py:59
  134.4 6.0 %collective-permute-start.15 = (bf16[4,48,1152]{2,1,0:T(8,128)(2,1)}, bf16[4,48,1152]{2,1,0:T(8,128)(2,1)}, u32[]{:S(2)}, u32[]{:S(2)}) collective-permute-start(bf16[4,48,1152]{2,1,0:T(8,128)(2,1)} %collective-permute-done.11.rest_3_), channel_id=1, source_target_pairs={{0,1},{1,0},{2,3},{3,2},{4,5},{5,4},{6,7},{7,6},{8,9},{9,8},{10,11... | collective-permute-start | bytes 1327112 | tf_op jit(solution)/shard_map/ppermute | solution.py:59
  139.9 31.1 %collective-permute-start.25 = (bf16[4,48,3456]{2,1,0:T(8,128)(2,1)S(1)}, bf16[4,48,3456]{2,1,0:T(8,128)(2,1)S(1)}, u32[]{:S(2)}, u32[]{:S(2)}) collective-permute-start(bf16[4,48,3456]{2,1,0:T(8,128)(2,1)S(1)} %pad_maximum_fusion.rest_0_), channel_id=1, source_target_pairs={{0,1},{1,0},{2,3},{3,2},{4,5},{5,4},{6,7},{7,6},{8,9},{9,8},{10,11... | collective-permute-start | bytes 3981320 | tf_op jit(solution)/shard_map/ppermute | solution.py:59
  150.0 20.9 %collective-permute-start.27 = (bf16[4,48,3456]{2,1,0:T(8,128)(2,1)S(1)}, bf16[4,48,3456]{2,1,0:T(8,128)(2,1)S(1)}, u32[]{:S(2)}, u32[]{:S(2)}) collective-permute-start(bf16[4,48,3456]{2,1,0:T(8,128)(2,1)S(1)} %constant_dynamic-update-slice_fusion.7.rest_2_), channel_id=1, source_target_pairs={{0,1},{1,0},{2,3},{3,2},{4,5},{5,4},{6,7},{7,6},{8,9},{9,8},{10,11... | collective-permute-start | bytes 3981320 | tf_op jit(solution)/shard_map/ppermute | solution.py:59
  150.1 20.8 %collective-permute-start.26 = (bf16[4,48,3456]{2,1,0:T(8,128)(2,1)}, bf16[4,48,3456]{2,1,0:T(8,128)(2,1)S(1)}, u32[]{:S(2)}, u32[]{:S(2)}) collective-permute-start(bf16[4,48,3456]{2,1,0:T(8,128)(2,1)} %collective-permute-done.21.rest_1_), channel_id=1, source_target_pairs={{0,1},{1,0},{2,3},{3,2},{4,5},{5,4},{6,7},{7,6},{8,9},{9,8},{10,11... | collective-permute-start | bytes 3981320 | tf_op jit(solution)/shard_map/ppermute | solution.py:59
  150.6 20.4 %collective-permute-start.28 = (bf16[4,48,3456]{2,1,0:T(8,128)(2,1)}, bf16[4,48,3456]{2,1,0:T(8,128)(2,1)}, u32[]{:S(2)}, u32[]{:S(2)}) collective-permute-start(bf16[4,48,3456]{2,1,0:T(8,128)(2,1)} %collective-permute-done.24.rest_3_), channel_id=1, source_target_pairs={{0,1},{1,0},{2,3},{3,2},{4,5},{5,4},{6,7},{7,6},{8,9},{9,8},{10,11... | collective-permute-start | bytes 3981320 | tf_op jit(solution)/shard_map/ppermute | solution.py:59
  279.7 4.8 %collective-permute-start.29 = (f32[16,288]{1,0:T(8,128)S(1)}, f32[16,288]{1,0:T(8,128)S(1)}, u32[]{:S(2)}, u32[]{:S(2)}) collective-permute-start(f32[16,288]{1,0:T(8,128)S(1)} %slice_select_fusion.8), channel_id=1, source_target_pairs={{0,16},{1,17},{2,18},{3,19},{4,20},{5,21},{6,22},{7,23},{8,24},{9,... | collective-permute-start | bytes 55304 | tf_op jit(solution)/shard_map/ppermute | solution.py:59
  284.5 14.4 %collective-permute-start.30 = (f32[8,288]{1,0:T(8,128)S(1)}, f32[8,288]{1,0:T(8,128)S(1)}, u32[]{:S(2)}, u32[]{:S(2)}) collective-permute-start(f32[8,288]{1,0:T(8,128)S(1)} %slice_select_fusion.9), channel_id=1, source_target_pairs={{0,8},{1,9},{2,10},{3,11},{4,12},{5,13},{6,14},{7,15},{8,0},{9,1},... | collective-permute-start | bytes 27656 | tf_op jit(solution)/shard_map/ppermute | solution.py:59
  298.9 5.8 %collective-permute-start.31 = (f32[4,288]{1,0:T(4,128)S(1)}, f32[4,288]{1,0:T(4,128)S(1)}, u32[]{:S(2)}, u32[]{:S(2)}) collective-permute-start(f32[4,288]{1,0:T(4,128)S(1)} %slice_select_fusion.10), channel_id=1, source_target_pairs={{0,4},{1,5},{2,6},{3,7},{4,0},{5,1},{6,2},{7,3},{8,12},{9,13},{10,... | collective-permute-start | bytes 13832 | tf_op jit(solution)/shard_map/ppermute | solution.py:59
  304.7 24.8 %collective-permute-start.42 = (bf16[4,4,48,384]{3,2,1,0:T(8,128)(2,1)}, bf16[4,4,48,384]{3,2,1,0:T(8,128)(2,1)S(1)}, u32[]{:S(2)}, u32[]{:S(2)}) collective-permute-start(bf16[4,4,48,384]{3,2,1,0:T(8,128)(2,1)} %get-tuple-element.78), channel_id=1, source_target_pairs={{0,1},{1,0},{2,3},{3,2},{4,5},{5,4},{6,7},{7,6},{8,9},{9,8},{10,11... | collective-permute-start | bytes 1769480 | tf_op jit(solution)/shard_map/ppermute | solution.py:59
  304.8 13.5 %collective-permute-start.32 = (f32[2,288]{1,0:T(2,128)S(1)}, f32[2,288]{1,0:T(2,128)S(1)}, u32[]{:S(2)}, u32[]{:S(2)}) collective-permute-start(f32[2,288]{1,0:T(2,128)S(1)} %broadcast_select_fusion.32), channel_id=1, source_target_pairs={{0,2},{1,3},{2,0},{3,1},{4,6},{5,7},{6,4},{7,5},{8,10},{9,11},{10,... | collective-permute-start | bytes 6920 | tf_op jit(solution)/shard_map/ppermute | solution.py:59
  318.3 10.5 %collective-permute-start.33 = (f32[1,288]{1,0:T(1,128)S(1)}, f32[1,288]{1,0:T(1,128)S(1)}, u32[]{:S(2)}, u32[]{:S(2)}) collective-permute-start(f32[1,288]{1,0:T(1,128)S(1)} %broadcast_select_fusion.28), channel_id=1, source_target_pairs={{0,1},{1,0},{2,3},{3,2},{4,5},{5,4},{6,7},{7,6},{8,9},{9,8},{10,11... | collective-permute-start | bytes 3464 | tf_op jit(solution)/shard_map/ppermute | solution.py:59
  328.1 17.9 %collective-permute-start.34 = (bf16[4,4,48,1152]{3,2,1,0:T(8,128)(2,1)}, bf16[4,4,48,1152]{3,2,1,0:T(8,128)(2,1)S(1)}, u32[]{:S(2)}, u32[]{:S(2)}) collective-permute-start(bf16[4,4,48,1152]{3,2,1,0:T(8,128)(2,1)} %get-tuple-element.75), channel_id=1, source_target_pairs={{0,1},{1,0},{2,3},{3,2},{4,5},{5,4},{6,7},{7,6},{8,9},{9,8},{10,11... | collective-permute-start | bytes 5308424 | tf_op jit(solution)/shard_map/ppermute | solution.py:59
  328.3 51.5 %collective-permute-start.50 = (bf16[4,4,48,1536]{3,2,1,0:T(8,128)(2,1)S(1)}, bf16[4,4,48,1536]{3,2,1,0:T(8,128)(2,1)S(1)}, u32[]{:S(2)}, u32[]{:S(2)}) collective-permute-start(bf16[4,4,48,1536]{3,2,1,0:T(8,128)(2,1)S(1)} %copy-done.21), channel_id=1, source_target_pairs={{0,1},{1,0},{2,3},{3,2},{4,5},{5,4},{6,7},{7,6},{8,9},{9,8},{10,11... | collective-permute-start | bytes 7077896 | tf_op jit(solution)/shard_map/ppermute | solution.py:59
  328.7 56.3 %collective-permute-start.58 = (bf16[4,4,192,384]{3,2,1,0:T(8,128)(2,1)S(1)}, bf16[4,4,192,384]{3,2,1,0:T(8,128)(2,1)S(1)}, u32[]{:S(2)}, u32[]{:S(2)}) collective-permute-start(bf16[4,4,192,384]{3,2,1,0:T(8,128)(2,1)S(1)} %copy-done.20), channel_id=1, source_target_pairs={{0,1},{1,0},{2,3},{3,2},{4,5},{5,4},{6,7},{7,6},{8,9},{9,8},{10,11... | collective-permute-start | bytes 7077896 | tf_op jit(solution)/shard_map/ppermute | solution.py:59
  329.6 6.1 %collective-permute-start.45 = (bf16[4,48,384]{2,1,0:T(8,128)(2,1)S(1)}, bf16[4,48,384]{2,1,0:T(8,128)(2,1)S(1)}, u32[]{:S(2)}, u32[]{:S(2)}) collective-permute-start(bf16[4,48,384]{2,1,0:T(8,128)(2,1)S(1)} %get-tuple-element.97), channel_id=1, source_target_pairs={{0,4},{1,5},{2,6},{3,7},{4,0},{5,1},{6,2},{7,3},{8,12},{9,13},{10,... | collective-permute-start | bytes 442376 | tf_op jit(solution)/shard_map/ppermute | solution.py:59
  331.2 5.8 %collective-permute-start.43 = (bf16[4,48,384]{2,1,0:T(8,128)(2,1)S(1)}, bf16[4,48,384]{2,1,0:T(8,128)(2,1)S(1)}, u32[]{:S(2)}, u32[]{:S(2)}) collective-permute-start(bf16[4,48,384]{2,1,0:T(8,128)(2,1)S(1)} %get-tuple-element.99), channel_id=1, source_target_pairs={{0,2},{1,3},{2,0},{3,1},{4,6},{5,7},{6,4},{7,5},{8,10},{9,11},{10,... | collective-permute-start | bytes 442376 | tf_op jit(solution)/shard_map/ppermute | solution.py:59
  335.8 4.4 collective-permute-start.46
  337.1 6.8 %collective-permute-start.44 = (bf16[2,48,384]{2,1,0:T(8,128)(2,1)S(1)}, bf16[2,48,384]{2,1,0:T(8,128)(2,1)S(1)}, u32[]{:S(2)}, u32[]{:S(2)}) collective-permute-start(bf16[2,48,384]{2,1,0:T(8,128)(2,1)S(1)} %fusion.27), channel_id=1, source_target_pairs={{0,4},{1,5},{2,6},{3,7},{4,0},{5,1},{6,2},{7,3},{8,12},{9,13},{10,... | collective-permute-start | bytes 221192 | tf_op jit(solution)/shard_map/ppermute | solution.py:59
  340.2 5.6 %collective-permute-start.47 = (bf16[2,48,384]{2,1,0:T(8,128)(2,1)S(1)}, bf16[2,48,384]{2,1,0:T(8,128)(2,1)S(1)}, u32[]{:S(2)}, u32[]{:S(2)}) collective-permute-start(bf16[2,48,384]{2,1,0:T(8,128)(2,1)S(1)} %add_convert_fusion.19), channel_id=1, source_target_pairs={{0,16},{1,17},{2,18},{3,19},{4,20},{5,21},{6,22},{7,23},{8,24},{9,... | collective-permute-start | bytes 221192 | tf_op jit(solution)/shard_map/ppermute | solution.py:59
  345.9 4.0 collective-permute-start.48
  346.4 9.6 %collective-permute-start.37 = (bf16[4,48,1152]{2,1,0:T(8,128)(2,1)S(1)}, bf16[4,48,1152]{2,1,0:T(8,128)(2,1)S(1)}, u32[]{:S(2)}, u32[]{:S(2)}) collective-permute-start(bf16[4,48,1152]{2,1,0:T(8,128)(2,1)S(1)} %get-tuple-element.93), channel_id=1, source_target_pairs={{0,4},{1,5},{2,6},{3,7},{4,0},{5,1},{6,2},{7,3},{8,12},{9,13},{10,... | collective-permute-start | bytes 1327112 | tf_op jit(solution)/shard_map/ppermute | solution.py:59
  349.9 20.2 %collective-permute-start.49 = (f32[24,384]{1,0:T(8,128)S(1)}, f32[24,384]{1,0:T(8,128)S(1)}, u32[]{:S(2)}, u32[]{:S(2)}) collective-permute-start(f32[24,384]{1,0:T(8,128)S(1)} %slice_select_fusion.6), channel_id=1, source_target_pairs={{0,1},{1,0},{2,3},{3,2},{4,5},{5,4},{6,7},{7,6},{8,9},{9,8},{10,11... | collective-permute-start | bytes 110600 | tf_op jit(solution)/shard_map/ppermute | solution.py:59
  350.0 13.0 %collective-permute-start.35 = (bf16[4,48,1152]{2,1,0:T(8,128)(2,1)S(1)}, bf16[4,48,1152]{2,1,0:T(8,128)(2,1)S(1)}, u32[]{:S(2)}, u32[]{:S(2)}) collective-permute-start(bf16[4,48,1152]{2,1,0:T(8,128)(2,1)S(1)} %get-tuple-element.95), channel_id=1, source_target_pairs={{0,2},{1,3},{2,0},{3,1},{4,6},{5,7},{6,4},{7,5},{8,10},{9,11},{10,... | collective-permute-start | bytes 1327112 | tf_op jit(solution)/shard_map/ppermute | solution.py:59
  356.1 11.2 %collective-permute-start.38 = (bf16[2,48,1152]{2,1,0:T(8,128)(2,1)S(1)}, bf16[2,48,1152]{2,1,0:T(8,128)(2,1)S(1)}, u32[]{:S(2)}, u32[]{:S(2)}) collective-permute-start(bf16[2,48,1152]{2,1,0:T(8,128)(2,1)S(1)} %fusion.14), channel_id=1, source_target_pairs={{0,2},{1,3},{2,0},{3,1},{4,6},{5,7},{6,4},{7,5},{8,10},{9,11},{10,... | collective-permute-start | bytes 663560 | tf_op jit(solution)/shard_map/ppermute | solution.py:59
  363.1 7.7 %collective-permute-start.36 = (bf16[2,48,1152]{2,1,0:T(8,128)(2,1)S(1)}, bf16[2,48,1152]{2,1,0:T(8,128)(2,1)S(1)}, u32[]{:S(2)}, u32[]{:S(2)}) collective-permute-start(bf16[2,48,1152]{2,1,0:T(8,128)(2,1)S(1)} %fusion.16), channel_id=1, source_target_pairs={{0,4},{1,5},{2,6},{3,7},{4,0},{5,1},{6,2},{7,3},{8,12},{9,13},{10,... | collective-permute-start | bytes 663560 | tf_op jit(solution)/shard_map/ppermute | solution.py:59
  367.4 12.2 %collective-permute-start.39 = (bf16[2,48,1152]{2,1,0:T(8,128)(2,1)S(1)}, bf16[2,48,1152]{2,1,0:T(8,128)(2,1)S(1)}, u32[]{:S(2)}, u32[]{:S(2)}) collective-permute-start(bf16[2,48,1152]{2,1,0:T(8,128)(2,1)S(1)} %add_convert_fusion.14), channel_id=1, source_target_pairs={{0,16},{1,17},{2,18},{3,19},{4,20},{5,21},{6,22},{7,23},{8,24},{9,... | collective-permute-start | bytes 663560 | tf_op jit(solution)/shard_map/ppermute | solution.py:59
  379.8 5.0 %collective-permute-start.40 = (bf16[48,1152]{1,0:T(8,128)(2,1)S(1)}, bf16[48,1152]{1,0:T(8,128)(2,1)S(1)}, u32[]{:S(2)}, u32[]{:S(2)}) collective-permute-start(bf16[48,1152]{1,0:T(8,128)(2,1)S(1)} %fusion.29), channel_id=1, source_target_pairs={{0,8},{1,9},{2,10},{3,11},{4,12},{5,13},{6,14},{7,15},{8,0},{9,1},... | collective-permute-start | bytes 331784 | tf_op jit(solution)/shard_map/ppermute | solution.py:59
  380.6 16.3 %collective-permute-start.53 = (bf16[4,48,1536]{2,1,0:T(8,128)(2,1)S(1)}, bf16[4,48,1536]{2,1,0:T(8,128)(2,1)S(1)}, u32[]{:S(2)}, u32[]{:S(2)}) collective-permute-start(bf16[4,48,1536]{2,1,0:T(8,128)(2,1)S(1)} %get-tuple-element.89), channel_id=1, source_target_pairs={{0,4},{1,5},{2,6},{3,7},{4,0},{5,1},{6,2},{7,3},{8,12},{9,13},{10,... | collective-permute-start | bytes 1769480 | tf_op jit(solution)/shard_map/ppermute | solution.py:59
  381.6 16.2 %collective-permute-start.51 = (bf16[4,48,1536]{2,1,0:T(8,128)(2,1)S(1)}, bf16[4,48,1536]{2,1,0:T(8,128)(2,1)S(1)}, u32[]{:S(2)}, u32[]{:S(2)}) collective-permute-start(bf16[4,48,1536]{2,1,0:T(8,128)(2,1)S(1)} %get-tuple-element.91), channel_id=1, source_target_pairs={{0,2},{1,3},{2,0},{3,1},{4,6},{5,7},{6,4},{7,5},{8,10},{9,11},{10,... | collective-permute-start | bytes 1769480 | tf_op jit(solution)/shard_map/ppermute | solution.py:59
  385.7 23.8 %collective-permute-start.61 = (bf16[4,192,384]{2,1,0:T(8,128)(2,1)S(1)}, bf16[4,192,384]{2,1,0:T(8,128)(2,1)S(1)}, u32[]{:S(2)}, u32[]{:S(2)}) collective-permute-start(bf16[4,192,384]{2,1,0:T(8,128)(2,1)S(1)} %get-tuple-element.85), channel_id=1, source_target_pairs={{0,4},{1,5},{2,6},{3,7},{4,0},{5,1},{6,2},{7,3},{8,12},{9,13},{10,... | collective-permute-start | bytes 1769480 | tf_op jit(solution)/shard_map/ppermute | solution.py:59
  386.7 33.5 %collective-permute-start.59 = (bf16[4,192,384]{2,1,0:T(8,128)(2,1)S(1)}, bf16[4,192,384]{2,1,0:T(8,128)(2,1)S(1)}, u32[]{:S(2)}, u32[]{:S(2)}) collective-permute-start(bf16[4,192,384]{2,1,0:T(8,128)(2,1)S(1)} %get-tuple-element.87), channel_id=1, source_target_pairs={{0,2},{1,3},{2,0},{3,1},{4,6},{5,7},{6,4},{7,5},{8,10},{9,11},{10,... | collective-permute-start | bytes 1769480 | tf_op jit(solution)/shard_map/ppermute | solution.py:59
  396.9 19.9 %collective-permute-start.54 = (bf16[2,48,1536]{2,1,0:T(8,128)(2,1)S(1)}, bf16[2,48,1536]{2,1,0:T(8,128)(2,1)S(1)}, u32[]{:S(2)}, u32[]{:S(2)}) collective-permute-start(bf16[2,48,1536]{2,1,0:T(8,128)(2,1)S(1)} %fusion.8), channel_id=1, source_target_pairs={{0,2},{1,3},{2,0},{3,1},{4,6},{5,7},{6,4},{7,5},{8,10},{9,11},{10,... | collective-permute-start | bytes 884744 | tf_op jit(solution)/shard_map/ppermute | solution.py:59
  397.9 25.8 %collective-permute-start.52 = (bf16[2,48,1536]{2,1,0:T(8,128)(2,1)S(1)}, bf16[2,48,1536]{2,1,0:T(8,128)(2,1)S(1)}, u32[]{:S(2)}, u32[]{:S(2)}) collective-permute-start(bf16[2,48,1536]{2,1,0:T(8,128)(2,1)S(1)} %fusion.10), channel_id=1, source_target_pairs={{0,4},{1,5},{2,6},{3,7},{4,0},{5,1},{6,2},{7,3},{8,12},{9,13},{10,... | collective-permute-start | bytes 884744 | tf_op jit(solution)/shard_map/ppermute | solution.py:59
  409.6 12.3 %collective-permute-start.62 = (bf16[2,192,384]{2,1,0:T(8,128)(2,1)S(1)}, bf16[2,192,384]{2,1,0:T(8,128)(2,1)S(1)}, u32[]{:S(2)}, u32[]{:S(2)}) collective-permute-start(bf16[2,192,384]{2,1,0:T(8,128)(2,1)S(1)} %fusion.4), channel_id=1, source_target_pairs={{0,2},{1,3},{2,0},{3,1},{4,6},{5,7},{6,4},{7,5},{8,10},{9,11},{10,... | collective-permute-start | bytes 884744 | tf_op jit(solution)/shard_map/ppermute | solution.py:59
  416.9 21.1 %collective-permute-start.55 = (bf16[2,48,1536]{2,1,0:T(8,128)(2,1)S(1)}, bf16[2,48,1536]{2,1,0:T(8,128)(2,1)S(1)}, u32[]{:S(2)}, u32[]{:S(2)}) collective-permute-start(bf16[2,48,1536]{2,1,0:T(8,128)(2,1)S(1)} %add_convert_fusion.13), channel_id=1, source_target_pairs={{0,16},{1,17},{2,18},{3,19},{4,20},{5,21},{6,22},{7,23},{8,24},{9,... | collective-permute-start | bytes 884744 | tf_op jit(solution)/shard_map/ppermute | solution.py:59
  420.3 18.0 %collective-permute-start.60 = (bf16[2,192,384]{2,1,0:T(8,128)(2,1)S(1)}, bf16[2,192,384]{2,1,0:T(8,128)(2,1)S(1)}, u32[]{:S(2)}, u32[]{:S(2)}) collective-permute-start(bf16[2,192,384]{2,1,0:T(8,128)(2,1)S(1)} %fusion.6), channel_id=1, source_target_pairs={{0,4},{1,5},{2,6},{3,7},{4,0},{5,1},{6,2},{7,3},{8,12},{9,13},{10,... | collective-permute-start | bytes 884744 | tf_op jit(solution)/shard_map/ppermute | solution.py:59
  422.0 21.5 %collective-permute-start.63 = (bf16[2,192,384]{2,1,0:T(8,128)(2,1)S(1)}, bf16[2,192,384]{2,1,0:T(8,128)(2,1)S(1)}, u32[]{:S(2)}, u32[]{:S(2)}) collective-permute-start(bf16[2,192,384]{2,1,0:T(8,128)(2,1)S(1)} %add_convert_fusion.12), channel_id=1, source_target_pairs={{0,16},{1,17},{2,18},{3,19},{4,20},{5,21},{6,22},{7,23},{8,24},{9,... | collective-permute-start | bytes 884744 | tf_op jit(solution)/shard_map/ppermute | solution.py:59
  438.2 8.4 %collective-permute-start.56 = (bf16[48,1536]{1,0:T(8,128)(2,1)S(1)}, bf16[48,1536]{1,0:T(8,128)(2,1)S(1)}, u32[]{:S(2)}, u32[]{:S(2)}) collective-permute-start(bf16[48,1536]{1,0:T(8,128)(2,1)S(1)} %fusion.23), channel_id=1, source_target_pairs={{0,8},{1,9},{2,10},{3,11},{4,12},{5,13},{6,14},{7,15},{8,0},{9,1},... | collective-permute-start | bytes 442376 | tf_op jit(solution)/shard_map/ppermute | solution.py:59
  443.6 6.0 %collective-permute-start.64 = (bf16[192,384]{1,0:T(8,128)(2,1)S(1)}, bf16[192,384]{1,0:T(8,128)(2,1)S(1)}, u32[]{:S(2)}, u32[]{:S(2)}) collective-permute-start(bf16[192,384]{1,0:T(8,128)(2,1)S(1)} %fusion.24), channel_id=1, source_target_pairs={{0,8},{1,9},{2,10},{3,11},{4,12},{5,13},{6,14},{7,15},{8,0},{9,1},... | collective-permute-start | bytes 442376 | tf_op jit(solution)/shard_map/ppermute | solution.py:59
  446.7 3.1 collective-permute-start.57
  (27 other events, 411.0 us)

commit v2 on v1

v2 whole, which is shorter than its diff:
```python
import functools
import math

import jax
import jax.numpy as jnp
from jax import lax
from jax.experimental import pallas as pl
from jax.experimental.pallas import tpu as pltpu
from jax.sharding import PartitionSpec as P

HD = 64
LEN = 1024
PAIR = 2 * HD
EPS = 1e-05
NEG = -1e30
AXES = ("dp", "fsdp")

F32 = jnp.float32
BF16 = jnp.bfloat16
NN = (((1,), (0,)), ((), ()))
NT = (((1,), (1,)), ((), ()))
TN = (((0,), (0,)), ((), ()))
ANY = pl.BlockSpec(memory_space=pl.ANY)
SMEM = pl.BlockSpec(memory_space=pltpu.SMEM)
VMEM_LIMIT = 56 << 20
SHARE = 1.0

CORE, X, Y, Z0, Z1 = 1, 2, 4, 8, 16
CX, CY, CZ0, CZ1 = 1, 2, 4, 8
GROUPS = tuple(tuple(near | far for far in (0, CZ0, CZ1, CZ0 | CZ1)) for near in (0, CX, CY, CX | CY))


def dot(a, b, dims):
    return lax.dot_general(a, b, dims, preferred_element_type=F32)


def params(**more):
    return pltpu.CompilerParams(vmem_limit_bytes=VMEM_LIMIT, **more)


def cost(flops, size):
    return pl.CostEstimate(flops=int(flops * SHARE), bytes_accessed=int(size * SHARE), transcendentals=0)


def whole(shape):
    return pl.BlockSpec(shape, lambda *g: (0,) * len(shape))


def rows(block, width):
    return pl.BlockSpec((block, width), lambda i: (i, 0))


def swap(array, bit):
    count = lax.axis_size("dp") * lax.axis_size("fsdp")
    return lax.ppermute(array, AXES, [(i, i ^ bit) for i in range(count)])


def halves(array, core):
    width = array.shape[1] // 2
    low, high = array[:, :width], array[:, width:]
    first = core == 0
    return jnp.where(first, low, high), jnp.where(first, high, low)


def pair_block(array, core):
    keep, send = halves(array, core)
    other = swap(send, CORE)
    first = core == 0
    return jnp.concatenate([jnp.where(first, keep, other), jnp.where(first, other, keep)], 0)


def gather_z(block, *after):
    got = tie([swap(block, bits) for bits in (Z0, Z1, Z0 | Z1)], *after)
    return jnp.stack([block] + got)


def gather_xy(column):
    return [column] + [swap(column, bits) for bits in (X, Y, X | Y)]


def gather_core(own):
    return [*own, *(swap(piece, CORE) for piece in own)]


def add(*terms):
    return functools.reduce(lambda a, b: a + b, [t.astype(F32) for t in terms])


def scatter_core(terms):
    mine, other = terms
    got = swap(other, CORE)
    return [add(mine[g], got[g]).astype(BF16) for g in range(4)]


def scatter_xy(sums, *after):
    got = tie([swap(part, bits) for part, bits in zip(sums[1:], (X, Y, X | Y))], *after)
    return [add(*(part[spot] for part in [sums[0]] + got)).astype(BF16) for spot in range(4)]


def scatter_z(sums, *after):
    got = tie([swap(part, bits) for part, bits in zip(sums[1:], (Z0, Z1, Z0 | Z1))], *after)
    return add(sums[0], *got)


def tie(arrays, *others):
    if not others:
        return list(arrays)
    return list(lax.optimization_barrier((*arrays, *others))[: len(arrays)])


def kernel_call(kernel, inputs, after, **how):
    count, extra = len(inputs), len(after)

    def body(*refs):
        kernel(*refs[:count], *refs[count + extra :])

    how["in_specs"] = how["in_specs"] + [ANY] * extra
    return pl.pallas_call(body, **how)(*inputs, *after)


def own_rows(block, core):
    count = block.shape[0] // 2
    low, high = block[:count], block[count:]
    first = core == 0
    keep = jnp.where(first, low, high)
    got = swap(jnp.where(first, high, low), CORE)
    return jnp.where(first, keep, got), jnp.where(first, got, keep)


def gather_all(array):
    return lax.all_gather(array, AXES, axis=0, tiled=True)


def scatter_all(array):
    return lax.psum_scatter(array, AXES, scatter_dimension=0, tiled=True)


def gather_small(vector, index):
    table = vector.reshape(1, -1)
    for bit in (CORE, X, Y, Z0, Z1):
        other = swap(table, bit)
        low = (index & bit) == 0
        table = jnp.concatenate([jnp.where(low, table, other), jnp.where(low, other, table)], 0)
    return table


def scatter_small(table, index):
    for bit in (Z1, Z0, Y, X, CORE):
        count = table.shape[0] // 2
        low = (index & bit) == 0
        keep = jnp.where(low, table[:count], table[count:])
        send = jnp.where(low, table[count:], table[:count])
        table = keep + swap(send, bit)
    return table.reshape(-1)


def fetch(place, pieces, which, lane, width, into, sem):
    if len(pieces) < 8:
        pltpu.make_async_copy(pieces[which], into, sem).start()
        return lambda: pltpu.make_async_copy(into, into, sem).wait()
    chip, core = place[0], place[1]
    step = into.shape[0] // 16
    for side in range(2):
        half = core if side == 0 else 1 - core
        column = pl.ds(pl.multiple_of(half * width, 128), width)
        for group in range(4):
            for spot, relative in enumerate(GROUPS[group]):
                owner = lax.bitwise_xor(chip, relative)
                pltpu.make_async_copy(
                    pieces[4 * side + group].at[spot, :, pl.ds(lane, width)],
                    into.at[pl.ds(pl.multiple_of(owner * step, step), step), column],
                    sem,
                ).start()
    return lambda: pltpu.make_async_copy(into, into, sem).wait()


def normal(v):
    center = v - jnp.mean(v, -1, keepdims=True)
    spread = jnp.mean(center * center, -1, keepdims=True)
    factor = lax.rsqrt(spread + EPS)
    return center * factor, factor


def allowed(q_doc, k_doc, first, shape, q_dim):
    q_pos = lax.broadcasted_iota(jnp.int32, shape, q_dim) + first
    k_pos = lax.broadcasted_iota(jnp.int32, shape, 1 - q_dim)
    allow = ((k_pos <= q_pos) & (q_doc == k_doc) & (k_doc > 0)) | (k_pos == q_pos)
    return jnp.where(allow, 0.0, NEG)


def project_attend_kernel(steps, block, place, x, gain, shift, q_bias, v_bias, q_docs, k_docs, *rest):
    pieces, rest = rest[:-8], rest[-8:]
    mixed, hidden, out, lse, kept, bias, weight, sem = rest
    width = x.shape[1]
    size = x.shape[0]
    step = pl.program_id(0)

    @pl.when(step == 0)
    def _():
        wait = fetch(place, pieces, 0, 0, 3 * width // 2, weight, sem)
        for i in range(LEN // block):
            sl, reach = slice(i * block, (i + 1) * block), (i + 1) * block
            bias[sl, :reach] = allowed(q_docs[sl, :], k_docs[:, :reach], i * block, (block, reach), 0)
        wait()

    @pl.when(step < steps)
    def _():
        unit, _ = normal(x[...].astype(F32))
        h = (unit * gain[...] + shift[...]).astype(BF16)
        hidden[...] = h
        scale = 1.0 / math.sqrt(HD)
        here = pl.ds(pl.multiple_of(step * size, size), size)
        for part in range(3):
            sl = slice(part * width, (part + 1) * width)
            value = dot(h, weight[:, sl], NN)
            if part == 0:
                value = (value + q_bias[...]).astype(BF16).astype(F32) * scale
            if part == 2:
                value = value + v_bias[...]
            value = value.astype(BF16)
            mixed[:, sl] = value
            kept[here, sl] = value

    @pl.when(step >= steps)
    def _():
        lane = (step - steps) * PAIR
        q_at, k_at, v_at = (pl.ds(pl.multiple_of(lane + part * width, PAIR), PAIR) for part in range(3))
        low = lax.broadcasted_iota(jnp.int32, (block, PAIR), 1) < HD
        for i in range(LEN // block):
            sl, reach = slice(i * block, (i + 1) * block), (i + 1) * block
            q = kept[sl, q_at]
            outs, logs = [], []
            for head in range(2):
                q_one = jnp.where(low if head == 0 else ~low, q, jnp.zeros_like(q))
                score = dot(q_one, kept[:reach, k_at], NT) + bias[sl, :reach]
                top = jnp.max(score, -1, keepdims=True)
                expo = jnp.exp(score - top)
                total = jnp.sum(expo, -1, keepdims=True)
                outs.append(dot(expo.astype(BF16), kept[:reach, v_at], NN) / total)
                logs.append(top + jnp.log(total))
            out[sl, :] = jnp.where(low, outs[0], outs[1]).astype(BF16)
            turned = jnp.where(low, logs[0], logs[1]).T
            lse[0, 0:1, sl] = turned[0:1, :]
            lse[0, 1:2, sl] = turned[HD : HD + 1, :]


def project_attend(place, x, gain, shift, q_bias, v_bias, docs, pieces, after=()):
    count, width = x.shape
    size, block = 256, 512
    steps = count // size
    pairs = width // PAIR
    early = lambda i: (jnp.minimum(i, steps - 1), 0)
    late = lambda i: jnp.maximum(i - steps, 0)
    return kernel_call(
        functools.partial(project_attend_kernel, steps, block),
        [place, x, gain, shift, q_bias, v_bias, docs.reshape(LEN, 1), docs.reshape(1, LEN), *pieces],
        after,
        grid=(steps + pairs,),
        in_specs=[SMEM, pl.BlockSpec((size, width), early)]
        + [whole((1, width))] * 4
        + [whole((LEN, 1)), whole((1, LEN))]
        + [ANY] * len(pieces),
        out_specs=[
            pl.BlockSpec((size, 3 * width), early),
            pl.BlockSpec((size, width), early),
            pl.BlockSpec((LEN, PAIR), lambda i: (0, late(i))),
            pl.BlockSpec((1, 2, LEN), lambda i: (late(i), 0, 0)),
        ],
        out_shape=[
            jax.ShapeDtypeStruct((count, 3 * width), BF16),
            jax.ShapeDtypeStruct((count, width), BF16),
            jax.ShapeDtypeStruct((count, width), BF16),
            jax.ShapeDtypeStruct((pairs, 2, LEN), F32),
        ],
        scratch_shapes=[
            pltpu.VMEM((count, 3 * width), BF16),
            pltpu.VMEM((LEN, LEN), F32),
            pltpu.VMEM((width, 3 * width), BF16),
            pltpu.SemaphoreType.DMA,
        ],
        compiler_params=params(),
        cost_estimate=cost(28e9, 20e6),
        name="project_attend",
    )


def norm_back(v, gain, grad):
    unit, factor = normal(v)
    g = grad * gain
    pulled = factor * (g - jnp.mean(g, -1, keepdims=True) - unit * jnp.mean(g * unit, -1, keepdims=True))
    return pulled, jnp.sum(grad * unit, 0, keepdims=True), jnp.sum(grad, 0, keepdims=True)


def send(place, tile, column, width, outs, lane, half, first, sem):
    here = pl.ds(column, width)
    if len(outs) == 1:
        per_half = outs[0].shape[1] // 2
        at = pl.ds(pl.multiple_of(half * per_half + lane, 128), width)
        top = pl.ds(pl.multiple_of(first * (outs[0].shape[0] // 16), 16), tile.shape[0])
        pltpu.make_async_copy(tile.at[:, here], outs[0].at[top, at], sem).start()
        return
    chip, core = place[0], place[1]
    step = outs[0].shape[2]
    at = pl.ds(pl.multiple_of(lane, 128), width)
    for index in range(tile.shape[0] // step):
        relative = lax.bitwise_xor(chip, first + index)
        group, spot = lax.bitwise_and(relative, 3), lax.shift_right_logical(relative, 2)
        source = tile.at[pl.ds(index * step, step), here]
        for own, target in ((True, outs[0]), (False, outs[1])):
            copy = pltpu.make_async_copy(source, target.at[group, spot, :, at], sem)
            pl.when((half == core) == own)(copy.start)


def finish(ref, sem):
    pltpu.make_async_copy(ref, ref, sem).wait()


def term_shapes(tall, wide, by_stage):
    if by_stage:
        return [jax.ShapeDtypeStruct((4, 4, tall // 16, wide // 2), BF16)] * 2
    return [jax.ShapeDtypeStruct((tall, wide), BF16)]


def widen_kernel(steps, terms, place, x, attended, out_bias, gain, shift, fc_bias, cot, *rest):
    count = terms + 13
    pieces, rest = rest[:-count], rest[-count:]
    resid, hidden, slope, active = rest[:4]
    outs, rest = rest[4 : 4 + terms], rest[4 + terms :]
    w_out, w_fc, kept, grad, stage, weight_sems, kept_sem, grad_sem, sems = rest
    size, width = x.shape
    depth = w_fc.shape[1]
    step = pl.program_id(0)
    here = pl.ds(pl.multiple_of(lax.rem(step, steps) * size, size), size)

    @pl.when(step == 0)
    def _():
        wait_out = fetch(place, pieces, 0, 0, width // 2, w_out, weight_sems.at[0])
        wait_fc = fetch(place, pieces, 1, width // 2, depth // 2, w_fc, weight_sems.at[1])
        pltpu.make_async_copy(cot, grad, grad_sem).start()
        wait_out()
        wait_fc()

    @pl.when(step < steps)
    def _():
        r = x[...].astype(F32) + dot(attended[...], w_out[...], NN) + out_bias[...]
        resid[...] = r
        unit, _ = normal(r)
        h = (unit * gain[...] + shift[...]).astype(BF16)
        hidden[...] = h
        c = math.sqrt(2.0 / math.pi)
        for first in range(0, depth, width):
            sl = slice(first, first + width)
            u = dot(h, w_fc[:, sl], NN) + fc_bias[:, sl]
            square = u * u
            t = jnp.tanh(u * (c + (c * 0.044715) * square))
            half = 0.5 * (1.0 + t)
            kept[here, sl] = (u * half).astype(BF16)
            slope[:, sl] = (half + 0.5 * u * (1.0 - t * t) * (c + (3 * c * 0.044715) * square)).astype(BF16)
        pltpu.make_async_copy(kept.at[here, :], active.at[here, :], kept_sem).start()

    @pl.when(step >= steps)
    def _():
        tile = step - steps
        slot = lax.rem(tile, 2)

        @pl.when(tile == 0)
        def _():
            finish(grad, grad_sem)

        @pl.when(tile >= 2)
        def _():
            finish(stage.at[slot], sems.at[slot])

        tall = stage.shape[1]
        part = kept[:, pl.ds(pl.multiple_of(tile * tall, tall), tall)]
        stage[slot] = dot(part, grad[...], TN).astype(BF16)
        chips = tall * 16 // depth
        for half in range(2):
            send(place, stage.at[slot], half * (width // 2), width // 2, outs, 0, half, tile * chips, sems.at[slot])

        @pl.when(tile == depth // tall - 1)
        def _():
            finish(stage.at[slot], sems.at[slot])
            finish(stage.at[1 - slot], sems.at[1 - slot])
            finish(kept, kept_sem)


def widen(place, x, attended, out_bias, gain, shift, fc_bias, cot, pieces, after=()):
    count, width = x.shape
    depth = fc_bias.shape[1]
    size, tall = 256, width
    steps = count // size
    early = lambda i: (jnp.minimum(i, steps - 1), 0)
    block = lambda wide: pl.BlockSpec((size, wide), early)
    terms = term_shapes(depth, width, len(pieces) == 8)
    return kernel_call(
        functools.partial(widen_kernel, steps, len(terms)),
        [place, x, attended, out_bias, gain, shift, fc_bias, cot, *pieces],
        after,
        grid=(steps + depth // tall,),
        in_specs=[SMEM, block(width), block(width)]
        + [whole((1, width))] * 3
        + [whole((1, depth)), ANY]
        + [ANY] * len(pieces),
        out_specs=[block(width), block(width), block(depth), ANY] + [ANY] * len(terms),
        out_shape=[
            jax.ShapeDtypeStruct((count, width), F32),
            jax.ShapeDtypeStruct((count, width), BF16),
            jax.ShapeDtypeStruct((count, depth), BF16),
            jax.ShapeDtypeStruct((count, depth), BF16),
        ]
        + terms,
        scratch_shapes=[
            pltpu.VMEM((width, width), BF16),
            pltpu.VMEM((width, depth), BF16),
            pltpu.VMEM((count, depth), BF16),
            pltpu.VMEM((count, width), BF16),
            pltpu.VMEM((2, tall, width), BF16),
            pltpu.SemaphoreType.DMA((2,)),
            pltpu.SemaphoreType.DMA,
            pltpu.SemaphoreType.DMA,
            pltpu.SemaphoreType.DMA((2,)),
        ],
        compiler_params=params(),
        cost_estimate=cost(2 * count * width * (width + 2 * depth), 30e6),
        name="widen",
    )


def narrow_kernel(steps, terms, sides, place, resid, active, slope, cot, proj_bias, gain, hidden, attended, *rest):
    count = terms + 19
    pieces, rest = rest[:-count], rest[-count:]
    wide_pieces, proj_pieces = pieces[:sides], pieces[sides:]
    result, grad_r, grad_o, fc_sum, proj_sum, gain_sum, shift_sum, bias_sum = rest[:8]
    outs, rest = rest[8 : 8 + terms], rest[8 + terms :]
    w_proj, w_fc, w_out, du, dt, h_kept, o_kept, stage, weight_sems, kept_sems, sems = rest
    size, width = resid.shape
    depth = active.shape[1]
    step = pl.program_id(0)
    here = pl.ds(pl.multiple_of(lax.rem(step, steps) * size, size), size)

    @pl.when(step == 0)
    def _():
        wait_proj = fetch(place, proj_pieces, 0, 0, width // 2, w_proj, weight_sems.at[0])
        wait_fc = fetch(place, wide_pieces, 1, width // 2, depth // 2, w_fc, weight_sems.at[1])
        wait_out = fetch(place, wide_pieces, 0, 0, width // 2, w_out, weight_sems.at[2])
        pltpu.make_async_copy(hidden, h_kept, kept_sems.at[0]).start()
        pltpu.make_async_copy(attended, o_kept, kept_sems.at[1]).start()
        for total in (fc_sum, proj_sum, gain_sum, shift_sum, bias_sum):
            total[...] = jnp.zeros_like(total)
        wait_proj()
        wait_fc()
        wait_out()

    @pl.when(step < steps)
    def _():
        g = cot[...]
        for first in range(0, depth, width):
            sl = slice(first, first + width)
            part = (dot(g, w_proj[sl, :], NT) * slope[:, sl].astype(F32)).astype(BF16)
            du[here, sl] = part
            fc_sum[:, sl] += jnp.sum(part.astype(F32), 0, keepdims=True)
        r = resid[...]
        result[...] = (r + dot(active[...], w_proj[...], NN) + proj_bias[...]).astype(BF16)
        wide = g.astype(F32)
        proj_sum[...] += jnp.sum(wide, 0, keepdims=True)
        grad_h = dot(du[here, :], w_fc[...], NT)
        pulled, gains, shifts = norm_back(r, gain[...], grad_h)
        total = wide + pulled
        grad_r[...] = total
        low = total.astype(BF16)
        dt[here, :] = low
        gain_sum[...] += gains
        shift_sum[...] += shifts
        bias_sum[...] += jnp.sum(low.astype(F32), 0, keepdims=True)
        grad_o[...] = dot(low, w_out[...], NT).astype(BF16)

    tiles = depth // width

    @pl.when(step >= steps)
    def _():
        tile = step - steps
        slot = lax.rem(tile, 2)

        @pl.when(tile == 0)
        def _():
            finish(h_kept, kept_sems.at[0])
            finish(o_kept, kept_sems.at[1])

        @pl.when(tile >= 2)
        def _():
            finish(stage.at[slot], sems.at[slot])

        @pl.when(tile < tiles)
        def _():
            part = du[:, pl.ds(pl.multiple_of(lax.rem(tile, tiles) * width, width), width)]
            stage[slot] = dot(h_kept[...], part, TN).astype(BF16)
            lane = lax.rem(tile, tiles // 2) * width
            send(place, stage.at[slot], 0, width, outs, lane, tile // (tiles // 2), 0, sems.at[slot])

        @pl.when(tile == tiles)
        def _():
            stage[slot] = dot(o_kept[...], dt[...], TN).astype(BF16)
            for half in range(2):
                send(place, stage.at[slot], half * (width // 2), width // 2, outs, depth // 2, half, 0, sems.at[slot])
            finish(stage.at[slot], sems.at[slot])
            finish(stage.at[1 - slot], sems.at[1 - slot])


def narrow(place, resid, active, slope, cot, proj_bias, gain, hidden, attended, wide_pieces, proj_pieces, after=()):
    count, width = resid.shape
    depth = active.shape[1]
    size = 256
    steps = count // size
    early = lambda i: (jnp.minimum(i, steps - 1), 0)
    block = lambda wide: pl.BlockSpec((size, wide), early)
    pieces = [*wide_pieces, *proj_pieces]
    terms = term_shapes(width, width + depth, len(proj_pieces) == 8)
    return kernel_call(
        functools.partial(narrow_kernel, steps, len(terms), len(wide_pieces)),
        [place, resid, active, slope, cot, proj_bias, gain, hidden, attended, *pieces],
        after,
        grid=(steps + depth // width + 1,),
        in_specs=[SMEM, block(width), block(depth), block(depth), block(width)]
        + [whole((1, width))] * 2
        + [ANY] * (2 + len(pieces)),
        out_specs=[block(width)] * 3
        + [whole((1, depth))]
        + [whole((1, width))] * 4
        + [ANY] * len(terms),
        out_shape=[
            jax.ShapeDtypeStruct((count, width), BF16),
            jax.ShapeDtypeStruct((count, width), F32),
            jax.ShapeDtypeStruct((count, width), BF16),
            jax.ShapeDtypeStruct((1, depth), F32),
        ]
        + [jax.ShapeDtypeStruct((1, width), F32)] * 4
        + terms,
        scratch_shapes=[
            pltpu.VMEM((depth, width), BF16),
            pltpu.VMEM((width, depth), BF16),
            pltpu.VMEM((width, width), BF16),
            pltpu.VMEM((count, depth), BF16),
            pltpu.VMEM((count, width), BF16),
            pltpu.VMEM((count, width), BF16),
            pltpu.VMEM((count, width), BF16),
            pltpu.VMEM((2, width, width), BF16),
            pltpu.SemaphoreType.DMA((3,)),
            pltpu.SemaphoreType.DMA((2,)),
            pltpu.SemaphoreType.DMA((2,)),
        ],
        compiler_params=params(),
        cost_estimate=cost(2 * count * width * (2 * width + 4 * depth), 40e6),
        name="narrow",
    )


def attend_back_kernel(block, number, terms, place, q_docs, k_docs, q_all, k_all, v_all, o_all, g_all, lse, hidden, *rest):
    dq, dk, dv = rest[:3]
    outs, rest = rest[3 : 3 + terms], rest[3 + terms :]
    bias, k_sum, v_sum, kept, h_kept, stage, sem, sems = rest
    count = LEN // block
    step = pl.program_id(0)

    @pl.when(step == 0)
    def _():
        pltpu.make_async_copy(hidden, h_kept, sem).start()
        for i in range(count):
            sl, reach = slice(i * block, (i + 1) * block), (i + 1) * block
            bias[:reach, sl] = allowed(q_docs[:, sl], k_docs[:reach, :], i * block, (reach, block), 1)

    @pl.when(step < number)
    def _():
        low = lax.broadcasted_iota(jnp.int32, (block, PAIR), 1) < HD
        low_all = lax.broadcasted_iota(jnp.int32, (LEN, PAIR), 1) < HD
        keys = k_all[...]
        key_one = [jnp.where(low_all, keys, jnp.zeros_like(keys)), jnp.where(low_all, jnp.zeros_like(keys), keys)]
        at = pl.ds(pl.multiple_of(lax.rem(step, number) * PAIR, PAIR), PAIR)
        for i in reversed(range(count)):
            sl, reach = slice(i * block, (i + 1) * block), (i + 1) * block
            q, grad = q_all[sl, :], g_all[sl, :]
            turned = (grad.astype(F32) * o_all[sl, :].astype(F32)).T
            parts = []
            for head in range(2):
                lane = low if head == 0 else ~low
                q_one = jnp.where(lane, q, jnp.zeros_like(q))
                g_one = jnp.where(lane, grad, jnp.zeros_like(grad))
                inner = jnp.sum(turned[head * HD : (head + 1) * HD, :], 0, keepdims=True)
                score = dot(k_all[:reach, :], q_one, NT) + bias[:reach, sl]
                prob = jnp.exp(score - lse[0, head : head + 1, sl])
                v_part = dot(prob.astype(BF16), g_one, NN)
                slope = dot(v_all[:reach, :], g_one, NT)
                dscore = (prob * (slope - inner)).astype(BF16)
                k_part = dot(dscore, q_one, NN)
                if i == count - 1 and head == 0:
                    k_sum[...] = k_part
                    v_sum[...] = v_part
                else:
                    k_sum[:reach, :] += k_part
                    v_sum[:reach, :] += v_part
                parts.append(dot(dscore, key_one[head][:reach], TN))
            part = ((parts[0] + parts[1]) * (1.0 / math.sqrt(HD))).astype(BF16)
            dq[sl, :] = part
            kept[0, sl, at] = part
        for index, (ref, total) in enumerate(((dk, k_sum), (dv, v_sum))):
            part = total[...].astype(BF16)
            ref[...] = part
            kept[1 + index, :, at] = part

    wide = stage.shape[3]

    @pl.when(step >= number)
    def _():
        tile = step - number
        slot = lax.rem(tile, 2)

        @pl.when(tile == 0)
        def _():
            finish(h_kept, sem)

        for index in range(3):
            part = kept[index, :, pl.ds(pl.multiple_of(tile * wide, wide), wide)]
            stage[slot, index] = dot(h_kept[...], part, TN).astype(BF16)
        for index in range(3):
            for half in range(2):
                send(
                    place,
                    stage.at[slot, index],
                    half * (wide // 2),
                    wide // 2,
                    outs,
                    index * (number * PAIR // 2) + tile * (wide // 2),
                    half,
                    0,
                    sems.at[slot],
                )

        @pl.when(tile == number * PAIR // wide - 1)
        def _():
            finish(stage.at[slot], sems.at[slot])
            if number * PAIR // wide > 1:
                finish(stage.at[1 - slot], sems.at[1 - slot])


def attend_back(place, mixed, attended, grad_o, lse, docs, hidden, first, number, by_stage, after=()):
    width = attended.shape[1]
    pairs = width // PAIR
    block = 256
    wide = 2 * PAIR
    steps = number * PAIR // wide
    pair = lambda i: jnp.minimum(i, number - 1)
    column = lambda base: pl.BlockSpec((LEN, PAIR), lambda i: (0, base + pair(i)))
    terms = term_shapes(width, 3 * number * PAIR, by_stage)
    return kernel_call(
        functools.partial(attend_back_kernel, block, number, len(terms)),
        [place, docs.reshape(1, LEN), docs.reshape(LEN, 1), mixed, mixed, mixed, attended, grad_o, lse, hidden],
        after,
        grid=(number + steps,),
        in_specs=[
            SMEM,
            whole((1, LEN)),
            whole((LEN, 1)),
            column(first),
            column(pairs + first),
            column(2 * pairs + first),
            column(first),
            column(first),
            pl.BlockSpec((1, 2, LEN), lambda i: (first + pair(i), 0, 0)),
            ANY,
        ],
        out_specs=[column(0)] * 3 + [ANY] * len(terms),
        out_shape=[jax.ShapeDtypeStruct((LEN, PAIR * number), BF16)] * 3 + terms,
        scratch_shapes=[
            pltpu.VMEM((LEN, LEN), F32),
            pltpu.VMEM((LEN, PAIR), F32),
            pltpu.VMEM((LEN, PAIR), F32),
            pltpu.VMEM((3, LEN, PAIR * number), BF16),
            pltpu.VMEM((LEN, width), BF16),
            pltpu.VMEM((2, 3, width, wide), BF16),
            pltpu.SemaphoreType.DMA,
            pltpu.SemaphoreType.DMA((2,)),
        ],
        compiler_params=params(),
        cost_estimate=cost(42e9 * number / pairs, 10e6),
        name="attend_back",
    )


def first_back_kernel(place, x, grad_r, gain, *rest):
    parts, pieces, rest = rest[:6], rest[6:-7], rest[-7:]
    grad_x, gain_sum, shift_sum, q_sum, v_sum, weight, sem = rest
    width = x.shape[1]

    @pl.when(pl.program_id(0) == 0)
    def _():
        fetch(place, pieces, 0, 0, 3 * width // 2, weight, sem)()
        for total in (gain_sum, shift_sum, q_sum, v_sum):
            total[...] = jnp.zeros_like(total)

    grad_h = None
    at = 0
    for index, part in enumerate(parts):
        wide = part.shape[1]
        term = dot(part[...], weight[:, at : at + wide], NT)
        grad_h = term if grad_h is None else grad_h + term
        if index // 2 != 1:
            into = q_sum if index // 2 == 0 else v_sum
            lane = at % width
            into[:, lane : lane + wide] += jnp.sum(part[...].astype(F32), 0, keepdims=True)
        at += wide
    pulled, gains, shifts = norm_back(x[...].astype(F32), gain[...], grad_h)
    grad_x[...] = grad_r[...] + pulled
    gain_sum[...] += gains
    shift_sum[...] += shifts


def first_back(place, x, grad_r, gain, parts, pieces, after=()):
    count, width = x.shape
    block = 256
    return kernel_call(
        first_back_kernel,
        [place, x, grad_r, gain, *parts, *pieces],
        after,
        grid=(count // block,),
        in_specs=[SMEM, rows(block, width), rows(block, width), whole((1, width))]
        + [rows(block, part.shape[1]) for part in parts]
        + [ANY] * len(pieces),
        out_specs=[rows(block, width)] + [whole((1, width))] * 4,
        out_shape=[jax.ShapeDtypeStruct((count, width), F32)] + [jax.ShapeDtypeStruct((1, width), F32)] * 4,
        scratch_shapes=[pltpu.VMEM((width, 3 * width), BF16), pltpu.SemaphoreType.DMA],
        compiler_params=params(),
        cost_estimate=cost(6 * count * width * width, 16e6),
        name="first_back",
    )


def one_hot(shape, base, span, first):
    lane = lax.broadcasted_iota(jnp.int32, shape, 0)
    element = lax.broadcasted_iota(jnp.int32, shape, 1) + first
    return lane == base + lax.rem(element, span)


def owner(shape, span, first):
    element = lax.broadcasted_iota(jnp.int32, shape, 1) + first
    return lax.broadcasted_iota(jnp.int32, shape, 0) == element // span


def slots(unit, width):
    found, base = [], 0
    for span in (1, 1, 2, 1, 1, 1, 4, 1):
        found += [(base * unit, span * unit, index * width) for index in range(span)]
        base += span
    return found


def unpack_kernel(table, out):
    devices, lanes = table.shape
    width = out.shape[1]
    for index, (base, span, first) in enumerate(slots(lanes // 12, width)):
        pick = one_hot((lanes, width), base, span, first).astype(BF16)
        value = dot(table[...], pick, NN)
        out[index : index + 1, :] = jnp.sum(jnp.where(owner((devices, width), span, first), value, 0.0), 0, keepdims=True)


def unpack(table):
    devices, lanes = table.shape
    width = devices * lanes // 12
    return pl.pallas_call(
        unpack_kernel,
        out_shape=jax.ShapeDtypeStruct((12, width), F32),
        compiler_params=params(),
        name="unpack",
    )(table)


def pack_kernel(*refs):
    vectors, out = refs[:-1], refs[-1]
    devices, lanes = out.shape
    width = vectors[0].shape[1]
    rows_of = [vector[:, first : first + width] for vector in vectors for first in range(0, vector.shape[1], width)]
    total = jnp.zeros(out.shape, F32)
    for row, (base, span, first) in zip(rows_of, slots(lanes // 12, width)):
        pick = one_hot((lanes, width), base, span, first).astype(BF16)
        spread = jnp.where(owner((devices, width), span, first), row, 0.0)
        for _ in range(3):
            part = spread.astype(BF16)
            total = total + dot(part, pick, NT)
            spread = spread - part.astype(F32)
    out[...] = total


def pack(vectors, devices):
    lanes = sum(v.shape[1] for v in vectors) // devices
    return pl.pallas_call(
        pack_kernel,
        out_shape=jax.ShapeDtypeStruct((devices, lanes), F32),
        compiler_params=params(),
        name="pack",
    )(*vectors)


def staged(
    tokens,
    doc_ids,
    d_out,
    ln1_gain,
    ln1_shift,
    qkv_weight,
    qv_bias,
    out_weight,
    out_bias,
    ln2_gain,
    ln2_shift,
    fc_weight,
    fc_bias,
    proj_weight,
    proj_bias,
):
    width = tokens.shape[1]
    depth = fc_weight.shape[1]
    devices = lax.axis_size("dp") * lax.axis_size("fsdp")
    index = lax.axis_index("dp") * lax.axis_size("fsdp") + lax.axis_index("fsdp")
    core = index & 1
    place = jnp.stack([index >> 1, core]).astype(jnp.int32)
    pairs = width // PAIR
    cut = 4
    by_stage = (lax.axis_size("dp"), lax.axis_size("fsdp")) == (8, 4)

    smalls = [ln1_gain, ln1_shift, qv_bias, out_bias, ln2_gain, ln2_shift, fc_bias, proj_bias]
    smalls = jnp.concatenate([v.astype(F32) for v in smalls]).reshape(1, -1).astype(BF16)
    if by_stage:
        first_column = gather_z(pair_block(qkv_weight, core))
        wide_block = jnp.concatenate([pair_block(out_weight, core), pair_block(fc_weight, core)], 1)
        proj_block = pair_block(proj_weight, core)
        first_own = gather_xy(first_column)
        smalls, wide_block = tie([smalls, wide_block], first_column)
        table = gather_small(smalls, index)
        wide_column = gather_z(wide_block)
        wide_column, *first_own = tie([wide_column], *first_own) + first_own
        wide_own = gather_xy(wide_column)
        first_pieces = gather_core(first_own)
        (proj_block,) = tie([proj_block], wide_column)
    else:
        first_pieces, proj_pieces = [gather_all(qkv_weight)], [gather_all(proj_weight)]
        wide_pieces = [gather_all(w) for w in (out_weight, fc_weight)]
        wide_column = None
        table = gather_all(smalls)
    hold = lambda *some: list(some) if by_stage else []
    cores = scatter_core if by_stage else lambda terms: terms[0]
    planes = scatter_xy if by_stage else lambda terms, *after: terms
    columns = scatter_z if by_stage else lambda terms, *after: scatter_all(terms.astype(F32))
    vectors = unpack(table)
    row = lambda at, count=1: vectors[at : at + count].reshape(1, -1)

    mixed, h_one, attended, lse = project_attend(
        place, tokens, row(0), row(1), row(2), row(3), doc_ids, first_pieces, after=hold(wide_column)
    )
    if by_stage:
        proj_column = gather_z(proj_block, lse)
        wide_own = tie(wide_own, lse)
        proj_column, *wide_own = tie([proj_column, *wide_own], proj_column)
        proj_own = gather_xy(proj_column)
        wide_pieces = gather_core(wide_own)
    resid, h_two, slope, active, *proj_terms = widen(
        place, tokens, attended, row(4), row(5), row(6), row(7, 4), d_out, wide_pieces
    )
    if by_stage:
        proj_own = tie(proj_own, resid)
        proj_pieces = gather_core(proj_own)
        proj_terms = tie(proj_terms, *proj_own)
    proj_sums = cores(proj_terms)
    result, grad_r, grad_o, fc_sum, proj_sum, gain_two, shift_two, out_sum, *wide_terms = narrow(
        place,
        resid,
        active,
        slope,
        d_out,
        row(11),
        row(5),
        h_two,
        attended,
        wide_pieces,
        proj_pieces,
        after=hold(*proj_sums),
    )
    if by_stage:
        proj_sums = planes(proj_sums, grad_o)
        wide_terms = tie(wide_terms, *proj_sums)
    wide_sums = cores(wide_terms)
    *head, head_one, head_two = (lambda found: found if by_stage else [*found, None])(
        attend_back(
            place,
            mixed,
            attended,
            grad_o,
            lse,
            doc_ids,
            h_one,
            0,
            cut,
            by_stage,
            after=hold(*proj_sums, *wide_sums),
        )
    )
    proj_grad = columns(proj_sums, head_one)
    wide_sums = planes(wide_sums, head_one)
    if by_stage:
        head_one, head_two = tie([head_one, head_two], proj_grad, *wide_sums)
    head_sums = cores([head_one, head_two])
    *tail, tail_one, tail_two = (lambda found: found if by_stage else [*found, None])(
        attend_back(
            place,
            mixed,
            attended,
            grad_o,
            lse,
            doc_ids,
            h_one,
            cut,
            pairs - cut,
            by_stage,
            after=hold(*head_sums, *wide_sums),
        )
    )
    parts = [part for both in zip(head, tail) for part in both]
    head_sums = planes(head_sums, tail_one)
    wide_grad = columns(wide_sums, tail_one)
    if by_stage:
        tail_one, tail_two = tie([tail_one, tail_two], wide_grad, *head_sums)
    tail_sums = cores([tail_one, tail_two])
    grad_x, gain_one, shift_one, q_sum, v_sum = first_back(
        place, tokens, grad_r, row(0), parts, first_pieces, after=hold(*head_sums, *tail_sums)
    )
    sums = [gain_one, shift_one, q_sum, v_sum, out_sum, gain_two, shift_two, fc_sum, proj_sum]
    sums = pack(sums, devices)
    head_grad = columns(head_sums, grad_x)
    tail_grad = columns(planes(tail_sums, grad_x))

    def sides(grad):
        if by_stage:
            return own_rows(grad, core)
        return jnp.split(grad, 2, 1)

    proj_grad = jnp.concatenate(sides(proj_grad), 1)
    both = sides(wide_grad)
    half = depth // 2
    fc_grad = jnp.concatenate([side[:, :half] for side in both], 1)
    out_grad = jnp.concatenate([side[:, half:] for side in both], 1)
    parts = []
    heads, tails = sides(head_grad), sides(tail_grad)
    for section in range(3):
        for both, number in ((heads, cut), (tails, pairs - cut)):
            start = section * number * PAIR // 2
            for pair in range(0, number, 2):
                lane = start + pair * PAIR // 2
                parts += [side[:, lane : lane + PAIR] for side in both]
    qkv_grad = jnp.concatenate(parts, 1)
    own = scatter_small(sums, index) if by_stage else scatter_all(sums).reshape(-1)
    n = width // devices
    spots = (0, n, 2 * n, 4 * n, 5 * n, 6 * n, 7 * n, 11 * n, 12 * n)
    s = [own[a:b] for a, b in zip(spots[:-1], spots[1:])]
    return (
        result,
        grad_x,
        s[0],
        s[1],
        qkv_grad,
        s[2],
        out_grad,
        s[3],
        s[4],
        s[5],
        fc_grad,
        s[6],
        proj_grad,
        s[7],
    )


def solution(mesh):
    every, block = P(AXES), P(AXES, None)
    ins = (block, every, block, every, every, block, every, block, every, every, every, block, every, block, every)
    outs = (block, block, every, every, block, every, block, every, every, every, block, every, block, every)
    return jax.shard_map(staged, mesh=mesh, in_specs=ins, out_specs=outs, check_vma=False)
```

time: 457 us -> 319 us (0.70)
  waiting for transfers between devices: 190 us -> 59.9 us
  local copies, waits for them, and re-layouts: 25.1 us -> 8.07 us
  starting transfers between devices: 56.6 us -> 72.3 us
  Pallas kernels: 164 us -> 152 us
  other arithmetic: 14.8 us -> 19.8 us
    ppermute x66 -> x76, waiting for transfers between devices: 190 us -> 59.9 us  [swap(): return lax.ppermute(array, AXES, [(i, i ^ bit) for i in range(count)])]
    ppermute x66 -> x76, starting transfers between devices: 56.6 us -> 72.3 us  [swap(): return lax.ppermute(array, AXES, [(i, i ^ bit) for i in range(count)])]
    pallas_call x12 -> x8, Pallas kernels: 164 us -> 152 us  [the longest x6 143 us: kernel_call(): return pl.pallas_call(body, **how)(*inputs, *after)]
    concatenate x11 -> x2, local copies, waits for them, and re-layouts: 7.84 us -> 0.86 us  [the longest x1 0.86 us: staged(): jnp.concatenate([v.astype(F32) for v in smalls]).reshape(1, -1).astype(BF16)]
    convert_element_type x12 -> x0, local copies, waits for them, and re-layouts: 4.86 us -> none  [the longest x8 4.8 us: unpack(): found.append(table[:, at:at + span * count].reshape(1, -1).astype(F32))]
  transfers between devices with their start and end apart: 66 -> 76, of which waited for: 28 -> 25; matrix products, arithmetic and copies ran while one was open for 5% -> 7% of each run, Pallas kernels for 15% -> 48%
where the time goes in v2:
time: 319 us; the launch traced here: 314 us
  Pallas kernels  152 us (48%)
  starting transfers between devices  72.3 us (23%)
  waiting for transfers between devices  59.9 us (19%)
  other arithmetic  19.8 us (6%)
  local copies, waits for them, and re-layouts  8.07 us (3%)
    pallas_call x6, Pallas kernels, kernel_call(): return pl.pallas_call(body, **how)(*inputs, *after)  143 us
    ppermute x76, starting transfers between devices, swap(): return lax.ppermute(array, AXES, [(i, i ^ bit) for i in range(count)])  72.3 us
    ppermute x76, waiting for transfers between devices, swap(): return lax.ppermute(array, AXES, [(i, i ^ bit) for i in range(count)])  59.9 us
    convert_element_type x4, other arithmetic, scatter_core(): return [add(mine[g], got[g]).astype(BF16) for g in range(4)]  6.73 us
  transfers between devices with their start and end apart: 76, of which 25 were waited for; matrix products, arithmetic and copies ran while one was open for 7% of the time, Pallas kernels for 48%

profile of v2, /device:TPU:0, one launch (start us, length us, event | category | flops | bytes accessed | tf_op | source)
XLA Modules:
  0.0 314.0 jit_solution(7014292371909254129)
XLA Ops:
  2.9 0.9 broadcast_select_fusion.10
  4.3 0.9 concatenate.77
  6.0 0.9 broadcast_select_fusion.13
  6.8 3.7 %collective-permute-start.4 = (bf16[48,1152]{1,0:T(8,128)(2,1)S(1)}, bf16[48,1152]{1,0:T(8,128)(2,1)S(1)}, u32[]{:S(2)}, u32[]{:S(2)}) collective-permute-start(bf16[48,1152]{1,0:T(8,128)(2,1)S(1)} %get-tuple-element.228), channel_id=1, source_target_pairs={{0,16},{1,17},{2,18},{3,19},{4,20},{5,21},{6,22},{7,23},{8,24},{9,... | collective-permute-start | bytes 331784 | tf_op jit(solution)/shard_map/ppermute | solution.py:55
  10.5 1.6 collective-permute-start.3
  12.1 0.9 broadcast_select_fusion.9
  13.1 3.7 %collective-permute-done.4 = bf16[48,1152]{1,0:T(8,128)(2,1)S(1)} collective-permute-done((bf16[48,1152]{1,0:T(8,128)(2,1)S(1)}, bf16[48,1152]{1,0:T(8,128)(2,1)S(1)}, u32[]{:S(2)}, u32[]{:S(2)}) %collective-permute-start.4) | collective-permute-done | bytes 110624 | tf_op jit(solution)/shard_map/ppermute | solution.py:55
  16.9 3.3 %collective-permute-done.5 = bf16[48,1152]{1,0:T(8,128)(2,1)S(1)} collective-permute-done((bf16[48,1152]{1,0:T(8,128)(2,1)S(1)}, bf16[48,1152]{1,0:T(8,128)(2,1)S(1)}, u32[]{:S(2)}, u32[]{:S(2)}) %collective-permute-start.5) | collective-permute-done | bytes 110624 | tf_op jit(solution)/shard_map/ppermute | solution.py:55
  20.3 1.1 collective-permute-done.6
  21.5 1.6 collective-permute-start.7
  23.2 2.0 collective-permute-done.7
  25.2 1.6 collective-permute-start.8
  27.4 1.0 copy.29.refs_6_.refs_2_
  28.9 2.0 collective-permute-start.9
  30.9 2.5 collective-permute-start.13
  34.4 3.4 %collective-permute-start.20 = (bf16[48,1920]{1,0:T(8,128)(2,1)S(1)}, bf16[48,1920]{1,0:T(8,128)(2,1)S(1)}, u32[]{:S(2)}, u32[]{:S(2)}) collective-permute-start(bf16[48,1920]{1,0:T(8,128)(2,1)S(1)} %maximum_maximum_fusion), channel_id=1, source_target_pairs={{0,24},{1,25},{2,26},{3,27},{4,28},{5,29},{6,30},{7,31},{8,16},{9,... | collective-permute-start | bytes 552968 | tf_op jit(solution)/shard_map/ppermute | solution.py:55
  37.9 8.2 %collective-permute-done.10 = bf16[16,288]{1,0:T(8,128)(2,1)S(1)} collective-permute-done((bf16[16,288]{1,0:T(8,128)(2,1)S(1)}, bf16[16,288]{1,0:T(8,128)(2,1)S(1)}, u32[]{:S(2)}, u32[]{:S(2)}) %collective-permute-start.10) | collective-permute-done | bytes 9248 | tf_op jit(solution)/shard_map/ppermute | solution.py:55
  46.1 2.7 collective-permute-start.18
  49.4 2.9 unpack.1
  52.3 1.5 collective-permute-done.19
  55.0 1.8 collective-permute-start.24
  57.5 6.2 %collective-permute-done.24 = bf16[192,384]{1,0:T(8,128)(2,1)S(1)} collective-permute-done((bf16[192,384]{1,0:T(8,128)(2,1)S(1)}, bf16[192,384]{1,0:T(8,128)(2,1)S(1)}, u32[]{:S(2)}, u32[]{:S(2)}) %collective-permute-start.24) | collective-permute-done | bytes 147488 | tf_op jit(solution)/shard_map/ppermute | solution.py:55
  63.7 3.1 collective-permute-start.27
  67.7 28.6 %project_attend.1 = (bf16[1024,2304]{1,0:T(8,128)(2,1)}, bf16[1024,768]{1,0:T(8,128)(2,1)}, bf16[1024,768]{1,0:T(8,128)(2,1)}, f32[6,2,1024]{2,1,0:T(2,128)}) custom-call(s32[2]{0:T(128)} %pad_add_fusion.refs_0_, bf16[1024,768]{1,0:T(8,128)(2,1)} %refs_1_.5, f32[1,768]{1,0:T(1,128)} %get-tuple-element.238.refs_2_.refs_3_, ...), custom_call_target="tpu_custom_call" | custom-call | flops 28000000000 | bytes 20000000 | tf_op jit(solution)/shard_map/project_attend/pallas_call | solution.py:118
  98.8 2.0 collective-permute-start.34
  103.6 27.9 %widen.1 = (f32[1024,768]{1,0:T(8,128)}, bf16[1024,768]{1,0:T(8,128)(2,1)}, bf16[1024,3072]{1,0:T(8,128)(2,1)}, bf16[1024,3072]{1,0:T(8,128)(2,1)}, bf16[4,4,192...) custom-call(s32[2]{0:T(128)} %pad_add_fusion.refs_0_, bf16[1024,768]{1,0:T(8,128)(2,1)} %refs_1_.5, ...), custom_call_target="tpu_custom_call" | custom-call | flops 10871635968 | bytes 30000000 | tf_op jit(solution)/shard_map/widen/pallas_call | solution.py:118
  132.7 4.5 %collective-permute-done.39 = bf16[4,4,192,384]{3,2,1,0:T(8,128)(2,1)S(1)} collective-permute-done((bf16[4,4,192,384]{3,2,1,0:T(8,128)(2,1)}, bf16[4,4,192,384]{3,2,1,0:T(8,128)(2,1)S(1)}, u32[]{:S(2)}, u32[]{:S(2)}) %collective-permute-start.39) | collective-permute-done | bytes 2359328 | tf_op jit(solution)/shard_map/ppermute | solution.py:55
  137.1 3.1 fusion.5
  140.3 1.9 collective-permute-start.42
  144.9 36.8 %narrow.1 = (bf16[1024,768]{1,0:T(8,128)(2,1)}, f32[1024,768]{1,0:T(8,128)}, bf16[1024,768]{1,0:T(8,128)(2,1)}, f32[1,3072]{1,0:T(1,128)}, f32[1,768]{1,0:T(1,12...) custom-call(s32[2]{0:T(128)} %pad_add_fusion.refs_0_, ...), custom_call_target="tpu_custom_call" | custom-call | flops 21743271936 | bytes 40000000 | tf_op jit(solution)/shard_map/narrow/pallas_call | solution.py:118
  181.7 1.0 fusion.43
  182.7 3.8 %collective-permute-start.46 = (bf16[192,384]{1,0:T(8,128)(2,1)S(1)}, bf16[192,384]{1,0:T(8,128)(2,1)S(1)}, u32[]{:S(2)}, u32[]{:S(2)}) collective-permute-start(bf16[192,384]{1,0:T(8,128)(2,1)S(1)} %get-tuple-element.198.refs_13_), channel_id=1, source_target_pairs={{0,24},{1,25},{2,26},{3,27},{4,28},{5,29},{6,30},{7,31},{8,16},{9,... | collective-permute-start | bytes 442376 | tf_op jit(solution)/shard_map/ppermute | solution.py:55
  187.1 1.1 collective-permute-done.43
  188.3 1.6 fusion.2
  189.9 1.9 collective-permute-start.49
  191.8 0.9 collective-permute-start.48
  193.5 24.5 %attend_back.2 = (bf16[1024,512]{1,0:T(8,128)(2,1)}, bf16[1024,512]{1,0:T(8,128)(2,1)}, bf16[1024,512]{1,0:T(8,128)(2,1)}, bf16[4,4,48,768]{3,2,1,0:T(8,128)(2,1)}, bf16[4,4,48,768]{3,2,1,0:T(8,128)(2,1)}) custom-call(s32[2]{0:T(128)} %pad_add_fusion.refs_0_, s32[1,1024]{1,0:T(1,128)} %bitcast.205, s32[1024,1]{1,0:T(8,128)} %copy.29.refs_6_.refs_2_, ...), custom_call_target="tpu_custom_call" | custom-call | flops 28000000000 | bytes 10000000 | tf_op jit(solution)/shard_map/attend_back/pallas_call | solution.py:118
  218.1 7.1 %collective-permute-done.48 = bf16[4,48,1920]{2,1,0:T(8,128)(2,1)S(1)} collective-permute-done((bf16[4,48,1920]{2,1,0:T(8,128)(2,1)S(1)}, bf16[4,48,1920]{2,1,0:T(8,128)(2,1)S(1)}, u32[]{:S(2)}, u32[]{:S(2)}) %collective-permute-start.48) | collective-permute-done | bytes 737312 | tf_op jit(solution)/shard_map/ppermute | solution.py:55
  225.2 1.0 fusion.36
  226.9 3.7 %collective-permute-start.56 = (bf16[48,1920]{1,0:T(8,128)(2,1)S(1)}, bf16[48,1920]{1,0:T(8,128)(2,1)S(1)}, u32[]{:S(2)}, u32[]{:S(2)}) collective-permute-start(bf16[48,1920]{1,0:T(8,128)(2,1)S(1)} %get-tuple-element.190.refs_17_), channel_id=1, source_target_pairs={{0,24},{1,25},{2,26},{3,27},{4,28},{5,29},{6,30},{7,31},{8,16},{9,... | collective-permute-start | bytes 552968 | tf_op jit(solution)/shard_map/ppermute | solution.py:55
  231.3 1.1 fusion.20
  232.4 1.8 collective-permute-start.53
  234.3 14.3 %attend_back.3 = (bf16[1024,256]{1,0:T(8,128)(2,1)}, bf16[1024,256]{1,0:T(8,128)(2,1)}, bf16[1024,256]{1,0:T(8,128)(2,1)}, bf16[4,4,48,384]{3,2,1,0:T(8,128)(2,1)}, bf16[4,4,48,384]{3,2,1,0:T(8,128)(2,1)}) custom-call(s32[2]{0:T(128)} %pad_add_fusion.refs_0_, s32[1,1024]{1,0:T(1,128)} %bitcast.206, s32[1024,1]{1,0:T(8,128)} %copy.29.refs_6_.refs_2_, ...), custom_call_target="tpu_custom_call" | custom-call | flops 14000000000 | bytes 10000000 | tf_op jit(solution)/shard_map/attend_back/pallas_call | solution.py:118
  248.6 1.0 collective-permute-start.52
  250.6 6.2 %collective-permute-done.52 = bf16[4,48,768]{2,1,0:T(8,128)(2,1)S(1)} collective-permute-done((bf16[4,48,768]{2,1,0:T(8,128)(2,1)S(1)}, bf16[4,48,768]{2,1,0:T(8,128)(2,1)S(1)}, u32[]{:S(2)}, u32[]{:S(2)}) %collective-permute-start.52) | collective-permute-done | bytes 294944 | tf_op jit(solution)/shard_map/ppermute | solution.py:55
  260.1 0.9 fusion.39
  261.0 11.3 %first_back.1 = (f32[1024,768]{1,0:T(8,128)}, f32[1,768]{1,0:T(1,128)}, f32[1,768]{1,0:T(1,128)}, f32[1,768]{1,0:T(1,128)}, f32[1,768]{1,0:T(1,128)}) custom-call(s32[2]{0:T(128)} %pad_add_fusion.refs_0_, bf16[1024,768]{1,0:T(8,128)(2,1)} %refs_1_.5, f32[1024,768]{1,0:T(8,128)} %get-tuple-element.129.refs_2_, f32[1,768]{1,0:T(1,128)} %get-tuple-element.238.refs_2_.refs_3_, ...), custom_call_target="tpu_custom_call" | custom-call | flops 3623878656 | bytes 16000000 | tf_op jit(solution)/shard_map/first_back/pallas_call | solution.py:118
  272.4 5.8 %pack.1 = f32[32,288]{1,0:T(8,128)} custom-call(f32[1,768]{1,0:T(1,128)} %get-tuple-element.167.refs_0_, f32[1,768]{1,0:T(1,128)} %get-tuple-element.168.refs_1_, f32[1,768]{1,0:T(1,128)} %get-tuple-element.169.refs_2_, f32[1,768]{1,0:T(1,128)} %get-tuple-element.170.refs_3_, f32[1,768]{1,0:T(1,128)} %get-tuple-element.171.refs_4_, ...), custom_call_target="tpu_custom_call" | custom-call | tf_op jit(solution)/shard_map/pack/pallas_call | solution.py:794
  279.1 2.3 collective-permute-start.58
  281.5 2.6 collective-permute-done.58
  284.1 1.2 collective-permute-start.59
  286.0 2.4 collective-permute-start.65
  288.8 1.7 collective-permute-start.63
  290.5 1.4 collective-permute-start.60
  292.5 1.2 collective-permute-start.69
  293.7 1.0 collective-permute-start.68
  295.0 1.0 collective-permute-start.67
  296.1 1.1 collective-permute-start.61
  297.2 3.9 %collective-permute-done.61 = f32[2,288]{1,0:T(2,128)S(1)} collective-permute-done((f32[2,288]{1,0:T(2,128)S(1)}, f32[2,288]{1,0:T(2,128)S(1)}, u32[]{:S(2)}, u32[]{:S(2)}) %collective-permute-start.61) | collective-permute-done | bytes 2336 | tf_op jit(solution)/shard_map/ppermute | solution.py:55
  304.4 2.3 collective-permute-start.72
  306.7 1.0 collective-permute-start.71
  308.3 1.9 collective-permute-done.72
  310.2 1.4 collective-permute-done.71
  311.8 1.2 collective-permute-done.73
  (302 shorter events, 33.4 us)
Async XLA Ops:
  3.8 8.3 %collective-permute-start.1 = (bf16[24,1536]{1,0:T(8,128)(2,1)S(1)}, bf16[24,1536]{1,0:T(8,128)(2,1)S(1)}, u32[]{:S(2)}, u32[]{:S(2)}) collective-permute-start(bf16[24,1536]{1,0:T(8,128)(2,1)S(1)} %broadcast_select_fusion.10), channel_id=1, source_target_pairs={{0,1},{1,0},{2,3},{3,2},{4,5},{5,4},{6,7},{7,6},{8,9},{9,8},{10,11... | collective-permute-start | bytes 221192 | tf_op jit(solution)/shard_map/ppermute | solution.py:55
  6.8 10.0 %collective-permute-start.4 = (bf16[48,1152]{1,0:T(8,128)(2,1)S(1)}, bf16[48,1152]{1,0:T(8,128)(2,1)S(1)}, u32[]{:S(2)}, u32[]{:S(2)}) collective-permute-start(bf16[48,1152]{1,0:T(8,128)(2,1)S(1)} %get-tuple-element.228), channel_id=1, source_target_pairs={{0,16},{1,17},{2,18},{3,19},{4,20},{5,21},{6,22},{7,23},{8,24},{9,... | collective-permute-start | bytes 331784 | tf_op jit(solution)/shard_map/ppermute | solution.py:55
  10.5 6.4 %collective-permute-start.3 = (bf16[48,1152]{1,0:T(8,128)(2,1)S(1)}, bf16[48,1152]{1,0:T(8,128)(2,1)S(1)}, u32[]{:S(2)}, u32[]{:S(2)}) collective-permute-start(bf16[48,1152]{1,0:T(8,128)(2,1)S(1)} %get-tuple-element.228), channel_id=1, source_target_pairs={{0,8},{1,9},{2,10},{3,11},{4,12},{5,13},{6,14},{7,15},{8,0},{9,1},... | collective-permute-start | bytes 331784 | tf_op jit(solution)/shard_map/ppermute | solution.py:55
  12.1 8.1 %collective-permute-start.5 = (bf16[48,1152]{1,0:T(8,128)(2,1)S(1)}, bf16[48,1152]{1,0:T(8,128)(2,1)S(1)}, u32[]{:S(2)}, u32[]{:S(2)}) collective-permute-start(bf16[48,1152]{1,0:T(8,128)(2,1)S(1)} %get-tuple-element.228), channel_id=1, source_target_pairs={{0,24},{1,25},{2,26},{3,27},{4,28},{5,29},{6,30},{7,31},{8,16},{9,... | collective-permute-start | bytes 331784 | tf_op jit(solution)/shard_map/ppermute | solution.py:55
  23.1 7.8 %collective-permute-start.21 = (bf16[96,384]{1,0:T(8,128)(2,1)S(1)}, bf16[96,384]{1,0:T(8,128)(2,1)S(1)}, u32[]{:S(2)}, u32[]{:S(2)}) collective-permute-start(bf16[96,384]{1,0:T(8,128)(2,1)S(1)} %broadcast_select_fusion.6), channel_id=1, source_target_pairs={{0,1},{1,0},{2,3},{3,2},{4,5},{5,4},{6,7},{7,6},{8,9},{9,8},{10,11... | collective-permute-start | bytes 221192 | tf_op jit(solution)/shard_map/ppermute | solution.py:55
  28.9 8.9 %collective-permute-start.9 = (bf16[8,288]{1,0:T(8,128)(2,1)S(1)}, bf16[8,288]{1,0:T(8,128)(2,1)S(1)}, u32[]{:S(2)}, u32[]{:S(2)}) collective-permute-start(bf16[8,288]{1,0:T(8,128)(2,1)S(1)} %pad_maximum_fusion.10), channel_id=1, source_target_pairs={{0,8},{1,9},{2,10},{3,11},{4,12},{5,13},{6,14},{7,15},{8,0},{9,1},... | collective-permute-start | bytes 13832 | tf_op jit(solution)/shard_map/ppermute | solution.py:55
  30.9 23.0 %collective-permute-start.13 = (bf16[4,48,1152]{2,1,0:T(8,128)(2,1)S(1)}, bf16[4,48,1152]{2,1,0:T(8,128)(2,1)S(1)}, u32[]{:S(2)}, u32[]{:S(2)}) collective-permute-start(bf16[4,48,1152]{2,1,0:T(8,128)(2,1)S(1)} %pad_maximum_fusion.2.refs_8_.refs_10_), channel_id=1, source_target_pairs={{0,6},{1,7},{2,4},{3,5},{4,2},{5,3},{6,0},{7,1},{8,14},{9,15},{10,... | collective-permute-start | bytes 1327112 | tf_op jit(solution)/shard_map/ppermute | solution.py:55
  33.4 21.0 %collective-permute-start.12 = (bf16[4,48,1152]{2,1,0:T(8,128)(2,1)S(1)}, bf16[4,48,1152]{2,1,0:T(8,128)(2,1)S(1)}, u32[]{:S(2)}, u32[]{:S(2)}) collective-permute-start(bf16[4,48,1152]{2,1,0:T(8,128)(2,1)S(1)} %pad_maximum_fusion.2.refs_8_.refs_10_), channel_id=1, source_target_pairs={{0,4},{1,5},{2,6},{3,7},{4,0},{5,1},{6,2},{7,3},{8,12},{9,13},{10,... | collective-permute-start | bytes 1327112 | tf_op jit(solution)/shard_map/ppermute | solution.py:55
  33.9 20.5 %collective-permute-start.11 = (bf16[4,48,1152]{2,1,0:T(8,128)(2,1)S(1)}, bf16[4,48,1152]{2,1,0:T(8,128)(2,1)S(1)}, u32[]{:S(2)}, u32[]{:S(2)}) collective-permute-start(bf16[4,48,1152]{2,1,0:T(8,128)(2,1)S(1)} %pad_maximum_fusion.2.refs_8_.refs_10_), channel_id=1, source_target_pairs={{0,2},{1,3},{2,0},{3,1},{4,6},{5,7},{6,4},{7,5},{8,10},{9,11},{10,... | collective-permute-start | bytes 1327112 | tf_op jit(solution)/shard_map/ppermute | solution.py:55
  34.4 11.7 %collective-permute-start.20 = (bf16[48,1920]{1,0:T(8,128)(2,1)S(1)}, bf16[48,1920]{1,0:T(8,128)(2,1)S(1)}, u32[]{:S(2)}, u32[]{:S(2)}) collective-permute-start(bf16[48,1920]{1,0:T(8,128)(2,1)S(1)} %maximum_maximum_fusion), channel_id=1, source_target_pairs={{0,24},{1,25},{2,26},{3,27},{4,28},{5,29},{6,30},{7,31},{8,16},{9,... | collective-permute-start | bytes 552968 | tf_op jit(solution)/shard_map/ppermute | solution.py:55
  37.8 8.3 %collective-permute-start.10 = (bf16[16,288]{1,0:T(8,128)(2,1)S(1)}, bf16[16,288]{1,0:T(8,128)(2,1)S(1)}, u32[]{:S(2)}, u32[]{:S(2)}) collective-permute-start(bf16[16,288]{1,0:T(8,128)(2,1)S(1)} %pad_maximum_fusion.9), channel_id=1, source_target_pairs={{0,16},{1,17},{2,18},{3,19},{4,20},{5,21},{6,22},{7,23},{8,24},{9,... | collective-permute-start | bytes 27656 | tf_op jit(solution)/shard_map/ppermute | solution.py:55
  46.1 7.7 %collective-permute-start.19 = (bf16[48,1920]{1,0:T(8,128)(2,1)S(1)}, bf16[48,1920]{1,0:T(8,128)(2,1)S(1)}, u32[]{:S(2)}, u32[]{:S(2)}) collective-permute-start(bf16[48,1920]{1,0:T(8,128)(2,1)S(1)} %maximum_maximum_fusion), channel_id=1, source_target_pairs={{0,16},{1,17},{2,18},{3,19},{4,20},{5,21},{6,22},{7,23},{8,24},{9,... | collective-permute-start | bytes 552968 | tf_op jit(solution)/shard_map/ppermute | solution.py:55
  46.1 8.7 %collective-permute-start.18 = (bf16[48,1920]{1,0:T(8,128)(2,1)S(1)}, bf16[48,1920]{1,0:T(8,128)(2,1)S(1)}, u32[]{:S(2)}, u32[]{:S(2)}) collective-permute-start(bf16[48,1920]{1,0:T(8,128)(2,1)S(1)} %maximum_maximum_fusion), channel_id=1, source_target_pairs={{0,8},{1,9},{2,10},{3,11},{4,12},{5,13},{6,14},{7,15},{8,0},{9,1},... | collective-permute-start | bytes 552968 | tf_op jit(solution)/shard_map/ppermute | solution.py:55
  53.9 9.8 %collective-permute-start.17 = (bf16[4,48,1152]{2,1,0:T(8,128)(2,1)S(1)}, bf16[4,48,1152]{2,1,0:T(8,128)(2,1)S(1)}, u32[]{:S(2)}, u32[]{:S(2)}) collective-permute-start(bf16[4,48,1152]{2,1,0:T(8,128)(2,1)S(1)} %collective-permute-done.13.refs_11_.refs_13_), channel_id=1, source_target_pairs={{0,1},{1,0},{2,3},{3,2},{4,5},{5,4},{6,7},{7,6},{8,9},{9,8},{10,11... | collective-permute-start | bytes 1327112 | tf_op jit(solution)/shard_map/ppermute | solution.py:55
  54.4 12.4 %collective-permute-start.16 = (bf16[4,48,1152]{2,1,0:T(8,128)(2,1)S(1)}, bf16[4,48,1152]{2,1,0:T(8,128)(2,1)S(1)}, u32[]{:S(2)}, u32[]{:S(2)}) collective-permute-start(bf16[4,48,1152]{2,1,0:T(8,128)(2,1)S(1)} %collective-permute-done.12.refs_10_.refs_12_), channel_id=1, source_target_pairs={{0,1},{1,0},{2,3},{3,2},{4,5},{5,4},{6,7},{7,6},{8,9},{9,8},{10,11... | collective-permute-start | bytes 1327112 | tf_op jit(solution)/shard_map/ppermute | solution.py:55
  54.5 12.3 %collective-permute-start.15 = (bf16[4,48,1152]{2,1,0:T(8,128)(2,1)S(1)}, bf16[4,48,1152]{2,1,0:T(8,128)(2,1)S(1)}, u32[]{:S(2)}, u32[]{:S(2)}) collective-permute-start(bf16[4,48,1152]{2,1,0:T(8,128)(2,1)S(1)} %collective-permute-done.11.refs_9_.refs_11_), channel_id=1, source_target_pairs={{0,1},{1,0},{2,3},{3,2},{4,5},{5,4},{6,7},{7,6},{8,9},{9,8},{10,11... | collective-permute-start | bytes 1327112 | tf_op jit(solution)/shard_map/ppermute | solution.py:55
  55.0 8.7 %collective-permute-start.24 = (bf16[192,384]{1,0:T(8,128)(2,1)S(1)}, bf16[192,384]{1,0:T(8,128)(2,1)S(1)}, u32[]{:S(2)}, u32[]{:S(2)}) collective-permute-start(bf16[192,384]{1,0:T(8,128)(2,1)S(1)} %pad_maximum_fusion.5), channel_id=1, source_target_pairs={{0,24},{1,25},{2,26},{3,27},{4,28},{5,29},{6,30},{7,31},{8,16},{9,... | collective-permute-start | bytes 442376 | tf_op jit(solution)/shard_map/ppermute | solution.py:55
  57.5 38.8 %collective-permute-start.23 = (bf16[192,384]{1,0:T(8,128)(2,1)S(1)}, bf16[192,384]{1,0:T(8,128)(2,1)S(1)}, u32[]{:S(2)}, u32[]{:S(2)}) collective-permute-start(bf16[192,384]{1,0:T(8,128)(2,1)S(1)} %pad_maximum_fusion.5), channel_id=1, source_target_pairs={{0,16},{1,17},{2,18},{3,19},{4,20},{5,21},{6,22},{7,23},{8,24},{9,... | collective-permute-start | bytes 442376 | tf_op jit(solution)/shard_map/ppermute | solution.py:55
  63.7 32.6 %collective-permute-start.22 = (bf16[192,384]{1,0:T(8,128)(2,1)S(1)}, bf16[192,384]{1,0:T(8,128)(2,1)S(1)}, u32[]{:S(2)}, u32[]{:S(2)}) collective-permute-start(bf16[192,384]{1,0:T(8,128)(2,1)S(1)} %pad_maximum_fusion.5), channel_id=1, source_target_pairs={{0,8},{1,9},{2,10},{3,11},{4,12},{5,13},{6,14},{7,15},{8,0},{9,1},... | collective-permute-start | bytes 442376 | tf_op jit(solution)/shard_map/ppermute | solution.py:55
  63.7 32.7 %collective-permute-start.27 = (bf16[4,48,1920]{2,1,0:T(8,128)(2,1)S(1)}, bf16[4,48,1920]{2,1,0:T(8,128)(2,1)S(1)}, u32[]{:S(2)}, u32[]{:S(2)}) collective-permute-start(bf16[4,48,1920]{2,1,0:T(8,128)(2,1)S(1)} %pad_maximum_fusion.refs_16_.refs_8_.refs_9_), channel_id=1, source_target_pairs={{0,6},{1,7},{2,4},{3,5},{4,2},{5,3},{6,0},{7,1},{8,14},{9,15},{10,... | collective-permute-start | bytes 2211848 | tf_op jit(solution)/shard_map/ppermute | solution.py:55
  66.8 30.4 %collective-permute-start.26 = (bf16[4,48,1920]{2,1,0:T(8,128)(2,1)S(1)}, bf16[4,48,1920]{2,1,0:T(8,128)(2,1)S(1)}, u32[]{:S(2)}, u32[]{:S(2)}) collective-permute-start(bf16[4,48,1920]{2,1,0:T(8,128)(2,1)S(1)} %pad_maximum_fusion.refs_16_.refs_8_.refs_9_), channel_id=1, source_target_pairs={{0,4},{1,5},{2,6},{3,7},{4,0},{5,1},{6,2},{7,3},{8,12},{9,13},{10,... | collective-permute-start | bytes 2211848 | tf_op jit(solution)/shard_map/ppermute | solution.py:55
  66.8 30.3 %collective-permute-start.25 = (bf16[4,48,1920]{2,1,0:T(8,128)(2,1)S(1)}, bf16[4,48,1920]{2,1,0:T(8,128)(2,1)S(1)}, u32[]{:S(2)}, u32[]{:S(2)}) collective-permute-start(bf16[4,48,1920]{2,1,0:T(8,128)(2,1)S(1)} %pad_maximum_fusion.refs_16_.refs_8_.refs_9_), channel_id=1, source_target_pairs={{0,2},{1,3},{2,0},{3,1},{4,6},{5,7},{6,4},{7,5},{8,10},{9,11},{10,... | collective-permute-start | bytes 2211848 | tf_op jit(solution)/shard_map/ppermute | solution.py:55
  97.2 4.5 %collective-permute-start.29 = (bf16[4,48,1920]{2,1,0:T(8,128)(2,1)S(1)}, bf16[4,48,1920]{2,1,0:T(8,128)(2,1)S(1)}, u32[]{:S(2)}, u32[]{:S(2)}) collective-permute-start(bf16[4,48,1920]{2,1,0:T(8,128)(2,1)S(1)} %collective-permute-done.25.refs_9_.refs_10_), channel_id=1, source_target_pairs={{0,1},{1,0},{2,3},{3,2},{4,5},{5,4},{6,7},{7,6},{8,9},{9,8},{10,11... | collective-permute-start | bytes 2211848 | tf_op jit(solution)/shard_map/ppermute | solution.py:55
  97.7 4.8 %collective-permute-start.30 = (bf16[4,48,1920]{2,1,0:T(8,128)(2,1)S(1)}, bf16[4,48,1920]{2,1,0:T(8,128)(2,1)S(1)}, u32[]{:S(2)}, u32[]{:S(2)}) collective-permute-start(bf16[4,48,1920]{2,1,0:T(8,128)(2,1)S(1)} %collective-permute-done.26.refs_10_.refs_11_), channel_id=1, source_target_pairs={{0,1},{1,0},{2,3},{3,2},{4,5},{5,4},{6,7},{7,6},{8,9},{9,8},{10,11... | collective-permute-start | bytes 2211848 | tf_op jit(solution)/shard_map/ppermute | solution.py:55
  97.8 4.8 %collective-permute-start.31 = (bf16[4,48,1920]{2,1,0:T(8,128)(2,1)S(1)}, bf16[4,48,1920]{2,1,0:T(8,128)(2,1)S(1)}, u32[]{:S(2)}, u32[]{:S(2)}) collective-permute-start(bf16[4,48,1920]{2,1,0:T(8,128)(2,1)S(1)} %collective-permute-done.27.refs_11_.refs_12_), channel_id=1, source_target_pairs={{0,1},{1,0},{2,3},{3,2},{4,5},{5,4},{6,7},{7,6},{8,9},{9,8},{10,11... | collective-permute-start | bytes 2211848 | tf_op jit(solution)/shard_map/ppermute | solution.py:55
  98.8 32.6 %collective-permute-start.34 = (bf16[4,192,384]{2,1,0:T(8,128)(2,1)S(1)}, bf16[4,192,384]{2,1,0:T(8,128)(2,1)}, u32[]{:S(2)}, u32[]{:S(2)}) collective-permute-start(bf16[4,192,384]{2,1,0:T(8,128)(2,1)S(1)} %pad_maximum_fusion.1.refs_17_), channel_id=1, source_target_pairs={{0,6},{1,7},{2,4},{3,5},{4,2},{5,3},{6,0},{7,1},{8,14},{9,15},{10,... | collective-permute-start | bytes 1769480 | tf_op jit(solution)/shard_map/ppermute | solution.py:55
  100.8 30.6 %collective-permute-start.33 = (bf16[4,192,384]{2,1,0:T(8,128)(2,1)S(1)}, bf16[4,192,384]{2,1,0:T(8,128)(2,1)}, u32[]{:S(2)}, u32[]{:S(2)}) collective-permute-start(bf16[4,192,384]{2,1,0:T(8,128)(2,1)S(1)} %pad_maximum_fusion.1.refs_17_), channel_id=1, source_target_pairs={{0,4},{1,5},{2,6},{3,7},{4,0},{5,1},{6,2},{7,3},{8,12},{9,13},{10,... | collective-permute-start | bytes 1769480 | tf_op jit(solution)/shard_map/ppermute | solution.py:55
  101.7 29.8 %collective-permute-start.32 = (bf16[4,192,384]{2,1,0:T(8,128)(2,1)S(1)}, bf16[4,192,384]{2,1,0:T(8,128)(2,1)}, u32[]{:S(2)}, u32[]{:S(2)}) collective-permute-start(bf16[4,192,384]{2,1,0:T(8,128)(2,1)S(1)} %pad_maximum_fusion.1.refs_17_), channel_id=1, source_target_pairs={{0,2},{1,3},{2,0},{3,1},{4,6},{5,7},{6,4},{7,5},{8,10},{9,11},{10,... | collective-permute-start | bytes 1769480 | tf_op jit(solution)/shard_map/ppermute | solution.py:55
  131.5 5.7 %collective-permute-start.39 = (bf16[4,4,192,384]{3,2,1,0:T(8,128)(2,1)}, bf16[4,4,192,384]{3,2,1,0:T(8,128)(2,1)S(1)}, u32[]{:S(2)}, u32[]{:S(2)}) collective-permute-start(bf16[4,4,192,384]{3,2,1,0:T(8,128)(2,1)} %get-tuple-element.127), channel_id=1, source_target_pairs={{0,1},{1,0},{2,3},{3,2},{4,5},{5,4},{6,7},{7,6},{8,9},{9,8},{10,11... | collective-permute-start | bytes 7077896 | tf_op jit(solution)/shard_map/ppermute | solution.py:55
  131.6 10.6 %collective-permute-start.35 = (bf16[4,192,384]{2,1,0:T(8,128)(2,1)S(1)}, bf16[4,192,384]{2,1,0:T(8,128)(2,1)S(1)}, u32[]{:S(2)}, u32[]{:S(2)}) collective-permute-start(bf16[4,192,384]{2,1,0:T(8,128)(2,1)S(1)} %pad_maximum_fusion.1.refs_17_), channel_id=1, source_target_pairs={{0,1},{1,0},{2,3},{3,2},{4,5},{5,4},{6,7},{7,6},{8,9},{9,8},{10,11... | collective-permute-start | bytes 1769480 | tf_op jit(solution)/shard_map/ppermute | solution.py:55
  132.1 11.0 %collective-permute-start.36 = (bf16[4,192,384]{2,1,0:T(8,128)(2,1)}, bf16[4,192,384]{2,1,0:T(8,128)(2,1)S(1)}, u32[]{:S(2)}, u32[]{:S(2)}) collective-permute-start(bf16[4,192,384]{2,1,0:T(8,128)(2,1)} %collective-permute-done.32.refs_18_), channel_id=1, source_target_pairs={{0,1},{1,0},{2,3},{3,2},{4,5},{5,4},{6,7},{7,6},{8,9},{9,8},{10,11... | collective-permute-start | bytes 1769480 | tf_op jit(solution)/shard_map/ppermute | solution.py:55
  132.2 11.7 %collective-permute-start.37 = (bf16[4,192,384]{2,1,0:T(8,128)(2,1)}, bf16[4,192,384]{2,1,0:T(8,128)(2,1)S(1)}, u32[]{:S(2)}, u32[]{:S(2)}) collective-permute-start(bf16[4,192,384]{2,1,0:T(8,128)(2,1)} %collective-permute-done.33.refs_19_), channel_id=1, source_target_pairs={{0,1},{1,0},{2,3},{3,2},{4,5},{5,4},{6,7},{7,6},{8,9},{9,8},{10,11... | collective-permute-start | bytes 1769480 | tf_op jit(solution)/shard_map/ppermute | solution.py:55
  132.6 11.3 %collective-permute-start.38 = (bf16[4,192,384]{2,1,0:T(8,128)(2,1)}, bf16[4,192,384]{2,1,0:T(8,128)(2,1)S(1)}, u32[]{:S(2)}, u32[]{:S(2)}) collective-permute-start(bf16[4,192,384]{2,1,0:T(8,128)(2,1)} %collective-permute-done.34.refs_20_), channel_id=1, source_target_pairs={{0,1},{1,0},{2,3},{3,2},{4,5},{5,4},{6,7},{7,6},{8,9},{9,8},{10,11... | collective-permute-start | bytes 1769480 | tf_op jit(solution)/shard_map/ppermute | solution.py:55
  140.3 41.4 %collective-permute-start.42 = (bf16[4,192,384]{2,1,0:T(8,128)(2,1)S(1)}, bf16[4,192,384]{2,1,0:T(8,128)(2,1)S(1)}, u32[]{:S(2)}, u32[]{:S(2)}) collective-permute-start(bf16[4,192,384]{2,1,0:T(8,128)(2,1)S(1)} %get-tuple-element.186.refs_28_), channel_id=1, source_target_pairs={{0,6},{1,7},{2,4},{3,5},{4,2},{5,3},{6,0},{7,1},{8,14},{9,15},{10,... | collective-permute-start | bytes 1769480 | tf_op jit(solution)/shard_map/ppermute | solution.py:55
  142.2 39.5 %collective-permute-start.41 = (bf16[4,192,384]{2,1,0:T(8,128)(2,1)S(1)}, bf16[4,192,384]{2,1,0:T(8,128)(2,1)S(1)}, u32[]{:S(2)}, u32[]{:S(2)}) collective-permute-start(bf16[4,192,384]{2,1,0:T(8,128)(2,1)S(1)} %get-tuple-element.187.refs_27_), channel_id=1, source_target_pairs={{0,4},{1,5},{2,6},{3,7},{4,0},{5,1},{6,2},{7,3},{8,12},{9,13},{10,... | collective-permute-start | bytes 1769480 | tf_op jit(solution)/shard_map/ppermute | solution.py:55
  143.1 38.6 %collective-permute-start.40 = (bf16[4,192,384]{2,1,0:T(8,128)(2,1)S(1)}, bf16[4,192,384]{2,1,0:T(8,128)(2,1)S(1)}, u32[]{:S(2)}, u32[]{:S(2)}) collective-permute-start(bf16[4,192,384]{2,1,0:T(8,128)(2,1)S(1)} %get-tuple-element.188.refs_26_), channel_id=1, source_target_pairs={{0,2},{1,3},{2,0},{3,1},{4,6},{5,7},{6,4},{7,5},{8,10},{9,11},{10,... | collective-permute-start | bytes 1769480 | tf_op jit(solution)/shard_map/ppermute | solution.py:55
  182.7 5.6 %collective-permute-start.43 = (bf16[4,4,48,1920]{3,2,1,0:T(8,128)(2,1)}, bf16[4,4,48,1920]{3,2,1,0:T(8,128)(2,1)S(1)}, u32[]{:S(2)}, u32[]{:S(2)}) collective-permute-start(bf16[4,4,48,1920]{3,2,1,0:T(8,128)(2,1)} %get-tuple-element.139), channel_id=1, source_target_pairs={{0,1},{1,0},{2,3},{3,2},{4,5},{5,4},{6,7},{7,6},{8,9},{9,8},{10,11... | collective-permute-start | bytes 8847368 | tf_op jit(solution)/shard_map/ppermute | solution.py:55
  182.7 10.0 %collective-permute-start.46 = (bf16[192,384]{1,0:T(8,128)(2,1)S(1)}, bf16[192,384]{1,0:T(8,128)(2,1)S(1)}, u32[]{:S(2)}, u32[]{:S(2)}) collective-permute-start(bf16[192,384]{1,0:T(8,128)(2,1)S(1)} %get-tuple-element.198.refs_13_), channel_id=1, source_target_pairs={{0,24},{1,25},{2,26},{3,27},{4,28},{5,29},{6,30},{7,31},{8,16},{9,... | collective-permute-start | bytes 442376 | tf_op jit(solution)/shard_map/ppermute | solution.py:55
  186.5 31.5 %collective-permute-start.45 = (bf16[192,384]{1,0:T(8,128)(2,1)S(1)}, bf16[192,384]{1,0:T(8,128)(2,1)S(1)}, u32[]{:S(2)}, u32[]{:S(2)}) collective-permute-start(bf16[192,384]{1,0:T(8,128)(2,1)S(1)} %get-tuple-element.199.refs_12_), channel_id=1, source_target_pairs={{0,16},{1,17},{2,18},{3,19},{4,20},{5,21},{6,22},{7,23},{8,24},{9,... | collective-permute-start | bytes 442376 | tf_op jit(solution)/shard_map/ppermute | solution.py:55
  186.5 31.5 %collective-permute-start.44 = (bf16[192,384]{1,0:T(8,128)(2,1)S(1)}, bf16[192,384]{1,0:T(8,128)(2,1)S(1)}, u32[]{:S(2)}, u32[]{:S(2)}) collective-permute-start(bf16[192,384]{1,0:T(8,128)(2,1)S(1)} %get-tuple-element.200.refs_11_), channel_id=1, source_target_pairs={{0,8},{1,9},{2,10},{3,11},{4,12},{5,13},{6,14},{7,15},{8,0},{9,1},... | collective-permute-start | bytes 442376 | tf_op jit(solution)/shard_map/ppermute | solution.py:55
  189.9 28.2 %collective-permute-start.49 = (bf16[4,48,1920]{2,1,0:T(8,128)(2,1)S(1)}, bf16[4,48,1920]{2,1,0:T(8,128)(2,1)S(1)}, u32[]{:S(2)}, u32[]{:S(2)}) collective-permute-start(bf16[4,48,1920]{2,1,0:T(8,128)(2,1)S(1)} %get-tuple-element.182.refs_17_), channel_id=1, source_target_pairs={{0,6},{1,7},{2,4},{3,5},{4,2},{5,3},{6,0},{7,1},{8,14},{9,15},{10,... | collective-permute-start | bytes 2211848 | tf_op jit(solution)/shard_map/ppermute | solution.py:55
  191.8 33.4 %collective-permute-start.48 = (bf16[4,48,1920]{2,1,0:T(8,128)(2,1)S(1)}, bf16[4,48,1920]{2,1,0:T(8,128)(2,1)S(1)}, u32[]{:S(2)}, u32[]{:S(2)}) collective-permute-start(bf16[4,48,1920]{2,1,0:T(8,128)(2,1)S(1)} %get-tuple-element.183.refs_16_), channel_id=1, source_target_pairs={{0,4},{1,5},{2,6},{3,7},{4,0},{5,1},{6,2},{7,3},{8,12},{9,13},{10,... | collective-permute-start | bytes 2211848 | tf_op jit(solution)/shard_map/ppermute | solution.py:55
  192.7 32.5 %collective-permute-start.47 = (bf16[4,48,1920]{2,1,0:T(8,128)(2,1)S(1)}, bf16[4,48,1920]{2,1,0:T(8,128)(2,1)S(1)}, u32[]{:S(2)}, u32[]{:S(2)}) collective-permute-start(bf16[4,48,1920]{2,1,0:T(8,128)(2,1)S(1)} %get-tuple-element.184.refs_15_), channel_id=1, source_target_pairs={{0,2},{1,3},{2,0},{3,1},{4,6},{5,7},{6,4},{7,5},{8,10},{9,11},{10,... | collective-permute-start | bytes 2211848 | tf_op jit(solution)/shard_map/ppermute | solution.py:55
  226.3 5.1 %collective-permute-start.50 = (bf16[4,4,48,768]{3,2,1,0:T(8,128)(2,1)S(1)}, bf16[4,4,48,768]{3,2,1,0:T(8,128)(2,1)S(1)}, u32[]{:S(2)}, u32[]{:S(2)}) collective-permute-start(bf16[4,4,48,768]{3,2,1,0:T(8,128)(2,1)S(1)} %copy-done.46), channel_id=1, source_target_pairs={{0,1},{1,0},{2,3},{3,2},{4,5},{5,4},{6,7},{7,6},{8,9},{9,8},{10,11... | collective-permute-start | bytes 3538952 | tf_op jit(solution)/shard_map/ppermute | solution.py:55
  226.4 31.8 %collective-permute-start.75 = (f32[96,384]{1,0:T(8,128)S(1)}, f32[96,384]{1,0:T(8,128)S(1)}, u32[]{:S(2)}, u32[]{:S(2)}) collective-permute-start(f32[96,384]{1,0:T(8,128)S(1)} %slice_select_fusion.2), channel_id=1, source_target_pairs={{0,1},{1,0},{2,3},{3,2},{4,5},{5,4},{6,7},{7,6},{8,9},{9,8},{10,11... | collective-permute-start | bytes 442376 | tf_op jit(solution)/shard_map/ppermute | solution.py:55
  226.9 21.7 %collective-permute-start.56 = (bf16[48,1920]{1,0:T(8,128)(2,1)S(1)}, bf16[48,1920]{1,0:T(8,128)(2,1)S(1)}, u32[]{:S(2)}, u32[]{:S(2)}) collective-permute-start(bf16[48,1920]{1,0:T(8,128)(2,1)S(1)} %get-tuple-element.190.refs_17_), channel_id=1, source_target_pairs={{0,24},{1,25},{2,26},{3,27},{4,28},{5,29},{6,30},{7,31},{8,16},{9,... | collective-permute-start | bytes 552968 | tf_op jit(solution)/shard_map/ppermute | solution.py:55
  230.6 19.1 %collective-permute-start.55 = (bf16[48,1920]{1,0:T(8,128)(2,1)S(1)}, bf16[48,1920]{1,0:T(8,128)(2,1)S(1)}, u32[]{:S(2)}, u32[]{:S(2)}) collective-permute-start(bf16[48,1920]{1,0:T(8,128)(2,1)S(1)} %get-tuple-element.191.refs_16_), channel_id=1, source_target_pairs={{0,16},{1,17},{2,18},{3,19},{4,20},{5,21},{6,22},{7,23},{8,24},{9,... | collective-permute-start | bytes 552968 | tf_op jit(solution)/shard_map/ppermute | solution.py:55
  230.6 19.8 %collective-permute-start.54 = (bf16[48,1920]{1,0:T(8,128)(2,1)S(1)}, bf16[48,1920]{1,0:T(8,128)(2,1)S(1)}, u32[]{:S(2)}, u32[]{:S(2)}) collective-permute-start(bf16[48,1920]{1,0:T(8,128)(2,1)S(1)} %get-tuple-element.192.refs_15_), channel_id=1, source_target_pairs={{0,8},{1,9},{2,10},{3,11},{4,12},{5,13},{6,14},{7,15},{8,0},{9,1},... | collective-permute-start | bytes 552968 | tf_op jit(solution)/shard_map/ppermute | solution.py:55
  232.4 18.2 %collective-permute-start.53 = (bf16[4,48,768]{2,1,0:T(8,128)(2,1)S(1)}, bf16[4,48,768]{2,1,0:T(8,128)(2,1)S(1)}, u32[]{:S(2)}, u32[]{:S(2)}) collective-permute-start(bf16[4,48,768]{2,1,0:T(8,128)(2,1)S(1)} %get-tuple-element.194.refs_13_), channel_id=1, source_target_pairs={{0,6},{1,7},{2,4},{3,5},{4,2},{5,3},{6,0},{7,1},{8,14},{9,15},{10,... | collective-permute-start | bytes 884744 | tf_op jit(solution)/shard_map/ppermute | solution.py:55
  248.6 8.2 %collective-permute-start.52 = (bf16[4,48,768]{2,1,0:T(8,128)(2,1)S(1)}, bf16[4,48,768]{2,1,0:T(8,128)(2,1)S(1)}, u32[]{:S(2)}, u32[]{:S(2)}) collective-permute-start(bf16[4,48,768]{2,1,0:T(8,128)(2,1)S(1)} %copy-done.35), channel_id=1, source_target_pairs={{0,4},{1,5},{2,6},{3,7},{4,0},{5,1},{6,2},{7,3},{8,12},{9,13},{10,... | collective-permute-start | bytes 884744 | tf_op jit(solution)/shard_map/ppermute | solution.py:55
  249.7 7.6 %collective-permute-start.51 = (bf16[4,48,768]{2,1,0:T(8,128)(2,1)S(1)}, bf16[4,48,768]{2,1,0:T(8,128)(2,1)S(1)}, u32[]{:S(2)}, u32[]{:S(2)}) collective-permute-start(bf16[4,48,768]{2,1,0:T(8,128)(2,1)S(1)} %copy-done.34), channel_id=1, source_target_pairs={{0,2},{1,3},{2,0},{3,1},{4,6},{5,7},{6,4},{7,5},{8,10},{9,11},{10,... | collective-permute-start | bytes 884744 | tf_op jit(solution)/shard_map/ppermute | solution.py:55
  258.9 22.5 %collective-permute-start.74 = (f32[24,1920]{1,0:T(8,128)S(1)}, f32[24,1920]{1,0:T(8,128)S(1)}, u32[]{:S(2)}, u32[]{:S(2)}) collective-permute-start(f32[24,1920]{1,0:T(8,128)S(1)} %slice_select_fusion), channel_id=1, source_target_pairs={{0,1},{1,0},{2,3},{3,2},{4,5},{5,4},{6,7},{7,6},{8,9},{9,8},{10,11... | collective-permute-start | bytes 552968 | tf_op jit(solution)/shard_map/ppermute | solution.py:55
  279.1 5.0 %collective-permute-start.58 = (f32[16,288]{1,0:T(8,128)S(1)}, f32[16,288]{1,0:T(8,128)S(1)}, u32[]{:S(2)}, u32[]{:S(2)}) collective-permute-start(f32[16,288]{1,0:T(8,128)S(1)} %slice_select_fusion.8), channel_id=1, source_target_pairs={{0,16},{1,17},{2,18},{3,19},{4,20},{5,21},{6,22},{7,23},{8,24},{9,... | collective-permute-start | bytes 55304 | tf_op jit(solution)/shard_map/ppermute | solution.py:55
  284.1 6.4 %collective-permute-start.59 = (f32[8,288]{1,0:T(8,128)S(1)}, f32[8,288]{1,0:T(8,128)S(1)}, u32[]{:S(2)}, u32[]{:S(2)}) collective-permute-start(f32[8,288]{1,0:T(8,128)S(1)} %slice_select_fusion.9), channel_id=1, source_target_pairs={{0,8},{1,9},{2,10},{3,11},{4,12},{5,13},{6,14},{7,15},{8,0},{9,1},... | collective-permute-start | bytes 27656 | tf_op jit(solution)/shard_map/ppermute | solution.py:55
  286.0 7.7 %collective-permute-start.65 = (bf16[48,768]{1,0:T(8,128)(2,1)S(1)}, bf16[48,768]{1,0:T(8,128)(2,1)S(1)}, u32[]{:S(2)}, u32[]{:S(2)}) collective-permute-start(bf16[48,768]{1,0:T(8,128)(2,1)S(1)} %copy-done.33), channel_id=1, source_target_pairs={{0,24},{1,25},{2,26},{3,27},{4,28},{5,29},{6,30},{7,31},{8,16},{9,... | collective-permute-start | bytes 221192 | tf_op jit(solution)/shard_map/ppermute | solution.py:55
  288.5 6.5 %collective-permute-start.64 = (bf16[48,768]{1,0:T(8,128)(2,1)S(1)}, bf16[48,768]{1,0:T(8,128)(2,1)S(1)}, u32[]{:S(2)}, u32[]{:S(2)}) collective-permute-start(bf16[48,768]{1,0:T(8,128)(2,1)S(1)} %copy-done.32), channel_id=1, source_target_pairs={{0,16},{1,17},{2,18},{3,19},{4,20},{5,21},{6,22},{7,23},{8,24},{9,... | collective-permute-start | bytes 221192 | tf_op jit(solution)/shard_map/ppermute | solution.py:55
  288.8 7.2 %collective-permute-start.63 = (bf16[48,768]{1,0:T(8,128)(2,1)S(1)}, bf16[48,768]{1,0:T(8,128)(2,1)S(1)}, u32[]{:S(2)}, u32[]{:S(2)}) collective-permute-start(bf16[48,768]{1,0:T(8,128)(2,1)S(1)} %copy-done.31), channel_id=1, source_target_pairs={{0,8},{1,9},{2,10},{3,11},{4,12},{5,13},{6,14},{7,15},{8,0},{9,1},... | collective-permute-start | bytes 221192 | tf_op jit(solution)/shard_map/ppermute | solution.py:55
  290.5 5.5 %collective-permute-start.60 = (f32[4,288]{1,0:T(4,128)S(1)}, f32[4,288]{1,0:T(4,128)S(1)}, u32[]{:S(2)}, u32[]{:S(2)}) collective-permute-start(f32[4,288]{1,0:T(4,128)S(1)} %slice_select_fusion.10), channel_id=1, source_target_pairs={{0,4},{1,5},{2,6},{3,7},{4,0},{5,1},{6,2},{7,3},{8,12},{9,13},{10,... | collective-permute-start | bytes 13832 | tf_op jit(solution)/shard_map/ppermute | solution.py:55
  292.5 11.6 %collective-permute-start.69 = (bf16[4,48,384]{2,1,0:T(8,128)(2,1)S(1)}, bf16[4,48,384]{2,1,0:T(8,128)(2,1)S(1)}, u32[]{:S(2)}, u32[]{:S(2)}) collective-permute-start(bf16[4,48,384]{2,1,0:T(8,128)(2,1)S(1)} %copy-done.22), channel_id=1, source_target_pairs={{0,6},{1,7},{2,4},{3,5},{4,2},{5,3},{6,0},{7,1},{8,14},{9,15},{10,... | collective-permute-start | bytes 442376 | tf_op jit(solution)/shard_map/ppermute | solution.py:55
  293.7 10.4 %collective-permute-start.68 = (bf16[4,48,384]{2,1,0:T(8,128)(2,1)S(1)}, bf16[4,48,384]{2,1,0:T(8,128)(2,1)S(1)}, u32[]{:S(2)}, u32[]{:S(2)}) collective-permute-start(bf16[4,48,384]{2,1,0:T(8,128)(2,1)S(1)} %copy-done.21), channel_id=1, source_target_pairs={{0,4},{1,5},{2,6},{3,7},{4,0},{5,1},{6,2},{7,3},{8,12},{9,13},{10,... | collective-permute-start | bytes 442376 | tf_op jit(solution)/shard_map/ppermute | solution.py:55
  295.0 9.1 %collective-permute-start.67 = (bf16[4,48,384]{2,1,0:T(8,128)(2,1)S(1)}, bf16[4,48,384]{2,1,0:T(8,128)(2,1)S(1)}, u32[]{:S(2)}, u32[]{:S(2)}) collective-permute-start(bf16[4,48,384]{2,1,0:T(8,128)(2,1)S(1)} %copy-done.20), channel_id=1, source_target_pairs={{0,2},{1,3},{2,0},{3,1},{4,6},{5,7},{6,4},{7,5},{8,10},{9,11},{10,... | collective-permute-start | bytes 442376 | tf_op jit(solution)/shard_map/ppermute | solution.py:55
  296.1 5.0 %collective-permute-start.61 = (f32[2,288]{1,0:T(2,128)S(1)}, f32[2,288]{1,0:T(2,128)S(1)}, u32[]{:S(2)}, u32[]{:S(2)}) collective-permute-start(f32[2,288]{1,0:T(2,128)S(1)} %broadcast_select_fusion.32), channel_id=1, source_target_pairs={{0,2},{1,3},{2,0},{3,1},{4,6},{5,7},{6,4},{7,5},{8,10},{9,11},{10,... | collective-permute-start | bytes 6920 | tf_op jit(solution)/shard_map/ppermute | solution.py:55
  304.4 5.8 %collective-permute-start.72 = (bf16[48,384]{1,0:T(8,128)(2,1)S(1)}, bf16[48,384]{1,0:T(8,128)(2,1)S(1)}, u32[]{:S(2)}, u32[]{:S(2)}) collective-permute-start(bf16[48,384]{1,0:T(8,128)(2,1)S(1)} %get-tuple-element.211), channel_id=1, source_target_pairs={{0,24},{1,25},{2,26},{3,27},{4,28},{5,29},{6,30},{7,31},{8,16},{9,... | collective-permute-start | bytes 110600 | tf_op jit(solution)/shard_map/ppermute | solution.py:55
  306.7 4.9 %collective-permute-start.71 = (bf16[48,384]{1,0:T(8,128)(2,1)S(1)}, bf16[48,384]{1,0:T(8,128)(2,1)S(1)}, u32[]{:S(2)}, u32[]{:S(2)}) collective-permute-start(bf16[48,384]{1,0:T(8,128)(2,1)S(1)} %get-tuple-element.212), channel_id=1, source_target_pairs={{0,16},{1,17},{2,18},{3,19},{4,20},{5,21},{6,22},{7,23},{8,24},{9,... | collective-permute-start | bytes 110600 | tf_op jit(solution)/shard_map/ppermute | solution.py:55
  (71 other events, 686.0 us)

commit v3 on v2

--- a/solution.py
+++ b/solution.py
@@ -21,9 +21,8 @@
 NT = (((1,), (1,)), ((), ()))
 TN = (((0,), (0,)), ((), ()))
 ANY = pl.BlockSpec(memory_space=pl.ANY)
+HBM = pl.BlockSpec(memory_space=pltpu.HBM)
 SMEM = pl.BlockSpec(memory_space=pltpu.SMEM)
-VMEM_LIMIT = 56 << 20
-SHARE = 1.0
 
 CORE, X, Y, Z0, Z1 = 1, 2, 4, 8, 16
 CX, CY, CZ0, CZ1 = 1, 2, 4, 8
@@ -34,12 +33,12 @@
     return lax.dot_general(a, b, dims, preferred_element_type=F32)
 
 
-def params(**more):
-    return pltpu.CompilerParams(vmem_limit_bytes=VMEM_LIMIT, **more)
+def params(size):
+    return pltpu.CompilerParams(vmem_limit_bytes=size << 20)
 
 
 def cost(flops, size):
-    return pl.CostEstimate(flops=int(flops * SHARE), bytes_accessed=int(size * SHARE), transcendentals=0)
+    return pl.CostEstimate(flops=int(flops), bytes_accessed=int(size), transcendentals=0)
 
 
 def whole(shape):
@@ -62,8 +61,10 @@
     return jnp.where(first, low, high), jnp.where(first, high, low)
 
 
-def pair_block(array, core):
+def pair_block(array, core, extra=None):
     keep, send = halves(array, core)
+    if extra is not None:
+        keep, send = jnp.concatenate([keep, extra], 1), jnp.concatenate([send, extra], 1)
     other = swap(send, CORE)
     first = core == 0
     return jnp.concatenate([jnp.where(first, keep, other), jnp.where(first, other, keep)], 0)
@@ -93,7 +94,10 @@
 
 
 def scatter_xy(sums, *after):
-    got = tie([swap(part, bits) for part, bits in zip(sums[1:], (X, Y, X | Y))], *after)
+    return sum_xy(sums, tie([swap(part, bits) for part, bits in zip(sums[1:], (X, Y, X | Y))], *after))
+
+
+def sum_xy(sums, got):
     return [add(*(part[spot] for part in [sums[0]] + got)).astype(BF16) for spot in range(4)]
 
 
@@ -109,13 +113,7 @@
 
 
 def kernel_call(kernel, inputs, after, **how):
-    count, extra = len(inputs), len(after)
-
-    def body(*refs):
-        kernel(*refs[:count], *refs[count + extra :])
-
-    how["in_specs"] = how["in_specs"] + [ANY] * extra
-    return pl.pallas_call(body, **how)(*inputs, *after)
+    return pl.pallas_call(kernel, **how)(*tie(inputs[:1], *after), *inputs[1:])
 
 
 def own_rows(block, core):
@@ -133,15 +131,6 @@
 
 def scatter_all(array):
     return lax.psum_scatter(array, AXES, scatter_dimension=0, tiled=True)
-
-
-def gather_small(vector, index):
-    table = vector.reshape(1, -1)
-    for bit in (CORE, X, Y, Z0, Z1):
-        other = swap(table, bit)
-        low = (index & bit) == 0
-        table = jnp.concatenate([jnp.where(low, table, other), jnp.where(low, other, table)], 0)
-    return table
 
 
 def scatter_small(table, index):
@@ -189,8 +178,8 @@
 
 
 def project_attend_kernel(steps, block, place, x, gain, shift, q_bias, v_bias, q_docs, k_docs, *rest):
-    pieces, rest = rest[:-8], rest[-8:]
-    mixed, hidden, out, lse, kept, bias, weight, sem = rest
+    pieces, rest = rest[:-9], rest[-9:]
+    mixed, hidden, out, lse, kept, bias, weight, sem, kept_sem = rest
     width = x.shape[1]
     size = x.shape[0]
     step = pl.program_id(0)
@@ -217,9 +206,8 @@
                 value = (value + q_bias[...]).astype(BF16).astype(F32) * scale
             if part == 2:
                 value = value + v_bias[...]
-            value = value.astype(BF16)
-            mixed[:, sl] = value
-            kept[here, sl] = value
+            kept[here, sl] = value.astype(BF16)
+        pltpu.make_async_copy(kept.at[here, :], mixed.at[here, :], kept_sem).start()
 
     @pl.when(step >= steps)
     def _():
@@ -243,6 +231,10 @@
             lse[0, 0:1, sl] = turned[0:1, :]
             lse[0, 1:2, sl] = turned[HD : HD + 1, :]
 
+    @pl.when(step == pl.num_programs(0) - 1)
+    def _():
+        finish(kept, kept_sem)
+
 
 def project_attend(place, x, gain, shift, q_bias, v_bias, docs, pieces, after=()):
     count, width = x.shape
@@ -259,9 +251,9 @@
         in_specs=[SMEM, pl.BlockSpec((size, width), early)]
         + [whole((1, width))] * 4
         + [whole((LEN, 1)), whole((1, LEN))]
-        + [ANY] * len(pieces),
+        + [HBM] * len(pieces),
         out_specs=[
-            pl.BlockSpec((size, 3 * width), early),
+            HBM,
             pl.BlockSpec((size, width), early),
             pl.BlockSpec((LEN, PAIR), lambda i: (0, late(i))),
             pl.BlockSpec((1, 2, LEN), lambda i: (late(i), 0, 0)),
@@ -277,8 +269,9 @@
             pltpu.VMEM((LEN, LEN), F32),
             pltpu.VMEM((width, 3 * width), BF16),
             pltpu.SemaphoreType.DMA,
+            pltpu.SemaphoreType.DMA,
         ],
-        compiler_params=params(),
+        compiler_params=params(24),
         cost_estimate=cost(28e9, 20e6),
         name="project_attend",
     )
@@ -322,11 +315,11 @@
 
 
 def widen_kernel(steps, terms, place, x, attended, out_bias, gain, shift, fc_bias, cot, *rest):
-    count = terms + 13
+    count = terms + 15
     pieces, rest = rest[:-count], rest[-count:]
     resid, hidden, slope, active = rest[:4]
     outs, rest = rest[4 : 4 + terms], rest[4 + terms :]
-    w_out, w_fc, kept, grad, stage, weight_sems, kept_sem, grad_sem, sems = rest
+    w_out, w_fc, kept, bent, grad, stage, weight_sems, kept_sem, bent_sem, grad_sem, sems = rest
     size, width = x.shape
     depth = w_fc.shape[1]
     step = pl.program_id(0)
@@ -355,8 +348,9 @@
             t = jnp.tanh(u * (c + (c * 0.044715) * square))
             half = 0.5 * (1.0 + t)
             kept[here, sl] = (u * half).astype(BF16)
-            slope[:, sl] = (half + 0.5 * u * (1.0 - t * t) * (c + (3 * c * 0.044715) * square)).astype(BF16)
+            bent[here, sl] = (half + 0.5 * u * (1.0 - t * t) * (c + (3 * c * 0.044715) * square)).astype(BF16)
         pltpu.make_async_copy(kept.at[here, :], active.at[here, :], kept_sem).start()
+        pltpu.make_async_copy(bent.at[here, :], slope.at[here, :], bent_sem).start()
 
     @pl.when(step >= steps)
     def _():
@@ -383,6 +377,7 @@
             finish(stage.at[slot], sems.at[slot])
             finish(stage.at[1 - slot], sems.at[1 - slot])
             finish(kept, kept_sem)
+            finish(bent, bent_sem)
 
 
 def widen(place, x, attended, out_bias, gain, shift, fc_bias, cot, pieces, after=()):
@@ -401,8 +396,8 @@
         in_specs=[SMEM, block(width), block(width)]
         + [whole((1, width))] * 3
         + [whole((1, depth)), ANY]
-        + [ANY] * len(pieces),
-        out_specs=[block(width), block(width), block(depth), ANY] + [ANY] * len(terms),
+        + [HBM] * len(pieces),
+        out_specs=[block(width), block(width), HBM, HBM] + [ANY] * len(terms),
         out_shape=[
             jax.ShapeDtypeStruct((count, width), F32),
             jax.ShapeDtypeStruct((count, width), BF16),
@@ -414,14 +409,16 @@
             pltpu.VMEM((width, width), BF16),
             pltpu.VMEM((width, depth), BF16),
             pltpu.VMEM((count, depth), BF16),
+            pltpu.VMEM((count, depth), BF16),
             pltpu.VMEM((count, width), BF16),
             pltpu.VMEM((2, tall, width), BF16),
             pltpu.SemaphoreType.DMA((2,)),
             pltpu.SemaphoreType.DMA,
             pltpu.SemaphoreType.DMA,
+            pltpu.SemaphoreType.DMA,
             pltpu.SemaphoreType.DMA((2,)),
         ],
-        compiler_params=params(),
+        compiler_params=params(32),
         cost_estimate=cost(2 * count * width * (width + 2 * depth), 30e6),
         name="widen",
     )
@@ -523,7 +520,7 @@
         grid=(steps + depth // width + 1,),
         in_specs=[SMEM, block(width), block(depth), block(depth), block(width)]
         + [whole((1, width))] * 2
-        + [ANY] * (2 + len(pieces)),
+        + [ANY] * 2 + [HBM] * len(pieces),
         out_specs=[block(width)] * 3
         + [whole((1, depth))]
         + [whole((1, width))] * 4
@@ -549,7 +546,7 @@
             pltpu.SemaphoreType.DMA((2,)),
             pltpu.SemaphoreType.DMA((2,)),
         ],
-        compiler_params=params(),
+        compiler_params=params(40),
         cost_estimate=cost(2 * count * width * (2 * width + 4 * depth), 40e6),
         name="narrow",
     )
@@ -618,6 +615,10 @@
         def _():
             finish(h_kept, sem)
 
+        @pl.when(tile >= 2)
+        def _():
+            finish(stage.at[slot], sems.at[slot])
+
         for index in range(3):
             part = kept[index, :, pl.ds(pl.multiple_of(tile * wide, wide), wide)]
             stage[slot, index] = dot(h_kept[...], part, TN).astype(BF16)
@@ -642,12 +643,12 @@
                 finish(stage.at[1 - slot], sems.at[1 - slot])
 
 
-def attend_back(place, mixed, attended, grad_o, lse, docs, hidden, first, number, by_stage, after=()):
+def attend_back(place, mixed, attended, grad_o, lse, docs, hidden, by_stage, after=()):
     width = attended.shape[1]
-    pairs = width // PAIR
+    number = width // PAIR
     block = 256
     wide = 2 * PAIR
-    steps = number * PAIR // wide
+    steps = width // wide
     pair = lambda i: jnp.minimum(i, number - 1)
     column = lambda base: pl.BlockSpec((LEN, PAIR), lambda i: (0, base + pair(i)))
     terms = term_shapes(width, 3 * number * PAIR, by_stage)
@@ -660,12 +661,12 @@
             SMEM,
             whole((1, LEN)),
             whole((LEN, 1)),
-            column(first),
-            column(pairs + first),
-            column(2 * pairs + first),
-            column(first),
-            column(first),
-            pl.BlockSpec((1, 2, LEN), lambda i: (first + pair(i), 0, 0)),
+            column(0),
+            column(number),
+            column(2 * number),
+            column(0),
+            column(0),
+            pl.BlockSpec((1, 2, LEN), lambda i: (pair(i), 0, 0)),
             ANY,
         ],
         out_specs=[column(0)] * 3 + [ANY] * len(terms),
@@ -680,14 +681,14 @@
             pltpu.SemaphoreType.DMA,
             pltpu.SemaphoreType.DMA((2,)),
         ],
-        compiler_params=params(),
-        cost_estimate=cost(42e9 * number / pairs, 10e6),
+        compiler_params=params(20),
+        cost_estimate=cost(42e9, 20e6),
         name="attend_back",
     )
 
 
 def first_back_kernel(place, x, grad_r, gain, *rest):
-    parts, pieces, rest = rest[:6], rest[6:-7], rest[-7:]
+    parts, pieces, rest = rest[:3], rest[3:-7], rest[-7:]
     grad_x, gain_sum, shift_sum, q_sum, v_sum, weight, sem = rest
     width = x.shape[1]
 
@@ -697,17 +698,11 @@
         for total in (gain_sum, shift_sum, q_sum, v_sum):
             total[...] = jnp.zeros_like(total)
 
-    grad_h = None
-    at = 0
-    for index, part in enumerate(parts):
-        wide = part.shape[1]
-        term = dot(part[...], weight[:, at : at + wide], NT)
-        grad_h = term if grad_h is None else grad_h + term
-        if index // 2 != 1:
-            into = q_sum if index // 2 == 0 else v_sum
-            lane = at % width
-            into[:, lane : lane + wide] += jnp.sum(part[...].astype(F32), 0, keepdims=True)
-        at += wide
+    grad_h = dot(parts[0][...], weight[:, :width], NT)
+    for index in (1, 2):
+        grad_h += dot(parts[index][...], weight[:, index * width : (index + 1) * width], NT)
+    for into, part in ((q_sum, parts[0]), (v_sum, parts[2])):
+        into[...] += jnp.sum(part[...].astype(F32), 0, keepdims=True)
     pulled, gains, shifts = norm_back(x[...].astype(F32), gain[...], grad_h)
     grad_x[...] = grad_r[...] + pulled
     gain_sum[...] += gains
@@ -724,11 +719,11 @@
         grid=(count // block,),
         in_specs=[SMEM, rows(block, width), rows(block, width), whole((1, width))]
         + [rows(block, part.shape[1]) for part in parts]
-        + [ANY] * len(pieces),
+        + [HBM] * len(pieces),
         out_specs=[rows(block, width)] + [whole((1, width))] * 4,
         out_shape=[jax.ShapeDtypeStruct((count, width), F32)] + [jax.ShapeDtypeStruct((1, width), F32)] * 4,
         scratch_shapes=[pltpu.VMEM((width, 3 * width), BF16), pltpu.SemaphoreType.DMA],
-        compiler_params=params(),
+        compiler_params=params(56),
         cost_estimate=cost(6 * count * width * width, 16e6),
         name="first_back",
     )
@@ -753,23 +748,61 @@
     return found
 
 
-def unpack_kernel(table, out):
-    devices, lanes = table.shape
+def unpack_rows(table, out, lanes):
+    devices = table.shape[0]
     width = out.shape[1]
     for index, (base, span, first) in enumerate(slots(lanes // 12, width)):
-        pick = one_hot((lanes, width), base, span, first).astype(BF16)
-        value = dot(table[...], pick, NN)
-        out[index : index + 1, :] = jnp.sum(jnp.where(owner((devices, width), span, first), value, 0.0), 0, keepdims=True)
-
-
-def unpack(table):
-    devices, lanes = table.shape
-    width = devices * lanes // 12
+        pick = one_hot((table.shape[1], width), base, span, first).astype(BF16)
+        value = dot(table, pick, NN)
+        mine = owner((devices, width), span, first)
+        out[index : index + 1, :] = jnp.sum(jnp.where(mine, value, 0.0), 0, keepdims=True)
+
+
+def unpack_kernel(place, *rest):
+    pieces, (out, kept, sem) = rest[:4], rest[4:]
+    lane = pieces[0].shape[2] - 128
+    chip = place[0]
+    step = pieces[0].shape[1]
+    for group in range(4):
+        for spot, relative in enumerate(GROUPS[group]):
+            there = pl.ds(pl.multiple_of(lax.bitwise_xor(chip, relative) * step, step), step)
+            pltpu.make_async_copy(pieces[group].at[spot, :, pl.ds(lane, 128)], kept.at[there, :], sem).start()
+    finish(kept, sem)
+    width = out.shape[1]
+    devices = width // (step // 2)
+    lanes = 12 * step // 2
+    parts = []
+    for part in range(-(-lanes // 128)):
+        shape = (devices, width)
+        device = lax.broadcasted_iota(jnp.int32, shape, 0)
+        pick = lax.broadcasted_iota(jnp.int32, shape, 1) == device * (step // 2) + part
+        parts.append(dot(pick.astype(BF16), kept[...], NN).astype(BF16))
+    unpack_rows(jnp.concatenate(parts, 1), out, lanes)
+
+
+def unpack(place, pieces):
+    width = 16 * pieces[0].shape[1]
     return pl.pallas_call(
         unpack_kernel,
+        in_specs=[SMEM] + [HBM] * 4,
         out_shape=jax.ShapeDtypeStruct((12, width), F32),
-        compiler_params=params(),
+        scratch_shapes=[pltpu.VMEM((width, 128), BF16), pltpu.SemaphoreType.DMA],
+        compiler_params=params(16),
         name="unpack",
+    )(place, *pieces)
+
+
+def unpack_whole_kernel(table, out):
+    unpack_rows(table[...], out, table.shape[1])
+
+
+def unpack_whole(table):
+    devices, lanes = table.shape
+    return pl.pallas_call(
+        unpack_whole_kernel,
+        out_shape=jax.ShapeDtypeStruct((12, devices * lanes // 12), F32),
+        compiler_params=params(32),
+        name="unpack_whole",
     )(table)
 
 
@@ -777,16 +810,31 @@
     vectors, out = refs[:-1], refs[-1]
     devices, lanes = out.shape
     width = vectors[0].shape[1]
+    unit = lanes // 12
     rows_of = [vector[:, first : first + width] for vector in vectors for first in range(0, vector.shape[1], width)]
-    total = jnp.zeros(out.shape, F32)
-    for row, (base, span, first) in zip(rows_of, slots(lanes // 12, width)):
-        pick = one_hot((lanes, width), base, span, first).astype(BF16)
-        spread = jnp.where(owner((devices, width), span, first), row, 0.0)
-        for _ in range(3):
-            part = spread.astype(BF16)
-            total = total + dot(part, pick, NT)
-            spread = spread - part.astype(F32)
-    out[...] = total
+    total = jnp.zeros((devices, 12 * unit + (-12 * unit) % 128), F32)
+    full = total.shape[1]
+    at, base = 0, 0
+    for span in (1, 1, 2, 1, 1, 1, 4, 1):
+        size = span * unit + (-span * unit) % 128
+        shape = (size, width)
+        spreads = []
+        for index in range(span):
+            mine = owner((devices, width), span * unit, index * width)
+            spreads.append(jnp.where(mine, rows_of[at + index], 0.0))
+        at += span
+        found = jnp.zeros((devices, size), F32)
+        for index, spread in enumerate(spreads):
+            pick = one_hot(shape, 0, span * unit, index * width).astype(BF16)
+            high = spread.astype(BF16)
+            low = (spread - high.astype(F32)).astype(BF16)
+            both = dot(jnp.concatenate([high, low], 0), pick, NT)
+            found = found + both[:devices] + both[devices:]
+        if size < full:
+            found = jnp.concatenate([found, jnp.zeros((devices, full - size), F32)], 1)
+        total = total + (found if base == 0 else pltpu.roll(found, base * unit, 1))
+        base += span
+    out[...] = total[:, :lanes]
 
 
 def pack(vectors, devices):
@@ -794,7 +842,7 @@
     return pl.pallas_call(
         pack_kernel,
         out_shape=jax.ShapeDtypeStruct((devices, lanes), F32),
-        compiler_params=params(),
+        compiler_params=params(16),
         name="pack",
     )(*vectors)
 
@@ -822,34 +870,34 @@
     index = lax.axis_index("dp") * lax.axis_size("fsdp") + lax.axis_index("fsdp")
     core = index & 1
     place = jnp.stack([index >> 1, core]).astype(jnp.int32)
-    pairs = width // PAIR
-    cut = 4
     by_stage = (lax.axis_size("dp"), lax.axis_size("fsdp")) == (8, 4)
 
     smalls = [ln1_gain, ln1_shift, qv_bias, out_bias, ln2_gain, ln2_shift, fc_bias, proj_bias]
-    smalls = jnp.concatenate([v.astype(F32) for v in smalls]).reshape(1, -1).astype(BF16)
+    smalls = jnp.concatenate([v.astype(F32).reshape(1, -1) for v in smalls], 1).reshape(-1)
     if by_stage:
-        first_column = gather_z(pair_block(qkv_weight, core))
+        extra = jnp.pad(smalls, (0, -smalls.size % 128)).reshape(-1, 128).astype(BF16)
+        extra = jnp.pad(extra, ((0, qkv_weight.shape[0] - extra.shape[0]), (0, 0)))
+        first_block = pair_block(qkv_weight, core, extra)
+        out_weight, fc_weight, proj_weight = tie([out_weight, fc_weight, proj_weight], first_block)
+        first_column = gather_z(first_block)
         wide_block = jnp.concatenate([pair_block(out_weight, core), pair_block(fc_weight, core)], 1)
         proj_block = pair_block(proj_weight, core)
         first_own = gather_xy(first_column)
-        smalls, wide_block = tie([smalls, wide_block], first_column)
-        table = gather_small(smalls, index)
-        wide_column = gather_z(wide_block)
-        wide_column, *first_own = tie([wide_column], *first_own) + first_own
+        (wide_block,) = tie([wide_block], first_column)
+        wide_column = gather_z(wide_block, *first_own)
+        first_pieces = gather_core(first_own)
         wide_own = gather_xy(wide_column)
-        first_pieces = gather_core(first_own)
+        vectors = unpack(place, first_own)
         (proj_block,) = tie([proj_block], wide_column)
     else:
         first_pieces, proj_pieces = [gather_all(qkv_weight)], [gather_all(proj_weight)]
         wide_pieces = [gather_all(w) for w in (out_weight, fc_weight)]
         wide_column = None
-        table = gather_all(smalls)
+        vectors = unpack_whole(gather_all(smalls.reshape(1, -1).astype(BF16)))
     hold = lambda *some: list(some) if by_stage else []
     cores = scatter_core if by_stage else lambda terms: terms[0]
     planes = scatter_xy if by_stage else lambda terms, *after: terms
     columns = scatter_z if by_stage else lambda terms, *after: scatter_all(terms.astype(F32))
-    vectors = unpack(table)
     row = lambda at, count=1: vectors[at : at + count].reshape(1, -1)
 
     mixed, h_one, attended, lse = project_attend(
@@ -887,54 +935,30 @@
         proj_sums = planes(proj_sums, grad_o)
         wide_terms = tie(wide_terms, *proj_sums)
     wide_sums = cores(wide_terms)
-    *head, head_one, head_two = (lambda found: found if by_stage else [*found, None])(
+    *grads, qkv_one, qkv_two = (lambda found: found if by_stage else [*found, None])(
         attend_back(
-            place,
-            mixed,
-            attended,
-            grad_o,
-            lse,
-            doc_ids,
-            h_one,
-            0,
-            cut,
-            by_stage,
-            after=hold(*proj_sums, *wide_sums),
+            place, mixed, attended, grad_o, lse, doc_ids, h_one, by_stage, after=hold(*proj_sums, *wide_sums)
         )
     )
-    proj_grad = columns(proj_sums, head_one)
-    wide_sums = planes(wide_sums, head_one)
+    proj_grad = columns(proj_sums, qkv_one)
+    wide_sums = planes(wide_sums, qkv_one)
     if by_stage:
-        head_one, head_two = tie([head_one, head_two], proj_grad, *wide_sums)
-    head_sums = cores([head_one, head_two])
-    *tail, tail_one, tail_two = (lambda found: found if by_stage else [*found, None])(
-        attend_back(
-            place,
-            mixed,
-            attended,
-            grad_o,
-            lse,
-            doc_ids,
-            h_one,
-            cut,
-            pairs - cut,
-            by_stage,
-            after=hold(*head_sums, *wide_sums),
-        )
-    )
-    parts = [part for both in zip(head, tail) for part in both]
-    head_sums = planes(head_sums, tail_one)
-    wide_grad = columns(wide_sums, tail_one)
+        qkv_one, qkv_two = tie([qkv_one, qkv_two], proj_grad, *wide_sums)
+    qkv_sums = cores([qkv_one, qkv_two])
+    grad_x, gain_one, shift_one, q_sum, v_sum = first_back(
+        place, tokens, grad_r, row(0), grads, first_pieces, after=hold(*qkv_sums)
+    )
+    sums = [gain_one, shift_one, q_sum, v_sum, out_sum, gain_two, shift_two, fc_sum, proj_sum]
+    wide_grad = columns(wide_sums, grad_x)
     if by_stage:
-        tail_one, tail_two = tie([tail_one, tail_two], wide_grad, *head_sums)
-    tail_sums = cores([tail_one, tail_two])
-    grad_x, gain_one, shift_one, q_sum, v_sum = first_back(
-        place, tokens, grad_r, row(0), parts, first_pieces, after=hold(*head_sums, *tail_sums)
-    )
-    sums = [gain_one, shift_one, q_sum, v_sum, out_sum, gain_two, shift_two, fc_sum, proj_sum]
-    sums = pack(sums, devices)
-    head_grad = columns(head_sums, grad_x)
-    tail_grad = columns(planes(tail_sums, grad_x))
+        by_x, by_y, by_both = (swap(part, bits) for part, bits in zip(qkv_sums[1:], (X, Y, X | Y)))
+        by_x, by_y = tie([by_x, by_y], grad_x)
+        sums[0] = tie(sums[:1], wide_grad, by_x, by_y)[0]
+        sums = pack(sums, devices)
+        qkv_sums = sum_xy(qkv_sums, tie([by_x, by_y, by_both], sums))
+    else:
+        sums = pack(sums, devices)
+    qkv_grad = columns(qkv_sums)
 
     def sides(grad):
         if by_stage:
@@ -946,15 +970,10 @@
     half = depth // 2
     fc_grad = jnp.concatenate([side[:, :half] for side in both], 1)
     out_grad = jnp.concatenate([side[:, half:] for side in both], 1)
-    parts = []
-    heads, tails = sides(head_grad), sides(tail_grad)
-    for section in range(3):
-        for both, number in ((heads, cut), (tails, pairs - cut)):
-            start = section * number * PAIR // 2
-            for pair in range(0, number, 2):
-                lane = start + pair * PAIR // 2
-                parts += [side[:, lane : lane + PAIR] for side in both]
-    qkv_grad = jnp.concatenate(parts, 1)
+    both = sides(qkv_grad)
+    qkv_grad = jnp.concatenate(
+        [side[:, lane : lane + PAIR] for lane in range(0, both[0].shape[1], PAIR) for side in both], 1
+    )
     own = scatter_small(sums, index) if by_stage else scatter_all(sums).reshape(-1)
     n = width // devices
     spots = (0, n, 2 * n, 4 * n, 5 * n, 6 * n, 7 * n, 11 * n, 12 * n)

time: 319 us -> 278 us (0.87)
  Pallas kernels: 152 us -> 136 us
  waiting for transfers between devices: 59.9 us -> 48.4 us
  other arithmetic: 19.8 us -> 10 us
  starting transfers between devices: 72.3 us -> 63.1 us
  local copies, waits for them, and re-layouts: 8.07 us -> 13.5 us
    ppermute x76 -> x63, waiting for transfers between devices: 59.9 us -> 48.4 us  [swap(): return lax.ppermute(array, AXES, [(i, i ^ bit) for i in range(count)])]
    pallas_call x7 -> x6, Pallas kernels: 146 us -> 135 us  [the longest x5 132 us: kernel_call(): return pl.pallas_call(kernel, **how)(*tie(inputs[:1], *after), *inputs[1:])]
    ppermute x76 -> x63, starting transfers between devices: 72.3 us -> 63.1 us  [swap(): return lax.ppermute(array, AXES, [(i, i ^ bit) for i in range(count)])]
    unnamed x137 -> x91, local copies, waits for them, and re-layouts: 3.74 us -> 9.87 us
    pallas_call x1, Pallas kernels: 5.85 us -> 1.02 us  [pack(): pl.pallas_call(pack_kernel, out_shape=jax.ShapeDtypeStruct((devices, lane...]
    convert_element_type x4 -> x3, other arithmetic: 6.73 us -> 3.3 us  [scatter_core(): return [add(mine[g], got[g]).astype(BF16) for g in range(4)]]
  transfers between devices with their start and end apart: 76 -> 63, of which waited for: 25 -> 21; matrix products, arithmetic and copies ran while one was open for 7% -> 4% of each run, Pallas kernels for 48% -> 49%
where the time goes in v3:
time: 278 us; the launch traced here: 273 us
  Pallas kernels  136 us (49%)
  starting transfers between devices  63.1 us (23%)
  waiting for transfers between devices  48.4 us (17%)
  local copies, waits for them, and re-layouts  13.5 us (5%)
  other arithmetic  10 us (4%)
    pallas_call x5, Pallas kernels, kernel_call(): return pl.pallas_call(kernel, **how)(*tie(inputs[:1], *after), *inputs[1:])  132 us
    ppermute x63, starting transfers between devices, swap(): return lax.ppermute(array, AXES, [(i, i ^ bit) for i in range(count)])  63.1 us
    ppermute x63, waiting for transfers between devices, swap(): return lax.ppermute(array, AXES, [(i, i ^ bit) for i in range(count)])  48.4 us
    unnamed x91, local copies, waits for them, and re-layouts  9.87 us
  transfers between devices with their start and end apart: 63, of which 21 were waited for; matrix products, arithmetic and copies ran while one was open for 4% of the time, Pallas kernels for 49%

profile of v3, /device:TPU:0, one launch (start us, length us, event | category | flops | bytes accessed | tf_op | source)
XLA Modules:
  0.0 273.4 jit_solution(9913603110455158107)
XLA Ops:
  0.7 0.9 concatenate.37
  1.6 0.9 broadcast_select_fusion.17
  3.0 0.9 copy.29.q_docs.k_docs
  4.0 2.9 %collective-permute-start.3 = (bf16[48,1280]{1,0:T(8,128)(2,1)S(1)}, bf16[48,1280]{1,0:T(8,128)(2,1)S(1)}, u32[]{:S(2)}, u32[]{:S(2)}) collective-permute-start(bf16[48,1280]{1,0:T(8,128)(2,1)S(1)} %get-tuple-element.212), channel_id=1, source_target_pairs={{0,8},{1,9},{2,10},{3,11},{4,12},{5,13},{6,14},{7,15},{8,0},{9,1},... | collective-permute-start | bytes 368648 | tf_op jit(solution)/shard_map/ppermute | solution.py:54
  7.0 2.6 collective-permute-start.4
  9.5 0.7 broadcast_select_fusion.20
  12.4 6.9 %collective-permute-done.4 = bf16[48,1280]{1,0:T(8,128)(2,1)S(1)} collective-permute-done((bf16[48,1280]{1,0:T(8,128)(2,1)S(1)}, bf16[48,1280]{1,0:T(8,128)(2,1)S(1)}, u32[]{:S(2)}, u32[]{:S(2)}) %collective-permute-start.4) | collective-permute-done | bytes 122912 | tf_op jit(solution)/shard_map/ppermute | solution.py:54
  19.4 1.6 collective-permute-start.10
  21.0 1.4 collective-permute-start.11
  22.9 2.2 collective-permute-start.6
  25.3 1.2 collective-permute-done.16
  26.5 1.0 collective-permute-start.7
  27.5 1.2 collective-permute-done.6
  28.7 3.2 %collective-permute-start.8 = (bf16[48,1920]{1,0:T(8,128)(2,1)S(1)}, bf16[48,1920]{1,0:T(8,128)(2,1)S(1)}, u32[]{:S(2)}, u32[]{:S(2)}) collective-permute-start(bf16[48,1920]{1,0:T(8,128)(2,1)S(1)} %maximum_maximum_fusion), channel_id=1, source_target_pairs={{0,24},{1,25},{2,26},{3,27},{4,28},{5,29},{6,30},{7,31},{8,16},{9,... | collective-permute-start | bytes 552968 | tf_op jit(solution)/shard_map/ppermute | solution.py:54
  31.9 10.4 %collective-permute-done.7 = bf16[48,1920]{1,0:T(8,128)(2,1)S(1)} collective-permute-done((bf16[48,1920]{1,0:T(8,128)(2,1)S(1)}, bf16[48,1920]{1,0:T(8,128)(2,1)S(1)}, u32[]{:S(2)}, u32[]{:S(2)}) %collective-permute-start.7) | collective-permute-done | bytes 184352 | tf_op jit(solution)/shard_map/ppermute | solution.py:54
  43.5 3.1 %collective-permute-start.17 = (bf16[192,384]{1,0:T(8,128)(2,1)S(1)}, bf16[192,384]{1,0:T(8,128)(2,1)S(1)}, u32[]{:S(2)}, u32[]{:S(2)}) collective-permute-start(bf16[192,384]{1,0:T(8,128)(2,1)S(1)} %pad_maximum_fusion.5), channel_id=1, source_target_pairs={{0,8},{1,9},{2,10},{3,11},{4,12},{5,13},{6,14},{7,15},{8,0},{9,1},... | collective-permute-start | bytes 442376 | tf_op jit(solution)/shard_map/ppermute | solution.py:54
  46.6 3.0 %unpack.1 = f32[12,768]{1,0:T(8,128)S(1)} custom-call(s32[2]{0:T(128)S(1)} %pad_add_fusion.place, bf16[4,48,1280]{2,1,0:T(8,128)(2,1)S(1)} %pad_maximum_fusion.2.rest_0_.rest_3_, bf16[4,48,1280]{2,1,0:T(8,128)(2,1)S(1)} %collective-permute-done.9.rest_1_.rest_4_, bf16[4,48,1280]{2,1,0:T(8,128)(2,1)S(1)} %collective-permute-done.10.rest_2_.rest_5_, ...), custom_call_target="tpu_custom_call" | custom-call | tf_op jit(solution)/shard_map/unpack/pallas_call | solution.py:785
  49.7 1.6 collective-permute-start.20
  51.3 1.5 collective-permute-start.21
  52.8 1.2 collective-permute-start.22
  54.0 2.8 %collective-permute-start.18 = (bf16[192,384]{1,0:T(8,128)(2,1)S(1)}, bf16[192,384]{1,0:T(8,128)(2,1)S(1)}, u32[]{:S(2)}, u32[]{:S(2)}) collective-permute-start(bf16[192,384]{1,0:T(8,128)(2,1)S(1)} %pad_maximum_fusion.5), channel_id=1, source_target_pairs={{0,16},{1,17},{2,18},{3,19},{4,20},{5,21},{6,22},{7,23},{8,24},{9,... | collective-permute-start | bytes 442376 | tf_op jit(solution)/shard_map/ppermute | solution.py:54
  56.7 1.3 collective-permute-start.19
  58.1 26.9 %project_attend.1 = (bf16[1024,2304]{1,0:T(8,128)(2,1)S(1)}, bf16[1024,768]{1,0:T(8,128)(2,1)S(1)}, bf16[1024,768]{1,0:T(8,128)(2,1)S(1)}, f32[6,2,1024]{2,1,0:T(2,128)S(1)}) custom-call(s32[2]{0:T(128)S(1)} %pad_add_fusion.place, bf16[1024,768]{1,0:T(8,128)(2,1)S(1)} %copy-done.12, f32[1,768]{1,0:T(1,128)S(1)} %get-tuple-element.226.gain, ...), custom_call_target="tpu_custom_call" | custom-call | flops 28000000000 | bytes 20000000 | tf_op jit(solution)/shard_map/project_attend/pallas_call | solution.py:116
  85.1 2.1 copy-done.24
  87.2 1.2 copy-done.25
  90.8 1.5 collective-permute-start.28
  92.3 1.0 collective-permute-start.29
  94.0 24.3 %widen.1 = (f32[1024,768]{1,0:T(8,128)S(1)}, bf16[1024,768]{1,0:T(8,128)(2,1)S(1)}, bf16[1024,3072]{1,0:T(8,128)(2,1)}, bf16[1024,3072]{1,0:T(8,128)(2,1)}, bf16...) custom-call(s32[2]{0:T(128)S(1)} %pad_add_fusion.place, bf16[1024,768]{1,0:T(8,128)(2,1)S(1)} %copy-done.12, ...), custom_call_target="tpu_custom_call" | custom-call | flops 10871635968 | bytes 30000000 | tf_op jit(solution)/shard_map/widen/pallas_call | solution.py:116
  118.3 1.7 copy-done.20
  121.2 3.4 %collective-permute-done.30 = bf16[4,4,192,384]{3,2,1,0:T(8,128)(2,1)S(1)} collective-permute-done((bf16[4,4,192,384]{3,2,1,0:T(8,128)(2,1)S(1)}, bf16[4,4,192,384]{3,2,1,0:T(8,128)(2,1)S(1)}, u32[]{:S(2)}, u32[]{:S(2)}) %collective-permute-start.30) | collective-permute-done | bytes 2359328 | tf_op jit(solution)/shard_map/ppermute | solution.py:54
  125.3 1.0 collective-permute-start.35
  126.3 1.1 collective-permute-start.36
  127.4 1.4 collective-permute-start.37
  128.8 34.1 %narrow.1 = (bf16[1024,768]{1,0:T(8,128)(2,1)}, f32[1024,768]{1,0:T(8,128)}, bf16[1024,768]{1,0:T(8,128)(2,1)S(1)}, f32[1,3072]{1,0:T(1,128)S(1)}, f32[1,768]{1,...) custom-call(s32[2]{0:T(128)S(1)} %pad_add_fusion.place, ...), custom_call_target="tpu_custom_call" | custom-call | flops 21743271936 | bytes 40000000 | tf_op jit(solution)/shard_map/narrow/pallas_call | solution.py:116
  163.5 3.0 %collective-permute-start.40 = (bf16[192,384]{1,0:T(8,128)(2,1)S(1)}, bf16[192,384]{1,0:T(8,128)(2,1)S(1)}, u32[]{:S(2)}, u32[]{:S(2)}) collective-permute-start(bf16[192,384]{1,0:T(8,128)(2,1)S(1)} %get-tuple-element.195), channel_id=1, source_target_pairs={{0,16},{1,17},{2,18},{3,19},{4,20},{5,21},{6,22},{7,23},{8,24},{9,... | collective-permute-start | bytes 442376 | tf_op jit(solution)/shard_map/ppermute | solution.py:54
  166.5 1.3 collective-permute-start.41
  167.8 1.1 collective-permute-done.38
  169.0 0.8 add_convert_fusion
  169.7 1.0 collective-permute-start.42
  170.7 1.1 collective-permute-start.43
  172.5 1.5 collective-permute-start.44
  174.0 35.6 %attend_back.1 = (bf16[1024,768]{1,0:T(8,128)(2,1)S(1)}, bf16[1024,768]{1,0:T(8,128)(2,1)S(1)}, bf16[1024,768]{1,0:T(8,128)(2,1)S(1)}, bf16[4,4,48,1152]{3,2,1,0:T(8,128)(2,1)S(1)}, bf16[4,4,48,1152]{3,2,1,0:T(8,128)(2,1)}) custom-call(s32[2]{0:T(128)S(1)} %pad_add_fusion.place, s32[1,1024]{1,0:T(1,128)S(1)} %bitcast.155, s32[1024,1]{1,0:T(8,128)S(1)} %copy.29.q_docs.k_docs, ...), custom_call_target="tpu_custom_call" | custom-call | flops 41999998976 | bytes 20000000 | tf_op jit(solution)/shard_map/attend_back/pallas_call | solution.py:116
  209.6 1.1 copy-done.19
  210.8 1.5 fusion.50
  213.1 2.9 %collective-permute-done.62 = f32[96,384]{1,0:T(8,128)S(1)} collective-permute-done((f32[96,384]{1,0:T(8,128)S(1)}, f32[96,384]{1,0:T(8,128)S(1)}, u32[]{:S(2)}, u32[]{:S(2)}) %collective-permute-start.62) | collective-permute-done | bytes 147488 | tf_op jit(solution)/shard_map/ppermute | solution.py:54
  216.8 2.4 collective-permute-start.47
  219.2 2.0 collective-permute-start.48
  221.2 1.8 add_convert_fusion.8
  223.1 1.5 collective-permute-start.49
  225.1 11.4 %first_back.1 = (f32[1024,768]{1,0:T(8,128)}, f32[1,768]{1,0:T(1,128)}, f32[1,768]{1,0:T(1,128)}, f32[1,768]{1,0:T(1,128)}, f32[1,768]{1,0:T(1,128)}) custom-call(s32[2]{0:T(128)} %copy-done.10, bf16[1024,768]{1,0:T(8,128)(2,1)} %x.9, f32[1024,768]{1,0:T(8,128)} %get-tuple-element.155.grad_r, f32[1,768]{1,0:T(1,128)} %copy-done.9, ...), custom_call_target="tpu_custom_call" | custom-call | flops 3623878656 | bytes 16000000 | tf_op jit(solution)/shard_map/first_back/pallas_call | solution.py:116
  239.4 1.0 pack.1
  240.5 1.0 collective-permute-start.51
  241.5 1.5 collective-permute-start.56
  243.1 2.5 collective-permute-done.51
  246.0 3.3 %collective-permute-done.52 = f32[8,288]{1,0:T(8,128)S(1)} collective-permute-done((f32[8,288]{1,0:T(8,128)S(1)}, f32[8,288]{1,0:T(8,128)S(1)}, u32[]{:S(2)}, u32[]{:S(2)}) %collective-permute-start.52) | collective-permute-done | bytes 9248 | tf_op jit(solution)/shard_map/ppermute | solution.py:54
  249.3 1.3 collective-permute-start.53
  251.4 2.6 collective-permute-done.53
  254.0 1.3 collective-permute-start.54
  255.9 1.7 collective-permute-done.54
  257.9 1.0 collective-permute-start.57
  258.9 1.6 collective-permute-start.58
  260.5 1.9 collective-permute-start.59
  263.5 1.5 collective-permute-done.57
  265.1 5.4 %collective-permute-done.58 = bf16[48,1152]{1,0:T(8,128)(2,1)S(1)} collective-permute-done((bf16[48,1152]{1,0:T(8,128)(2,1)S(1)}, bf16[48,1152]{1,0:T(8,128)(2,1)S(1)}, u32[]{:S(2)}, u32[]{:S(2)}) %collective-permute-start.58) | collective-permute-done | bytes 110624 | tf_op jit(solution)/shard_map/ppermute | solution.py:54
  (218 shorter events, 21.4 us)
Async XLA Ops:
  2.5 1.5 collective-permute-start
  4.0 8.4 %collective-permute-start.3 = (bf16[48,1280]{1,0:T(8,128)(2,1)S(1)}, bf16[48,1280]{1,0:T(8,128)(2,1)S(1)}, u32[]{:S(2)}, u32[]{:S(2)}) collective-permute-start(bf16[48,1280]{1,0:T(8,128)(2,1)S(1)} %get-tuple-element.212), channel_id=1, source_target_pairs={{0,8},{1,9},{2,10},{3,11},{4,12},{5,13},{6,14},{7,15},{8,0},{9,1},... | collective-permute-start | bytes 368648 | tf_op jit(solution)/shard_map/ppermute | solution.py:54
  7.0 12.4 %collective-permute-start.4 = (bf16[48,1280]{1,0:T(8,128)(2,1)S(1)}, bf16[48,1280]{1,0:T(8,128)(2,1)S(1)}, u32[]{:S(2)}, u32[]{:S(2)}) collective-permute-start(bf16[48,1280]{1,0:T(8,128)(2,1)S(1)} %get-tuple-element.212), channel_id=1, source_target_pairs={{0,16},{1,17},{2,18},{3,19},{4,20},{5,21},{6,22},{7,23},{8,24},{9,... | collective-permute-start | bytes 368648 | tf_op jit(solution)/shard_map/ppermute | solution.py:54
  9.5 9.8 %collective-permute-start.5 = (bf16[48,1280]{1,0:T(8,128)(2,1)S(1)}, bf16[48,1280]{1,0:T(8,128)(2,1)S(1)}, u32[]{:S(2)}, u32[]{:S(2)}) collective-permute-start(bf16[48,1280]{1,0:T(8,128)(2,1)S(1)} %get-tuple-element.212), channel_id=1, source_target_pairs={{0,24},{1,25},{2,26},{3,27},{4,28},{5,29},{6,30},{7,31},{8,16},{9,... | collective-permute-start | bytes 368648 | tf_op jit(solution)/shard_map/ppermute | solution.py:54
  10.3 1.2 collective-permute-start.1
  10.3 1.5 collective-permute-start.2
  19.4 23.4 %collective-permute-start.10 = (bf16[4,48,1280]{2,1,0:T(8,128)(2,1)S(1)}, bf16[4,48,1280]{2,1,0:T(8,128)(2,1)S(1)}, u32[]{:S(2)}, u32[]{:S(2)}) collective-permute-start(bf16[4,48,1280]{2,1,0:T(8,128)(2,1)S(1)} %pad_maximum_fusion.2.rest_0_.rest_3_), channel_id=1, source_target_pairs={{0,4},{1,5},{2,6},{3,7},{4,0},{5,1},{6,2},{7,3},{8,12},{9,13},{10,... | collective-permute-start | bytes 1474568 | tf_op jit(solution)/shard_map/ppermute | solution.py:54
  21.0 22.1 %collective-permute-start.11 = (bf16[4,48,1280]{2,1,0:T(8,128)(2,1)S(1)}, bf16[4,48,1280]{2,1,0:T(8,128)(2,1)S(1)}, u32[]{:S(2)}, u32[]{:S(2)}) collective-permute-start(bf16[4,48,1280]{2,1,0:T(8,128)(2,1)S(1)} %pad_maximum_fusion.2.rest_0_.rest_3_), channel_id=1, source_target_pairs={{0,6},{1,7},{2,4},{3,5},{4,2},{5,3},{6,0},{7,1},{8,14},{9,15},{10,... | collective-permute-start | bytes 1474568 | tf_op jit(solution)/shard_map/ppermute | solution.py:54
  22.4 20.2 %collective-permute-start.9 = (bf16[4,48,1280]{2,1,0:T(8,128)(2,1)S(1)}, bf16[4,48,1280]{2,1,0:T(8,128)(2,1)S(1)}, u32[]{:S(2)}, u32[]{:S(2)}) collective-permute-start(bf16[4,48,1280]{2,1,0:T(8,128)(2,1)S(1)} %pad_maximum_fusion.2.rest_0_.rest_3_), channel_id=1, source_target_pairs={{0,2},{1,3},{2,0},{3,1},{4,6},{5,7},{6,4},{7,5},{8,10},{9,11},{10,... | collective-permute-start | bytes 1474568 | tf_op jit(solution)/shard_map/ppermute | solution.py:54
  22.9 5.7 %collective-permute-start.6 = (bf16[48,1920]{1,0:T(8,128)(2,1)S(1)}, bf16[48,1920]{1,0:T(8,128)(2,1)S(1)}, u32[]{:S(2)}, u32[]{:S(2)}) collective-permute-start(bf16[48,1920]{1,0:T(8,128)(2,1)S(1)} %maximum_maximum_fusion), channel_id=1, source_target_pairs={{0,8},{1,9},{2,10},{3,11},{4,12},{5,13},{6,14},{7,15},{8,0},{9,1},... | collective-permute-start | bytes 552968 | tf_op jit(solution)/shard_map/ppermute | solution.py:54
  25.2 1.3 collective-permute-start.16
  25.3 148.6 %copy-start.10 = (s32[2]{0:T(128)}, s32[2]{0:T(128)S(1)}, u32[]{:S(2)}) copy-start(s32[2]{0:T(128)S(1)} %pad_add_fusion.place) | copy-start | bytes 28
  26.5 15.8 %collective-permute-start.7 = (bf16[48,1920]{1,0:T(8,128)(2,1)S(1)}, bf16[48,1920]{1,0:T(8,128)(2,1)S(1)}, u32[]{:S(2)}, u32[]{:S(2)}) collective-permute-start(bf16[48,1920]{1,0:T(8,128)(2,1)S(1)} %maximum_maximum_fusion), channel_id=1, source_target_pairs={{0,16},{1,17},{2,18},{3,19},{4,20},{5,21},{6,22},{7,23},{8,24},{9,... | collective-permute-start | bytes 552968 | tf_op jit(solution)/shard_map/ppermute | solution.py:54
  28.7 14.7 %collective-permute-start.8 = (bf16[48,1920]{1,0:T(8,128)(2,1)S(1)}, bf16[48,1920]{1,0:T(8,128)(2,1)S(1)}, u32[]{:S(2)}, u32[]{:S(2)}) collective-permute-start(bf16[48,1920]{1,0:T(8,128)(2,1)S(1)} %maximum_maximum_fusion), channel_id=1, source_target_pairs={{0,24},{1,25},{2,26},{3,27},{4,28},{5,29},{6,30},{7,31},{8,16},{9,... | collective-permute-start | bytes 552968 | tf_op jit(solution)/shard_map/ppermute | solution.py:54
  42.3 7.4 %collective-permute-start.12 = (bf16[4,48,1280]{2,1,0:T(8,128)(2,1)S(1)}, bf16[4,48,1280]{2,1,0:T(8,128)(2,1)S(1)}, u32[]{:S(2)}, u32[]{:S(2)}) collective-permute-start(bf16[4,48,1280]{2,1,0:T(8,128)(2,1)S(1)} %pad_maximum_fusion.2.rest_0_.rest_3_), channel_id=1, source_target_pairs={{0,1},{1,0},{2,3},{3,2},{4,5},{5,4},{6,7},{7,6},{8,9},{9,8},{10,11... | collective-permute-start | bytes 1474568 | tf_op jit(solution)/shard_map/ppermute | solution.py:54
  42.6 10.2 %collective-permute-start.13 = (bf16[4,48,1280]{2,1,0:T(8,128)(2,1)S(1)}, bf16[4,48,1280]{2,1,0:T(8,128)(2,1)S(1)}, u32[]{:S(2)}, u32[]{:S(2)}) collective-permute-start(bf16[4,48,1280]{2,1,0:T(8,128)(2,1)S(1)} %collective-permute-done.9.rest_1_.rest_4_), channel_id=1, source_target_pairs={{0,1},{1,0},{2,3},{3,2},{4,5},{5,4},{6,7},{7,6},{8,9},{9,8},{10,11... | collective-permute-start | bytes 1474568 | tf_op jit(solution)/shard_map/ppermute | solution.py:54
  42.8 11.1 %collective-permute-start.14 = (bf16[4,48,1280]{2,1,0:T(8,128)(2,1)S(1)}, bf16[4,48,1280]{2,1,0:T(8,128)(2,1)S(1)}, u32[]{:S(2)}, u32[]{:S(2)}) collective-permute-start(bf16[4,48,1280]{2,1,0:T(8,128)(2,1)S(1)} %collective-permute-done.10.rest_2_.rest_5_), channel_id=1, source_target_pairs={{0,1},{1,0},{2,3},{3,2},{4,5},{5,4},{6,7},{7,6},{8,9},{9,8},{10,11... | collective-permute-start | bytes 1474568 | tf_op jit(solution)/shard_map/ppermute | solution.py:54
  43.1 13.6 %collective-permute-start.15 = (bf16[4,48,1280]{2,1,0:T(8,128)(2,1)S(1)}, bf16[4,48,1280]{2,1,0:T(8,128)(2,1)S(1)}, u32[]{:S(2)}, u32[]{:S(2)}) collective-permute-start(bf16[4,48,1280]{2,1,0:T(8,128)(2,1)S(1)} %collective-permute-done.11.rest_3_.rest_6_), channel_id=1, source_target_pairs={{0,1},{1,0},{2,3},{3,2},{4,5},{5,4},{6,7},{7,6},{8,9},{9,8},{10,11... | collective-permute-start | bytes 1474568 | tf_op jit(solution)/shard_map/ppermute | solution.py:54
  43.5 7.7 %collective-permute-start.17 = (bf16[192,384]{1,0:T(8,128)(2,1)S(1)}, bf16[192,384]{1,0:T(8,128)(2,1)S(1)}, u32[]{:S(2)}, u32[]{:S(2)}) collective-permute-start(bf16[192,384]{1,0:T(8,128)(2,1)S(1)} %pad_maximum_fusion.5), channel_id=1, source_target_pairs={{0,8},{1,9},{2,10},{3,11},{4,12},{5,13},{6,14},{7,15},{8,0},{9,1},... | collective-permute-start | bytes 442376 | tf_op jit(solution)/shard_map/ppermute | solution.py:54
  49.7 38.8 %collective-permute-start.20 = (bf16[4,48,1920]{2,1,0:T(8,128)(2,1)S(1)}, bf16[4,48,1920]{2,1,0:T(8,128)(2,1)S(1)}, u32[]{:S(2)}, u32[]{:S(2)}) collective-permute-start(bf16[4,48,1920]{2,1,0:T(8,128)(2,1)S(1)} %pad_maximum_fusion.rest_0_), channel_id=1, source_target_pairs={{0,2},{1,3},{2,0},{3,1},{4,6},{5,7},{6,4},{7,5},{8,10},{9,11},{10,... | collective-permute-start | bytes 2211848 | tf_op jit(solution)/shard_map/ppermute | solution.py:54
  51.3 37.3 %collective-permute-start.21 = (bf16[4,48,1920]{2,1,0:T(8,128)(2,1)S(1)}, bf16[4,48,1920]{2,1,0:T(8,128)(2,1)S(1)}, u32[]{:S(2)}, u32[]{:S(2)}) collective-permute-start(bf16[4,48,1920]{2,1,0:T(8,128)(2,1)S(1)} %pad_maximum_fusion.rest_0_), channel_id=1, source_target_pairs={{0,4},{1,5},{2,6},{3,7},{4,0},{5,1},{6,2},{7,3},{8,12},{9,13},{10,... | collective-permute-start | bytes 2211848 | tf_op jit(solution)/shard_map/ppermute | solution.py:54
  52.8 35.8 %collective-permute-start.22 = (bf16[4,48,1920]{2,1,0:T(8,128)(2,1)S(1)}, bf16[4,48,1920]{2,1,0:T(8,128)(2,1)S(1)}, u32[]{:S(2)}, u32[]{:S(2)}) collective-permute-start(bf16[4,48,1920]{2,1,0:T(8,128)(2,1)S(1)} %pad_maximum_fusion.rest_0_), channel_id=1, source_target_pairs={{0,6},{1,7},{2,4},{3,5},{4,2},{5,3},{6,0},{7,1},{8,14},{9,15},{10,... | collective-permute-start | bytes 2211848 | tf_op jit(solution)/shard_map/ppermute | solution.py:54
  54.0 34.4 %collective-permute-start.18 = (bf16[192,384]{1,0:T(8,128)(2,1)S(1)}, bf16[192,384]{1,0:T(8,128)(2,1)S(1)}, u32[]{:S(2)}, u32[]{:S(2)}) collective-permute-start(bf16[192,384]{1,0:T(8,128)(2,1)S(1)} %pad_maximum_fusion.5), channel_id=1, source_target_pairs={{0,16},{1,17},{2,18},{3,19},{4,20},{5,21},{6,22},{7,23},{8,24},{9,... | collective-permute-start | bytes 442376 | tf_op jit(solution)/shard_map/ppermute | solution.py:54
  56.7 31.7 %collective-permute-start.19 = (bf16[192,384]{1,0:T(8,128)(2,1)S(1)}, bf16[192,384]{1,0:T(8,128)(2,1)S(1)}, u32[]{:S(2)}, u32[]{:S(2)}) collective-permute-start(bf16[192,384]{1,0:T(8,128)(2,1)S(1)} %pad_maximum_fusion.5), channel_id=1, source_target_pairs={{0,24},{1,25},{2,26},{3,27},{4,28},{5,29},{6,30},{7,31},{8,16},{9,... | collective-permute-start | bytes 442376 | tf_op jit(solution)/shard_map/ppermute | solution.py:54
  88.5 2.3 collective-permute-start.23
  88.6 3.7 %collective-permute-start.24 = (bf16[4,48,1920]{2,1,0:T(8,128)(2,1)S(1)}, bf16[4,48,1920]{2,1,0:T(8,128)(2,1)S(1)}, u32[]{:S(2)}, u32[]{:S(2)}) collective-permute-start(bf16[4,48,1920]{2,1,0:T(8,128)(2,1)S(1)} %collective-permute-done.20.rest_1_), channel_id=1, source_target_pairs={{0,1},{1,0},{2,3},{3,2},{4,5},{5,4},{6,7},{7,6},{8,9},{9,8},{10,11... | collective-permute-start | bytes 2211848 | tf_op jit(solution)/shard_map/ppermute | solution.py:54
  89.1 4.3 %collective-permute-start.25 = (bf16[4,48,1920]{2,1,0:T(8,128)(2,1)S(1)}, bf16[4,48,1920]{2,1,0:T(8,128)(2,1)S(1)}, u32[]{:S(2)}, u32[]{:S(2)}) collective-permute-start(bf16[4,48,1920]{2,1,0:T(8,128)(2,1)S(1)} %collective-permute-done.21.rest_2_), channel_id=1, source_target_pairs={{0,1},{1,0},{2,3},{3,2},{4,5},{5,4},{6,7},{7,6},{8,9},{9,8},{10,11... | collective-permute-start | bytes 2211848 | tf_op jit(solution)/shard_map/ppermute | solution.py:54
  89.2 4.8 %collective-permute-start.26 = (bf16[4,48,1920]{2,1,0:T(8,128)(2,1)S(1)}, bf16[4,48,1920]{2,1,0:T(8,128)(2,1)S(1)}, u32[]{:S(2)}, u32[]{:S(2)}) collective-permute-start(bf16[4,48,1920]{2,1,0:T(8,128)(2,1)S(1)} %collective-permute-done.22.rest_3_), channel_id=1, source_target_pairs={{0,1},{1,0},{2,3},{3,2},{4,5},{5,4},{6,7},{7,6},{8,9},{9,8},{10,11... | collective-permute-start | bytes 2211848 | tf_op jit(solution)/shard_map/ppermute | solution.py:54
  89.6 30.3 %collective-permute-start.27 = (bf16[4,192,384]{2,1,0:T(8,128)(2,1)S(1)}, bf16[4,192,384]{2,1,0:T(8,128)(2,1)S(1)}, u32[]{:S(2)}, u32[]{:S(2)}) collective-permute-start(bf16[4,192,384]{2,1,0:T(8,128)(2,1)S(1)} %pad_maximum_fusion.1.rest_8_), channel_id=1, source_target_pairs={{0,2},{1,3},{2,0},{3,1},{4,6},{5,7},{6,4},{7,5},{8,10},{9,11},{10,... | collective-permute-start | bytes 1769480 | tf_op jit(solution)/shard_map/ppermute | solution.py:54
  90.8 29.1 %collective-permute-start.28 = (bf16[4,192,384]{2,1,0:T(8,128)(2,1)S(1)}, bf16[4,192,384]{2,1,0:T(8,128)(2,1)S(1)}, u32[]{:S(2)}, u32[]{:S(2)}) collective-permute-start(bf16[4,192,384]{2,1,0:T(8,128)(2,1)S(1)} %pad_maximum_fusion.1.rest_8_), channel_id=1, source_target_pairs={{0,4},{1,5},{2,6},{3,7},{4,0},{5,1},{6,2},{7,3},{8,12},{9,13},{10,... | collective-permute-start | bytes 1769480 | tf_op jit(solution)/shard_map/ppermute | solution.py:54
  92.3 27.6 %collective-permute-start.29 = (bf16[4,192,384]{2,1,0:T(8,128)(2,1)S(1)}, bf16[4,192,384]{2,1,0:T(8,128)(2,1)S(1)}, u32[]{:S(2)}, u32[]{:S(2)}) collective-permute-start(bf16[4,192,384]{2,1,0:T(8,128)(2,1)S(1)} %pad_maximum_fusion.1.rest_8_), channel_id=1, source_target_pairs={{0,6},{1,7},{2,4},{3,5},{4,2},{5,3},{6,0},{7,1},{8,14},{9,15},{10,... | collective-permute-start | bytes 1769480 | tf_op jit(solution)/shard_map/ppermute | solution.py:54
  119.9 4.6 %collective-permute-start.30 = (bf16[4,4,192,384]{3,2,1,0:T(8,128)(2,1)S(1)}, bf16[4,4,192,384]{3,2,1,0:T(8,128)(2,1)S(1)}, u32[]{:S(2)}, u32[]{:S(2)}) collective-permute-start(bf16[4,4,192,384]{3,2,1,0:T(8,128)(2,1)S(1)} %get-tuple-element.127), channel_id=1, source_target_pairs={{0,1},{1,0},{2,3},{3,2},{4,5},{5,4},{6,7},{7,6},{8,9},{9,8},{10,11... | collective-permute-start | bytes 7077896 | tf_op jit(solution)/shard_map/ppermute | solution.py:54
  120.2 6.1 %collective-permute-start.31 = (bf16[4,192,384]{2,1,0:T(8,128)(2,1)S(1)}, bf16[4,192,384]{2,1,0:T(8,128)(2,1)S(1)}, u32[]{:S(2)}, u32[]{:S(2)}) collective-permute-start(bf16[4,192,384]{2,1,0:T(8,128)(2,1)S(1)} %pad_maximum_fusion.1.rest_8_), channel_id=1, source_target_pairs={{0,1},{1,0},{2,3},{3,2},{4,5},{5,4},{6,7},{7,6},{8,9},{9,8},{10,11... | collective-permute-start | bytes 1769480 | tf_op jit(solution)/shard_map/ppermute | solution.py:54
  120.5 6.9 %collective-permute-start.32 = (bf16[4,192,384]{2,1,0:T(8,128)(2,1)S(1)}, bf16[4,192,384]{2,1,0:T(8,128)(2,1)S(1)}, u32[]{:S(2)}, u32[]{:S(2)}) collective-permute-start(bf16[4,192,384]{2,1,0:T(8,128)(2,1)S(1)} %collective-permute-done.27.rest_9_), channel_id=1, source_target_pairs={{0,1},{1,0},{2,3},{3,2},{4,5},{5,4},{6,7},{7,6},{8,9},{9,8},{10,11... | collective-permute-start | bytes 1769480 | tf_op jit(solution)/shard_map/ppermute | solution.py:54
  120.7 8.2 %collective-permute-start.33 = (bf16[4,192,384]{2,1,0:T(8,128)(2,1)S(1)}, bf16[4,192,384]{2,1,0:T(8,128)(2,1)S(1)}, u32[]{:S(2)}, u32[]{:S(2)}) collective-permute-start(bf16[4,192,384]{2,1,0:T(8,128)(2,1)S(1)} %collective-permute-done.28.rest_10_), channel_id=1, source_target_pairs={{0,1},{1,0},{2,3},{3,2},{4,5},{5,4},{6,7},{7,6},{8,9},{9,8},{10,11... | collective-permute-start | bytes 1769480 | tf_op jit(solution)/shard_map/ppermute | solution.py:54
  121.0 7.8 %collective-permute-start.34 = (bf16[4,192,384]{2,1,0:T(8,128)(2,1)S(1)}, bf16[4,192,384]{2,1,0:T(8,128)(2,1)S(1)}, u32[]{:S(2)}, u32[]{:S(2)}) collective-permute-start(bf16[4,192,384]{2,1,0:T(8,128)(2,1)S(1)} %collective-permute-done.29.rest_11_), channel_id=1, source_target_pairs={{0,1},{1,0},{2,3},{3,2},{4,5},{5,4},{6,7},{7,6},{8,9},{9,8},{10,11... | collective-permute-start | bytes 1769480 | tf_op jit(solution)/shard_map/ppermute | solution.py:54
  125.3 37.7 %collective-permute-start.35 = (bf16[4,192,384]{2,1,0:T(8,128)(2,1)S(1)}, bf16[4,192,384]{2,1,0:T(8,128)(2,1)S(1)}, u32[]{:S(2)}, u32[]{:S(2)}) collective-permute-start(bf16[4,192,384]{2,1,0:T(8,128)(2,1)S(1)} %get-tuple-element.185), channel_id=1, source_target_pairs={{0,2},{1,3},{2,0},{3,1},{4,6},{5,7},{6,4},{7,5},{8,10},{9,11},{10,... | collective-permute-start | bytes 1769480 | tf_op jit(solution)/shard_map/ppermute | solution.py:54
  126.3 36.7 %collective-permute-start.36 = (bf16[4,192,384]{2,1,0:T(8,128)(2,1)S(1)}, bf16[4,192,384]{2,1,0:T(8,128)(2,1)S(1)}, u32[]{:S(2)}, u32[]{:S(2)}) collective-permute-start(bf16[4,192,384]{2,1,0:T(8,128)(2,1)S(1)} %get-tuple-element.184), channel_id=1, source_target_pairs={{0,4},{1,5},{2,6},{3,7},{4,0},{5,1},{6,2},{7,3},{8,12},{9,13},{10,... | collective-permute-start | bytes 1769480 | tf_op jit(solution)/shard_map/ppermute | solution.py:54
  127.4 35.5 %collective-permute-start.37 = (bf16[4,192,384]{2,1,0:T(8,128)(2,1)S(1)}, bf16[4,192,384]{2,1,0:T(8,128)(2,1)S(1)}, u32[]{:S(2)}, u32[]{:S(2)}) collective-permute-start(bf16[4,192,384]{2,1,0:T(8,128)(2,1)S(1)} %get-tuple-element.183), channel_id=1, source_target_pairs={{0,6},{1,7},{2,4},{3,5},{4,2},{5,3},{6,0},{7,1},{8,14},{9,15},{10,... | collective-permute-start | bytes 1769480 | tf_op jit(solution)/shard_map/ppermute | solution.py:54
  163.3 5.7 %collective-permute-start.38 = (bf16[4,4,48,1920]{3,2,1,0:T(8,128)(2,1)}, bf16[4,4,48,1920]{3,2,1,0:T(8,128)(2,1)S(1)}, u32[]{:S(2)}, u32[]{:S(2)}) collective-permute-start(bf16[4,4,48,1920]{3,2,1,0:T(8,128)(2,1)} %get-tuple-element.140), channel_id=1, source_target_pairs={{0,1},{1,0},{2,3},{3,2},{4,5},{5,4},{6,7},{7,6},{8,9},{9,8},{10,11... | collective-permute-start | bytes 8847368 | tf_op jit(solution)/shard_map/ppermute | solution.py:54
  163.4 9.1 %collective-permute-start.39 = (bf16[192,384]{1,0:T(8,128)(2,1)S(1)}, bf16[192,384]{1,0:T(8,128)(2,1)S(1)}, u32[]{:S(2)}, u32[]{:S(2)}) collective-permute-start(bf16[192,384]{1,0:T(8,128)(2,1)S(1)} %get-tuple-element.196), channel_id=1, source_target_pairs={{0,8},{1,9},{2,10},{3,11},{4,12},{5,13},{6,14},{7,15},{8,0},{9,1},... | collective-permute-start | bytes 442376 | tf_op jit(solution)/shard_map/ppermute | solution.py:54
  163.5 47.2 %collective-permute-start.40 = (bf16[192,384]{1,0:T(8,128)(2,1)S(1)}, bf16[192,384]{1,0:T(8,128)(2,1)S(1)}, u32[]{:S(2)}, u32[]{:S(2)}) collective-permute-start(bf16[192,384]{1,0:T(8,128)(2,1)S(1)} %get-tuple-element.195), channel_id=1, source_target_pairs={{0,16},{1,17},{2,18},{3,19},{4,20},{5,21},{6,22},{7,23},{8,24},{9,... | collective-permute-start | bytes 442376 | tf_op jit(solution)/shard_map/ppermute | solution.py:54
  166.5 44.2 %collective-permute-start.41 = (bf16[192,384]{1,0:T(8,128)(2,1)S(1)}, bf16[192,384]{1,0:T(8,128)(2,1)S(1)}, u32[]{:S(2)}, u32[]{:S(2)}) collective-permute-start(bf16[192,384]{1,0:T(8,128)(2,1)S(1)} %get-tuple-element.194), channel_id=1, source_target_pairs={{0,24},{1,25},{2,26},{3,27},{4,28},{5,29},{6,30},{7,31},{8,16},{9,... | collective-permute-start | bytes 442376 | tf_op jit(solution)/shard_map/ppermute | solution.py:54
  169.7 41.1 %collective-permute-start.42 = (bf16[4,48,1920]{2,1,0:T(8,128)(2,1)S(1)}, bf16[4,48,1920]{2,1,0:T(8,128)(2,1)S(1)}, u32[]{:S(2)}, u32[]{:S(2)}) collective-permute-start(bf16[4,48,1920]{2,1,0:T(8,128)(2,1)S(1)} %get-tuple-element.181), channel_id=1, source_target_pairs={{0,2},{1,3},{2,0},{3,1},{4,6},{5,7},{6,4},{7,5},{8,10},{9,11},{10,... | collective-permute-start | bytes 2211848 | tf_op jit(solution)/shard_map/ppermute | solution.py:54
  170.7 40.1 %collective-permute-start.43 = (bf16[4,48,1920]{2,1,0:T(8,128)(2,1)S(1)}, bf16[4,48,1920]{2,1,0:T(8,128)(2,1)S(1)}, u32[]{:S(2)}, u32[]{:S(2)}) collective-permute-start(bf16[4,48,1920]{2,1,0:T(8,128)(2,1)S(1)} %get-tuple-element.180), channel_id=1, source_target_pairs={{0,4},{1,5},{2,6},{3,7},{4,0},{5,1},{6,2},{7,3},{8,12},{9,13},{10,... | collective-permute-start | bytes 2211848 | tf_op jit(solution)/shard_map/ppermute | solution.py:54
  172.5 38.4 %collective-permute-start.44 = (bf16[4,48,1920]{2,1,0:T(8,128)(2,1)S(1)}, bf16[4,48,1920]{2,1,0:T(8,128)(2,1)S(1)}, u32[]{:S(2)}, u32[]{:S(2)}) collective-permute-start(bf16[4,48,1920]{2,1,0:T(8,128)(2,1)S(1)} %get-tuple-element.179), channel_id=1, source_target_pairs={{0,6},{1,7},{2,4},{3,5},{4,2},{5,3},{6,0},{7,1},{8,14},{9,15},{10,... | collective-permute-start | bytes 2211848 | tf_op jit(solution)/shard_map/ppermute | solution.py:54
  212.5 8.7 %collective-permute-start.45 = (bf16[4,4,48,1152]{3,2,1,0:T(8,128)(2,1)}, bf16[4,4,48,1152]{3,2,1,0:T(8,128)(2,1)}, u32[]{:S(2)}, u32[]{:S(2)}) collective-permute-start(bf16[4,4,48,1152]{3,2,1,0:T(8,128)(2,1)} %get-tuple-element.153), channel_id=1, source_target_pairs={{0,1},{1,0},{2,3},{3,2},{4,5},{5,4},{6,7},{7,6},{8,9},{9,8},{10,11... | collective-permute-start | bytes 5308424 | tf_op jit(solution)/shard_map/ppermute | solution.py:54
  212.5 3.5 %collective-permute-start.62 = (f32[96,384]{1,0:T(8,128)S(1)}, f32[96,384]{1,0:T(8,128)S(1)}, u32[]{:S(2)}, u32[]{:S(2)}) collective-permute-start(f32[96,384]{1,0:T(8,128)S(1)} %slice_select_fusion.2), channel_id=1, source_target_pairs={{0,1},{1,0},{2,3},{3,2},{4,5},{5,4},{6,7},{7,6},{8,9},{9,8},{10,11... | collective-permute-start | bytes 442376 | tf_op jit(solution)/shard_map/ppermute | solution.py:54
  216.8 19.8 %collective-permute-start.46 = (bf16[48,1920]{1,0:T(8,128)(2,1)S(1)}, bf16[48,1920]{1,0:T(8,128)(2,1)S(1)}, u32[]{:S(2)}, u32[]{:S(2)}) collective-permute-start(bf16[48,1920]{1,0:T(8,128)(2,1)S(1)} %copy-done.31), channel_id=1, source_target_pairs={{0,8},{1,9},{2,10},{3,11},{4,12},{5,13},{6,14},{7,15},{8,0},{9,1},... | collective-permute-start | bytes 552968 | tf_op jit(solution)/shard_map/ppermute | solution.py:54
  216.8 19.8 %collective-permute-start.47 = (bf16[48,1920]{1,0:T(8,128)(2,1)S(1)}, bf16[48,1920]{1,0:T(8,128)(2,1)S(1)}, u32[]{:S(2)}, u32[]{:S(2)}) collective-permute-start(bf16[48,1920]{1,0:T(8,128)(2,1)S(1)} %copy-done.30), channel_id=1, source_target_pairs={{0,16},{1,17},{2,18},{3,19},{4,20},{5,21},{6,22},{7,23},{8,24},{9,... | collective-permute-start | bytes 552968 | tf_op jit(solution)/shard_map/ppermute | solution.py:54
  219.2 17.4 %collective-permute-start.48 = (bf16[48,1920]{1,0:T(8,128)(2,1)S(1)}, bf16[48,1920]{1,0:T(8,128)(2,1)S(1)}, u32[]{:S(2)}, u32[]{:S(2)}) collective-permute-start(bf16[48,1920]{1,0:T(8,128)(2,1)S(1)} %get-tuple-element.190), channel_id=1, source_target_pairs={{0,24},{1,25},{2,26},{3,27},{4,28},{5,29},{6,30},{7,31},{8,16},{9,... | collective-permute-start | bytes 552968 | tf_op jit(solution)/shard_map/ppermute | solution.py:54
  223.1 13.7 %collective-permute-start.49 = (bf16[4,48,1152]{2,1,0:T(8,128)(2,1)S(1)}, bf16[4,48,1152]{2,1,0:T(8,128)(2,1)S(1)}, u32[]{:S(2)}, u32[]{:S(2)}) collective-permute-start(bf16[4,48,1152]{2,1,0:T(8,128)(2,1)S(1)} %get-tuple-element.189), channel_id=1, source_target_pairs={{0,2},{1,3},{2,0},{3,1},{4,6},{5,7},{6,4},{7,5},{8,10},{9,11},{10,... | collective-permute-start | bytes 1327112 | tf_op jit(solution)/shard_map/ppermute | solution.py:54
  224.6 12.1 %collective-permute-start.50 = (bf16[4,48,1152]{2,1,0:T(8,128)(2,1)S(1)}, bf16[4,48,1152]{2,1,0:T(8,128)(2,1)S(1)}, u32[]{:S(2)}, u32[]{:S(2)}) collective-permute-start(bf16[4,48,1152]{2,1,0:T(8,128)(2,1)S(1)} %get-tuple-element.188), channel_id=1, source_target_pairs={{0,4},{1,5},{2,6},{3,7},{4,0},{5,1},{6,2},{7,3},{8,12},{9,13},{10,... | collective-permute-start | bytes 1327112 | tf_op jit(solution)/shard_map/ppermute | solution.py:54
  240.5 5.0 %collective-permute-start.51 = (f32[16,288]{1,0:T(8,128)S(1)}, f32[16,288]{1,0:T(8,128)S(1)}, u32[]{:S(2)}, u32[]{:S(2)}) collective-permute-start(f32[16,288]{1,0:T(8,128)S(1)} %slice_select_fusion.6), channel_id=1, source_target_pairs={{0,16},{1,17},{2,18},{3,19},{4,20},{5,21},{6,22},{7,23},{8,24},{9,... | collective-permute-start | bytes 55304 | tf_op jit(solution)/shard_map/ppermute | solution.py:54
  241.5 14.4 %collective-permute-start.56 = (bf16[4,48,1152]{2,1,0:T(8,128)(2,1)S(1)}, bf16[4,48,1152]{2,1,0:T(8,128)(2,1)S(1)}, u32[]{:S(2)}, u32[]{:S(2)}) collective-permute-start(bf16[4,48,1152]{2,1,0:T(8,128)(2,1)S(1)} %get-tuple-element.187), channel_id=1, source_target_pairs={{0,6},{1,7},{2,4},{3,5},{4,2},{5,3},{6,0},{7,1},{8,14},{9,15},{10,... | collective-permute-start | bytes 1327112 | tf_op jit(solution)/shard_map/ppermute | solution.py:54
  243.1 2.9 %collective-permute-start.61 = (f32[24,1920]{1,0:T(8,128)S(1)}, f32[24,1920]{1,0:T(8,128)S(1)}, u32[]{:S(2)}, u32[]{:S(2)}) collective-permute-start(f32[24,1920]{1,0:T(8,128)S(1)} %slice_select_fusion), channel_id=1, source_target_pairs={{0,1},{1,0},{2,3},{3,2},{4,5},{5,4},{6,7},{7,6},{8,9},{9,8},{10,11... | collective-permute-start | bytes 552968 | tf_op jit(solution)/shard_map/ppermute | solution.py:54
  245.5 3.8 %collective-permute-start.52 = (f32[8,288]{1,0:T(8,128)S(1)}, f32[8,288]{1,0:T(8,128)S(1)}, u32[]{:S(2)}, u32[]{:S(2)}) collective-permute-start(f32[8,288]{1,0:T(8,128)S(1)} %slice_select_fusion.7), channel_id=1, source_target_pairs={{0,8},{1,9},{2,10},{3,11},{4,12},{5,13},{6,14},{7,15},{8,0},{9,1},... | collective-permute-start | bytes 27656 | tf_op jit(solution)/shard_map/ppermute | solution.py:54
  249.3 4.6 %collective-permute-start.53 = (f32[4,288]{1,0:T(4,128)S(1)}, f32[4,288]{1,0:T(4,128)S(1)}, u32[]{:S(2)}, u32[]{:S(2)}) collective-permute-start(f32[4,288]{1,0:T(4,128)S(1)} %slice_select_fusion.8), channel_id=1, source_target_pairs={{0,4},{1,5},{2,6},{3,7},{4,0},{5,1},{6,2},{7,3},{8,12},{9,13},{10,... | collective-permute-start | bytes 13832 | tf_op jit(solution)/shard_map/ppermute | solution.py:54
  254.0 3.7 %collective-permute-start.54 = (f32[2,288]{1,0:T(2,128)S(1)}, f32[2,288]{1,0:T(2,128)S(1)}, u32[]{:S(2)}, u32[]{:S(2)}) collective-permute-start(f32[2,288]{1,0:T(2,128)S(1)} %broadcast_select_fusion.22), channel_id=1, source_target_pairs={{0,2},{1,3},{2,0},{3,1},{4,6},{5,7},{6,4},{7,5},{8,10},{9,11},{10,... | collective-permute-start | bytes 6920 | tf_op jit(solution)/shard_map/ppermute | solution.py:54
  257.6 4.7 %collective-permute-start.55 = (f32[1,288]{1,0:T(1,128)S(1)}, f32[1,288]{1,0:T(1,128)S(1)}, u32[]{:S(2)}, u32[]{:S(2)}) collective-permute-start(f32[1,288]{1,0:T(1,128)S(1)} %broadcast_select_fusion.23), channel_id=1, source_target_pairs={{0,1},{1,0},{2,3},{3,2},{4,5},{5,4},{6,7},{7,6},{8,9},{9,8},{10,11... | collective-permute-start | bytes 3464 | tf_op jit(solution)/shard_map/ppermute | solution.py:54
  257.9 7.2 %collective-permute-start.57 = (bf16[48,1152]{1,0:T(8,128)(2,1)S(1)}, bf16[48,1152]{1,0:T(8,128)(2,1)S(1)}, u32[]{:S(2)}, u32[]{:S(2)}) collective-permute-start(bf16[48,1152]{1,0:T(8,128)(2,1)S(1)} %get-tuple-element.198), channel_id=1, source_target_pairs={{0,8},{1,9},{2,10},{3,11},{4,12},{5,13},{6,14},{7,15},{8,0},{9,1},... | collective-permute-start | bytes 331784 | tf_op jit(solution)/shard_map/ppermute | solution.py:54
  258.9 11.6 %collective-permute-start.58 = (bf16[48,1152]{1,0:T(8,128)(2,1)S(1)}, bf16[48,1152]{1,0:T(8,128)(2,1)S(1)}, u32[]{:S(2)}, u32[]{:S(2)}) collective-permute-start(bf16[48,1152]{1,0:T(8,128)(2,1)S(1)} %get-tuple-element.200), channel_id=1, source_target_pairs={{0,16},{1,17},{2,18},{3,19},{4,20},{5,21},{6,22},{7,23},{8,24},{9,... | collective-permute-start | bytes 331784 | tf_op jit(solution)/shard_map/ppermute | solution.py:54
  260.5 10.0 %collective-permute-start.59 = (bf16[48,1152]{1,0:T(8,128)(2,1)S(1)}, bf16[48,1152]{1,0:T(8,128)(2,1)S(1)}, u32[]{:S(2)}, u32[]{:S(2)}) collective-permute-start(bf16[48,1152]{1,0:T(8,128)(2,1)S(1)} %get-tuple-element.199), channel_id=1, source_target_pairs={{0,24},{1,25},{2,26},{3,27},{4,28},{5,29},{6,30},{7,31},{8,16},{9,... | collective-permute-start | bytes 331784 | tf_op jit(solution)/shard_map/ppermute | solution.py:54
  270.6 1.4 collective-permute-start.60
  (35 other events, 533.4 us)
